TPU v7x, 32 devices: a whole 2x2x4 slice. The times are simulated.
32 devices in a mesh: win: 4 (over x, core), chan: 8 (over z, y).
Axes of the slice: x: 2, y: 2, z: 4, core: 2. Of those that a mesh axis runs over, the one named last changes fastest.
Arguments:
- traces: bfloat16 [32, 256, 7680], P('win', 'chan'), may hold values from -6 to 6
- filter_taps: bfloat16 [32], replicated, may hold values from 0.019897461 to 0.14941406
- good_channels: int32 [256], P('chan'), may hold values 0 or 1
- source_index: int32 [256], replicated, may hold values from 0 to 255, as said below
Outputs:
- correlations: float32 [256, 256, 2048], P('win', 'chan')
Inputs may be any that keep to these rules, and one draw needn't show every extreme that they name: `source_index`: 256 distinct channel numbers; channels 0 and 255 are among them; how many fall in one device's block varies.
All inputs are finite; a program needn't handle non-finite values. No bound on the sum of `good_channels` on one device may be relied on, other than what follows from the above.
Results may differ from a plain program's by a relative error of at most 0.0071.
Values may be sent and summed in bfloat16 or wider, within the bound.
No kernel may reach another device: no remote copies, remote signals or barrier semaphores. Data moves between devices by JAX's collectives and lax.ppermute only.
A program may use at most 192 MiB of HBM per device.

v0:
```python
import functools
import math

import jax
import jax.numpy as jnp
import numpy as np
from jax import lax
from jax.experimental import pallas as pl
from jax.experimental.pallas import tpu as pltpu
from jax.sharding import PartitionSpec as P

L = 7680
F = 512
LAGS = 2048
HALO = 16
SMOOTH = 64
K0 = 31
QUARTER = L // 4
STEP = 640
FINE = 32
CHUNKS = tuple((start, 128) for start in range(0, F, 128))
Z_GROUPS = ((0, 1), (1, 2), (2, 4))
GROUP = 16
LAG_FINE = 128
LAG_ROWS = 8
NT = (((1,), (1,)), ((), ()))
MIB = 1024 * 1024


def unit_angles(positions, axis):
    bins = K0 + np.arange(F, dtype=np.int64)
    phase = np.mod(np.expand_dims(positions, 1 - axis) * np.expand_dims(bins, axis), L)
    angles = phase * (2.0 * math.pi / L)
    return np.cos(angles).astype(np.float32), np.sin(angles).astype(np.float32)


def keep_column(good):
    count = good.shape[1]
    rows = lax.broadcasted_iota(jnp.int32, (count, count), 0)
    cols = lax.broadcasted_iota(jnp.int32, (count, count), 1)
    return jnp.sum(jnp.where(rows == cols, good[...].astype(jnp.float32), 0.0), axis=1, keepdims=True)


def transform_kernel(x0, x1, x2, x3, angles, good, spec, head, tail, table, total):
    step = pl.program_id(0)
    rows = x0.shape[0]
    coarse = QUARTER // FINE

    def fill(of_step):
        fine_cos = angles[2 * coarse : 2 * coarse + FINE, :]
        fine_sin = angles[2 * coarse + FINE :, :]
        for part in range(STEP // FINE):
            big_cos = angles[pl.ds(of_step * (STEP // FINE) + part, 1), :]
            big_sin = angles[pl.ds(coarse + of_step * (STEP // FINE) + part, 1), :]
            at = pl.ds(part * FINE, FINE)
            table[of_step % 2, at, :F] = (big_cos * fine_cos - big_sin * fine_sin).astype(jnp.bfloat16)
            table[of_step % 2, at, F:] = (-(big_sin * fine_cos + big_cos * fine_sin)).astype(jnp.bfloat16)

    @pl.when(step == 0)
    def _():
        total[...] = jnp.zeros_like(total)
        fill(step)

    for quarter, x in enumerate((x0, x1, x2, x3)):
        at = pl.ds(quarter * rows, rows)
        total[at, :] += jnp.dot(x[...], table[step % 2], preferred_element_type=jnp.float32)
    fill(jnp.minimum(step + 1, pl.num_programs(0) - 1))

    @pl.when(step == pl.num_programs(0) - 1)
    def _():
        turn = (K0 + lax.broadcasted_iota(jnp.int32, (1, F), 1)) % 4
        even = turn % 2 == 0
        sign = jnp.where(turn < 2, 1.0, -1.0)
        channels = good.shape[1]
        keep = keep_column(good)
        for window in range(rows // channels):
            re = [total[pl.ds(q * rows + window * channels, channels), :F] for q in range(4)]
            im = [total[pl.ds(q * rows + window * channels, channels), F:] for q in range(4)]
            real = jnp.where(even, re[0] + re[2] + sign * (re[1] + re[3]), re[0] - re[2] + sign * (im[1] - im[3])) * keep
            imag = jnp.where(even, im[0] + im[2] + sign * (im[1] + im[3]), im[0] - im[2] - sign * (re[1] - re[3])) * keep
            spec[window, :, :F] = real
            spec[window, :, F:] = imag
            head[window, :, :F] = real[:HALO].astype(jnp.bfloat16)
            head[window, :, F:] = imag[:HALO].astype(jnp.bfloat16)
            tail[window, :, :F] = real[channels - HALO :].astype(jnp.bfloat16)
            tail[window, :, F:] = imag[channels - HALO :].astype(jnp.bfloat16)


def transform(traces, good):
    windows, channels, length = traces.shape
    rows = windows * channels
    steps = QUARTER // STEP
    flat = traces.reshape(rows, length)
    coarse = unit_angles(np.arange(QUARTER // FINE) * FINE, 0)
    angles = np.concatenate(coarse + unit_angles(np.arange(FINE), 0), axis=0)
    whole = lambda *shape: pl.BlockSpec(shape, lambda k: (0,) * len(shape))
    return pl.pallas_call(
        transform_kernel,
        grid=(steps,),
        in_specs=[pl.BlockSpec((rows, STEP), functools.partial(lambda q, k: (0, q * steps + k), q)) for q in range(4)]
        + [whole(*angles.shape), whole(1, channels)],
        out_specs=[whole(windows, channels, 2 * F), whole(windows, HALO, 2 * F), whole(windows, HALO, 2 * F)],
        out_shape=[
            jax.ShapeDtypeStruct((windows, channels, 2 * F), jnp.float32),
            jax.ShapeDtypeStruct((windows, HALO, 2 * F), jnp.bfloat16),
            jax.ShapeDtypeStruct((windows, HALO, 2 * F), jnp.bfloat16),
        ],
        scratch_shapes=[pltpu.VMEM((2, STEP, 2 * F), jnp.bfloat16), pltpu.VMEM((4 * rows, 2 * F), jnp.float32)],
        compiler_params=pltpu.CompilerParams(vmem_limit_bytes=60 * MIB),
        cost_estimate=pl.CostEstimate(flops=2 * rows * length * 2 * F, bytes_accessed=rows * length * 2, transcendentals=0),
    )(flat, flat, flat, flat, angles, good)


def pieces(value):
    high = value.astype(jnp.bfloat16)
    rest = value - high.astype(jnp.float32)
    middle = rest.astype(jnp.bfloat16)
    return high, middle, (rest - middle.astype(jnp.float32)).astype(jnp.bfloat16)


def whiten_kernel(spec, left, right, band, good, *outs):
    windows, channels = spec.shape[:2]
    filtered = []
    keep = keep_column(good)
    for window in range(windows):
        stack = jnp.concatenate([left[window], *pieces(spec[window]), right[window]], axis=0)
        own = band[:, HALO : HALO + channels]
        taps = jnp.concatenate([band[:, :HALO], own, own, own, band[:, HALO + channels :]], axis=1)
        filtered.append(jnp.dot(taps, stack, preferred_element_type=jnp.float32) * keep)
    spectrum = jnp.concatenate(filtered, axis=0)
    real, imag = spectrum[:, :F], spectrum[:, F:]
    magnitude = jnp.sqrt(real * real + imag * imag)
    bins = lax.broadcasted_iota(jnp.int32, (F, F), 0)
    others = lax.broadcasted_iota(jnp.int32, (F, F), 1)
    near = jnp.where(jnp.abs(bins - others) <= SMOOTH, 1.0, 0.0).astype(jnp.bfloat16)
    amplitude = sum(jnp.dot(piece, near, preferred_element_type=jnp.float32) for piece in pieces(magnitude))
    bin_row = lax.broadcasted_iota(jnp.int32, (1, F), 1)
    count = jnp.minimum(bin_row + SMOOTH, F - 1) - jnp.maximum(bin_row - SMOOTH, 0) + 1
    amplitude = amplitude * (1.0 / count.astype(jnp.float32))
    inverse = 1.0 / (amplitude + 1e-06)
    real = (real * inverse).astype(jnp.bfloat16)
    imag = (imag * inverse).astype(jnp.bfloat16)
    full, *parts = outs
    for window in range(windows):
        rows = slice(window * channels, (window + 1) * channels)
        full[window, :, :F] = real[rows]
        full[window, :, F:] = imag[rows]
        for part, (begin, end) in zip(parts, Z_GROUPS):
            for at, (start, width) in enumerate(CHUNKS[begin:end]):
                part[at, 0, window, :, :width] = real[rows, start : start + width]
                part[at, 0, window, :, width:] = imag[rows, start : start + width]


def whiten(spec, left, right, band, good):
    windows, channels, _ = spec.shape
    return pl.pallas_call(
        whiten_kernel,
        out_shape=[
            jax.ShapeDtypeStruct(shape, jnp.bfloat16)
            for shape in [(windows, channels, 2 * F)]
            + [(end - begin, 1, windows, channels, 2 * CHUNKS[0][1]) for begin, end in Z_GROUPS]
        ],
        compiler_params=pltpu.CompilerParams(vmem_limit_bytes=40 * MIB),
        cost_estimate=pl.CostEstimate(flops=2 * windows * channels * F * F * 3, bytes_accessed=5 * MIB // 2, transcendentals=windows * channels * F),
    )(spec, left, right, band, good)


def eye(size):
    rows = lax.broadcasted_iota(jnp.int32, (size, size), 0)
    cols = lax.broadcasted_iota(jnp.int32, (size, size), 1)
    return jnp.where(rows == cols, 1.0, 0.0).astype(jnp.bfloat16)


def turned(left_unit, rows):
    return lax.dot_general(left_unit, rows, NT, preferred_element_type=jnp.float32)


def swapper(outer, inner):
    size = outer * inner
    rows = lax.broadcasted_iota(jnp.int32, (size, size), 0)
    cols = lax.broadcasted_iota(jnp.int32, (size, size), 1)
    return jnp.where(cols == rows % outer * inner + rows // outer, 1.0, 0.0).astype(jnp.bfloat16)


def moved(swap, rows):
    return jnp.dot(swap, rows, preferred_element_type=jnp.float32).astype(jnp.bfloat16)


def own_kernel(here, near, far, out, by_window):
    own = [here, near.at[0], far, near.at[1]]
    each, channels, _ = here.shape
    windows, quads = each * len(own), channels // 4
    joined = GROUP // each
    swap = swapper(GROUP, GROUP)
    for start in range(0, windows, GROUP):
        for channel in range(0, channels, GROUP):
            block = [o[:, channel : channel + GROUP, :] for o in own[start // each : start // each + joined]]
            rows = moved(swap, jnp.concatenate(block, axis=0).reshape(GROUP * GROUP, 2 * F))
            by_window[channel : channel + GROUP, start : start + GROUP, :] = rows.reshape(GROUP, GROUP, 2 * F)
    unit = eye(F // 2)
    for quad in range(quads):
        for start in range(0, F, F // 2):
            rows = []
            for channel in range(quad, channels, quads):
                rows += [by_window[channel, :, side + start : side + start + F // 2] for side in (0, F)]
            out[quad, start : start + F // 2, :] = turned(unit, jnp.concatenate(rows, axis=0)).astype(jnp.bfloat16)


def turn_own(here, near, far):
    each, channels, _ = here.shape
    windows = each * 4
    return pl.pallas_call(
        own_kernel,
        out_shape=jax.ShapeDtypeStruct((channels // 4, F, 8 * windows), jnp.bfloat16),
        scratch_shapes=[pltpu.VMEM((channels, windows, 2 * F), jnp.bfloat16)],
        compiler_params=pltpu.CompilerParams(vmem_limit_bytes=40 * MIB),
        cost_estimate=pl.CostEstimate(flops=2 * 8192 * 65536, bytes_accessed=4 * MIB, transcendentals=0),
    )(here, near, far)


def cross_kernel(here, near, far, by_channel, out, by_window, sums):
    sources = [here, near.at[0], far.at[0], near.at[1]]
    each, count, both = here.shape
    quads, _, wide = by_channel.shape
    channels, half = 4 * quads, wide // 4
    windows, width = half // 2, both // 2
    unit = eye(width)
    swap = swapper(GROUP, GROUP)
    swap_quads = swapper(quads, GROUP)
    for window in range(0, windows, 2):
        rows = []
        for one in range(window, window + 2):
            source = sources[one // each]
            rows += [source[one % each, :, :width], source[one % each, :, width:]]
        both_turned = turned(unit, jnp.concatenate(rows, axis=0)).astype(jnp.bfloat16)
        by_window[window] = both_turned[:, : 2 * count]
        by_window[window + 1] = both_turned[:, 2 * count :]
    first = lax.broadcasted_iota(jnp.int32, (1, 2 * half), 1) < half
    sign = jnp.where(lax.broadcasted_iota(jnp.int32, (1, 2 * count), 1) < count, 1.0, -1.0)
    empty = jnp.zeros((2 * windows, 2 * count), jnp.bfloat16)

    def one_group(group, carry):
        bins = pl.ds(pl.multiple_of(group * GROUP, GROUP), GROUP)
        rows = [
            by_window[start : start + GROUP, bins, :].reshape(GROUP * GROUP, 2 * count)
            for start in range(0, windows, GROUP)
        ]
        rights = jnp.dot(swap, jnp.concatenate(rows, axis=1), preferred_element_type=jnp.float32)
        lefts = jnp.dot(
            swap_quads, by_channel[:, bins, :].reshape(quads * GROUP, 4 * half), preferred_element_type=jnp.float32
        )
        results = []
        for at in range(0, GROUP, 2):
            two = []
            for one in range(at, at + 2):
                here = rights[one * GROUP : (one + 1) * GROUP]
                src = jnp.concatenate(
                    [here[:, i * 2 * count : (i + 1) * 2 * count] for i in range(windows // GROUP)], axis=0
                )
                two.append(jnp.concatenate([src * sign, pltpu.roll(src, count, axis=1)], axis=0).astype(jnp.bfloat16))
            right = jnp.concatenate(
                [jnp.concatenate([two[0], empty], axis=1), jnp.concatenate([empty, two[1]], axis=1)], axis=0
            )
            left = []
            for tile in range(0, 4 * half, 2 * half):
                one, other = (lefts[i * quads : (i + 1) * quads, tile : tile + 2 * half] for i in (at, at + 1))
                left.append(jnp.where(first, one, pltpu.roll(other, half, axis=1)))
                left.append(jnp.where(first, pltpu.roll(one, half, axis=1), other))
            left = jnp.concatenate(left, axis=0).astype(jnp.bfloat16)
            result = jnp.dot(left, right, preferred_element_type=jnp.float32).astype(jnp.bfloat16)
            results += [result[:, : 2 * count], result[:, 2 * count :]]
        halves = [
            jnp.concatenate([r[start : start + GROUP] for r in results], axis=0) for start in range(0, channels, GROUP)
        ]
        done = moved(swap, jnp.concatenate(halves, axis=1))
        for channel in range(channels):
            row, side = channel % GROUP, channel // GROUP
            sums[channel, bins, :] = done[
                row * GROUP : (row + 1) * GROUP, side * 2 * count : (side + 1) * 2 * count
            ]
        return carry

    lax.fori_loop(0, width // GROUP, one_group, 0, unroll=8)
    unit = eye(2 * count)
    part = 256 // LAG_ROWS
    swap = swapper(LAG_ROWS, part)
    for group in range(channels // LAG_ROWS):
        by_bin = []
        for channel in range(group * LAG_ROWS, (group + 1) * LAG_ROWS, 2):
            rows = jnp.concatenate([sums[channel], sums[channel + 1]], axis=0)
            both_turned = turned(unit, rows).astype(jnp.bfloat16)
            by_bin += [both_turned[:, :width], both_turned[:, width:]]
        for start in range(0, count, part):
            rows = jnp.concatenate(
                [
                    jnp.concatenate([b[start : start + part], b[count + start : count + start + part]], axis=1)
                    for b in by_bin
                ],
                axis=0,
            )
            rows = moved(swap, rows)
            at = slice(start * LAG_ROWS, (start + part) * LAG_ROWS)
            out[group, 0, at, :] = rows[:, :width]
            out[group, 1, at, :] = rows[:, width:]


def cross(here, near, far, by_channel, first_bin):
    each, count, both = here.shape
    quads, _, wide = by_channel.shape
    channels, windows, width = 4 * quads, wide // 8, both // 2
    return pl.pallas_call(
        cross_kernel,
        grid=(1,),
        in_specs=[pl.BlockSpec(a.shape, functools.partial(lambda n, i: (0,) * n, a.ndim)) for a in (here, near, far)]
        + [pl.BlockSpec((quads, width, wide), lambda i: (0, first_bin // width, 0))],
        out_specs=pl.BlockSpec((channels // LAG_ROWS, 2, count * LAG_ROWS, width), lambda i: (0, 0, 0, 0)),
        out_shape=jax.ShapeDtypeStruct((channels // LAG_ROWS, 2, count * LAG_ROWS, width), jnp.bfloat16),
        scratch_shapes=[
            pltpu.VMEM((windows, width, 2 * count), jnp.bfloat16),
            pltpu.VMEM((channels, width, 2 * count), jnp.bfloat16),
        ],
        compiler_params=pltpu.CompilerParams(vmem_limit_bytes=40 * MIB),
        cost_estimate=pl.CostEstimate(flops=2 * width * 36 * 65536, bytes_accessed=4 * MIB, transcendentals=0),
    )(here, near, far, by_channel)


def lag_kernel(scaling, *refs):
    *stacked, table, edge, out = refs
    count, channels, _ = out.shape
    real, imag = (jnp.concatenate([chunk[0, side] for chunk in stacked], axis=1) for side in range(2))
    size = count * channels
    lane = lax.broadcasted_iota(jnp.int32, (size, LAG_FINE), 1)
    mirror = (LAG_FINE - lane) % LAG_FINE

    def parts(start, width):
        even = jnp.dot(real, table[:F, start : start + width], preferred_element_type=jnp.float32)
        odd = jnp.dot(imag, table[F:, start : start + width], preferred_element_type=jnp.float32)
        return even, odd

    half = LAGS // 2
    products = real.astype(jnp.float32) * edge[:1] + imag.astype(jnp.float32) * edge[1:]
    above = jnp.sum(products, axis=1, keepdims=True) * scaling
    for start in range(half - 2 * LAG_FINE, -1, -2 * LAG_FINE):
        even, odd = parts(start, 2 * LAG_FINE)
        after_zero = (even - odd) * scaling
        before_zero = (even + odd) * scaling
        out[:, :, half + start : half + start + 2 * LAG_FINE] = after_zero.reshape(count, channels, 2 * LAG_FINE)
        for tile in (1, 0):
            turned_round = jnp.take_along_axis(
                before_zero[:, tile * LAG_FINE : (tile + 1) * LAG_FINE], mirror, axis=1, mode="promise_in_bounds"
            )
            at = half - start - (tile + 1) * LAG_FINE
            out[:, :, at : at + LAG_FINE] = jnp.where(lane == 0, above, turned_round).reshape(count, channels, LAG_FINE)
            above = turned_round


def lagged(stacked, table, scaling):
    groups, _, size, _ = stacked[0].shape
    edge = np.concatenate(unit_angles(np.array([LAGS // 2]), 0), axis=0).astype(jnp.bfloat16).astype(np.float32)
    count = size // LAG_ROWS
    return pl.pallas_call(
        functools.partial(lag_kernel, scaling),
        grid=(groups,),
        in_specs=[pl.BlockSpec((1, 2, size, s.shape[3]), lambda i: (i, 0, 0, 0)) for s in stacked]
        + [pl.BlockSpec(a.shape, lambda i: (0, 0)) for a in (table, edge)],
        out_specs=pl.BlockSpec((count, LAG_ROWS, LAGS), lambda i: (0, i, 0)),
        out_shape=jax.ShapeDtypeStruct((count, groups * LAG_ROWS, LAGS), jnp.float32),
        compiler_params=pltpu.CompilerParams(vmem_limit_bytes=48 * MIB),
        cost_estimate=pl.CostEstimate(
            flops=2 * groups * size * F * LAGS, bytes_accessed=groups * size * LAGS * 4, transcendentals=0
        ),
    )(*stacked, table, edge)


def table_kernel(angles, out):
    fine_cos, fine_sin = angles[:, :LAG_FINE], angles[:, LAG_FINE : 2 * LAG_FINE]
    tiles = out.shape[1] // LAG_FINE
    for tile in range(tiles):
        big_cos = angles[:, 2 * LAG_FINE + tile : 2 * LAG_FINE + tile + 1]
        big_sin = angles[:, 2 * LAG_FINE + tiles + tile : 2 * LAG_FINE + tiles + tile + 1]
        cols = slice(tile * LAG_FINE, (tile + 1) * LAG_FINE)
        out[:F, cols] = (big_cos * fine_cos - big_sin * fine_sin).astype(jnp.bfloat16)
        out[F:, cols] = (big_sin * fine_cos + big_cos * fine_sin).astype(jnp.bfloat16)


def lag_table():
    tiles = LAGS // 2 // LAG_FINE
    coarse = unit_angles(np.arange(tiles) * LAG_FINE, 1)
    angles = np.concatenate(unit_angles(np.arange(LAG_FINE), 1) + coarse, axis=1)
    return pl.pallas_call(
        table_kernel,
        out_shape=jax.ShapeDtypeStruct((2 * F, tiles * LAG_FINE), jnp.bfloat16),
        compiler_params=pltpu.CompilerParams(vmem_limit_bytes=40 * MIB),
        cost_estimate=pl.CostEstimate(flops=8 * F * tiles * LAG_FINE, bytes_accessed=4 * MIB, transcendentals=0),
    )(angles)


def make_band(filter_taps, channel_count):
    kernel = jnp.concatenate(
        [
            -filter_taps[:HALO].astype(jnp.float32),
            jnp.ones((1,), jnp.float32),
            -filter_taps[HALO:].astype(jnp.float32),
        ]
    )
    row_ids = jnp.arange(channel_count, dtype=jnp.int32)[:, None]
    columns = jnp.arange(channel_count + 2 * HALO, dtype=jnp.int32)[None, :]
    offset = columns - row_ids
    choose = offset[:, :, None] == jnp.arange(2 * HALO + 1, dtype=jnp.int32)[None, None, :]
    return jnp.sum(jnp.where(choose, kernel[None, None, :], 0.0), axis=2).astype(jnp.bfloat16)


def pick_kernel(held, across, selector, here, near, far):
    count = here.shape[1]
    for window in range(held.shape[1]):
        rows = [blocks[i, window] for blocks in (held, across) for i in range(blocks.shape[0])]
        picked = jnp.dot(selector[...], jnp.concatenate(rows, axis=0), preferred_element_type=jnp.float32)
        picked = picked.astype(jnp.bfloat16)
        here[window] = picked[:count]
        near[window] = picked[count : 2 * count]
        for at in range(far.shape[0]):
            far[at, window] = picked[(2 + at) * count : (3 + at) * count]


def pick(held, across, selector, groups):
    _, windows, _, both = held.shape
    count = selector.shape[0] // groups
    one = (windows, count, both)
    return pl.pallas_call(
        pick_kernel,
        out_shape=[jax.ShapeDtypeStruct(shape, jnp.bfloat16) for shape in (one, one, (groups - 2, *one))],
        compiler_params=pltpu.CompilerParams(vmem_limit_bytes=40 * MIB),
        cost_estimate=pl.CostEstimate(
            flops=2 * windows * selector.size * both, bytes_accessed=2 * windows * both * sum(selector.shape), transcendentals=0
        ),
    )(held, across, selector)


def swapped(value, axis, step):
    return lax.ppermute(value, axis, [(i, i ^ step) for i in range(lax.axis_size(axis))])


def after(value, earlier):
    return lax.optimization_barrier((value, earlier))[0]


def per_device(traces, filter_taps, good_channels, source_index):
    window_count, channel_count, _ = traces.shape
    good = good_channels[None, :]
    spec, head, tail = transform(traces, good)
    blocks = lax.axis_size("chan")
    groups = lax.axis_size("win")
    left = lax.ppermute(tail, "chan", [(i, i + 1) for i in range(blocks - 1)])
    right = lax.ppermute(head, "chan", [(i + 1, i) for i in range(blocks - 1)])
    table = lag_table()
    left = after(left, table)
    full, *parts = whiten(spec, left, right, make_band(filter_taps, channel_count), good)

    order = [0]
    step = blocks // 2
    while step:
        order += [place ^ step for place in order]
        step //= 2
    order = jnp.asarray(order, jnp.int32) ^ lax.axis_index("chan")
    own_ids = jnp.arange(channel_count, dtype=jnp.int32)
    channel_ids = (order[:, None] * channel_count + own_ids[None, :]).reshape(-1)
    by_group = source_index.reshape(groups, -1)
    here = lax.axis_index("win")
    wanted = jnp.concatenate([lax.dynamic_slice_in_dim(by_group, here ^ step, 1) for step in range(groups)], axis=0)
    selector = (wanted.reshape(-1)[:, None] == channel_ids[None, :]).astype(jnp.bfloat16)

    own_far = swapped(full, "win", 2)
    own_near = swapped(jnp.stack([full, own_far]), "win", 1)
    by_channel = turn_own(full, own_near, own_far)
    gathered, picked, stacked = [], [], []
    chunks = len(CHUNKS)

    def gather(part):
        held, step = part, blocks // 2
        while step > 1:
            received = swapped(held, "chan", step)
            if step > 2:
                held = jnp.concatenate([held, received], axis=1)
                if step == blocks // 2:
                    first_held.append(held)
                    if len(gathered) > 1:
                        held = after(held, picked[0][0])
            step //= 2
        gathered.extend(jnp.concatenate([held[i], received[i]], axis=0) for i in range(part.shape[0]))

    def exchange(at):
        held = after(gathered[at], picked[-1][0]) if at else gathered[at]
        across = swapped(held, "chan", 1)
        if at > 1:
            finish(at - 2)
        if at:
            across = after(across, stacked[-1] if stacked else by_channel)
        here, near, far = pick(held, across, selector, groups)
        picked.append((here, near, swapped(far, "win", 2)))

    def finish(at):
        here, near, far = picked[at]
        if stacked:
            far = after(far, stacked[-1])
        near = swapped(jnp.stack([near, far[1]]), "win", 1)
        stacked.append(cross(here, near, far, by_channel, CHUNKS[at][0]))

    first_held = []
    for part in parts:
        gather(after(part, [first_held[-1]] + [own_far] * (len(first_held) > 1)) if first_held else part)
        if len(gathered) == 2:
            exchange(0)
    for at in range(1, chunks):
        exchange(at)
    for at in range(len(stacked), chunks):
        finish(at)
    return lagged(stacked, table, 1.0 / math.sqrt(F * window_count * groups))


def solution(mesh):
    placed = (P("win", "chan", None), P(), P("chan"), P())
    return jax.shard_map(
        per_device, mesh=mesh, in_specs=placed, out_specs=P("win", "chan", None), check_vma=False
    )
```

profile of v0, /device:TPU:0, one launch (start us, length us, event | category | flops | bytes accessed | tf_op | source)
XLA Modules:
  0.0 143.2 jit_solution(3698082773961365200)
XLA Ops:
  0.0 10.6 %shard_map.82 = (f32[8,32,1024]{2,1,0:T(8,128)}, bf16[8,16,1024]{2,1,0:T(8,128)(2,1)}, bf16[8,16,1024]{2,1,0:T(8,128)(2,1)}) custom-call(bf16[256,7680]{1,0:T(8,128)(2,1)} %bitcast.28, bf16[256,7680]{1,0:T(8,128)(2,1)} %bitcast.29, bf16[256,7680]{1,0:T(8,128)(2,1)} %bitcast.30, bf16[256,7680]{1,0:T(8,128)(2,1)} %bitcast.31, ...), custom_call_target="tpu_custom_call" | custom-call | flops 4026531840 | bytes 3932160 | tf_op jit(solution)/shard_map/pallas_call | solution.py:97
  10.6 5.0 %collective-permute-start = (bf16[8,16,1024]{2,1,0:T(8,128)(2,1)}, bf16[8,16,1024]{2,1,0:T(8,128)(2,1)S(1)}, u32[]{:S(2)}, u32[]{:S(2)}) collective-permute-start(bf16[8,16,1024]{2,1,0:T(8,128)(2,1)} %get-tuple-element.38), channel_id=1, source_target_pairs={{0,1},{1,2},{2,3},{3,4},{4,5},{5,6},{6,7},{8,9},{9,10},{10,11},{11... | collective-permute-start | bytes 786440 | tf_op jit(solution)/shard_map/ppermute | solution.py:453
  15.6 1.5 %collective-permute-start.1 = (bf16[8,16,1024]{2,1,0:T(8,128)(2,1)}, bf16[8,16,1024]{2,1,0:T(8,128)(2,1)S(1)}, u32[]{:S(2)}, u32[]{:S(2)}) collective-permute-start(bf16[8,16,1024]{2,1,0:T(8,128)(2,1)} %get-tuple-element.40), channel_id=1, source_target_pairs={{1,0},{2,1},{3,2},{4,3},{5,4},{6,5},{7,6},{9,8},{10,9},{11,10},{12... | collective-permute-start | bytes 786440 | tf_op jit(solution)/shard_map/ppermute | solution.py:454
  17.2 1.3 shard_map.83.refs_4_
  18.5 1.4 copy-done
  20.0 7.0 %collective-permute-done.left = bf16[8,16,1024]{2,1,0:T(8,128)(2,1)S(1)} collective-permute-done((bf16[8,16,1024]{2,1,0:T(8,128)(2,1)}, bf16[8,16,1024]{2,1,0:T(8,128)(2,1)S(1)}, u32[]{:S(2)}, u32[]{:S(2)}) %collective-permute-start) | collective-permute-done | bytes 262176 | tf_op jit(solution)/shard_map/ppermute | solution.py:453
  29.5 4.4 %collective-permute-start.2 = (bf16[1,1,8,32,256]{4,3,2,1,0:T(8,128)(2,1)S(1)}, bf16[1,1,8,32,256]{4,3,2,1,0:T(8,128)(2,1)S(1)}, u32[]{:S(2)}, u32[]{:S(2)}) collective-permute-start(bf16[1,1,8,32,256]{4,3,2,1,0:T(8,128)(2,1)S(1)} %get-tuple-element.41), channel_id=1, source_target_pairs={{0,4},{1,5},{2,6},{3,7},{4,0},{5,1},{6,2},{7,3},{8,12},{9,13},{10,... | collective-permute-start | bytes 393224 | tf_op jit(solution)/shard_map/ppermute | solution.py:440
  34.0 1.5 %collective-permute-start.7 = (bf16[8,32,1024]{2,1,0:T(8,128)(2,1)S(1)}, bf16[8,32,1024]{2,1,0:T(8,128)(2,1)S(1)}, u32[]{:S(2)}, u32[]{:S(2)}) collective-permute-start(bf16[8,32,1024]{2,1,0:T(8,128)(2,1)S(1)} %get-tuple-element.45.here), channel_id=1, source_target_pairs={{0,16},{8,24},{16,0},{24,8},{1,17},{9,25},{17,1},{25,9},{2,18},{10... | collective-permute-start | bytes 1572872 | tf_op jit(solution)/shard_map/ppermute | solution.py:440
  35.5 5.0 %collective-permute-done.2 = bf16[1,1,8,32,256]{4,3,2,1,0:T(8,128)(2,1)S(1)} collective-permute-done((bf16[1,1,8,32,256]{4,3,2,1,0:T(8,128)(2,1)S(1)}, bf16[1,1,8,32,256]{4,3,2,1,0:T(8,128)(2,1)S(1)}, u32[]{:S(2)}, u32[]{:S(2)}) %collective-permute-start.2) | collective-permute-done | bytes 131104 | tf_op jit(solution)/shard_map/ppermute | solution.py:440
  41.5 3.4 %collective-permute-start.9 = (bf16[1,1,8,32,256]{4,3,2,1,0:T(8,128)(2,1)S(1)}, bf16[1,1,8,32,256]{4,3,2,1,0:T(8,128)(2,1)S(1)}, u32[]{:S(2)}, u32[]{:S(2)}) collective-permute-start(bf16[1,1,8,32,256]{4,3,2,1,0:T(8,128)(2,1)S(1)} %get-tuple-element.47), channel_id=1, source_target_pairs={{0,4},{1,5},{2,6},{3,7},{4,0},{5,1},{6,2},{7,3},{8,12},{9,13},{10,... | collective-permute-start | bytes 393224 | tf_op jit(solution)/shard_map/ppermute | solution.py:440
  45.6 5.5 %collective-permute-done.3 = bf16[1,2,8,32,256]{4,3,2,1,0:T(8,128)(2,1)S(1)} collective-permute-done((bf16[1,2,8,32,256]{4,3,2,1,0:T(8,128)(2,1)S(1)}, bf16[1,2,8,32,256]{4,3,2,1,0:T(8,128)(2,1)S(1)}, u32[]{:S(2)}, u32[]{:S(2)}) %collective-permute-start.3) | collective-permute-done | bytes 262176 | tf_op jit(solution)/shard_map/ppermute | solution.py:440
  53.0 1.7 %collective-permute-start.10 = (bf16[1,2,8,32,256]{4,3,2,1,0:T(8,128)(2,1)}, bf16[1,2,8,32,256]{4,3,2,1,0:T(8,128)(2,1)}, u32[]{:S(2)}, u32[]{:S(2)}) collective-permute-start(bf16[1,2,8,32,256]{4,3,2,1,0:T(8,128)(2,1)} %constant_dynamic-update-slice_fusion.2), channel_id=1, source_target_pairs={{0,2},{1,3},{2,0},{3,1},{4,6},{5,7},{6,4},{7,5},{8,10},{9,11},{10,... | collective-permute-start | bytes 786440 | tf_op jit(solution)/shard_map/ppermute | solution.py:440
  54.8 3.0 %collective-permute-start.14 = (bf16[2,1,8,32,256]{4,3,2,1,0:T(8,128)(2,1)S(1)}, bf16[2,1,8,32,256]{4,3,2,1,0:T(8,128)(2,1)S(1)}, u32[]{:S(2)}, u32[]{:S(2)}) collective-permute-start(bf16[2,1,8,32,256]{4,3,2,1,0:T(8,128)(2,1)S(1)} %get-tuple-element.55), channel_id=1, source_target_pairs={{0,4},{1,5},{2,6},{3,7},{4,0},{5,1},{6,2},{7,3},{8,12},{9,13},{10,... | collective-permute-start | bytes 786440 | tf_op jit(solution)/shard_map/ppermute | solution.py:440
  57.9 5.8 %collective-permute-done.4.across = bf16[4,8,32,256]{3,2,1,0:T(8,128)(2,1)S(1)} collective-permute-done((bf16[4,8,32,256]{3,2,1,0:T(8,128)(2,1)S(1)}, bf16[4,8,32,256]{3,2,1,0:T(8,128)(2,1)S(1)}, u32[]{:S(2)}, u32[]{:S(2)}) %collective-permute-start.4) | collective-permute-done | bytes 524320 | tf_op jit(solution)/shard_map/ppermute | solution.py:440
  64.1 1.6 %collective-permute-start.5 = (bf16[2,8,64,256]{3,2,1,0:T(8,128)(2,1)S(1)}, bf16[2,8,64,256]{3,2,1,0:T(8,128)(2,1)S(1)}, u32[]{:S(2)}, u32[]{:S(2)}) collective-permute-start(bf16[2,8,64,256]{3,2,1,0:T(8,128)(2,1)S(1)} %get-tuple-element.44), channel_id=1, source_target_pairs={{0,16},{8,24},{16,0},{24,8},{1,17},{9,25},{17,1},{25,9},{2,18},{10... | collective-permute-start | bytes 1572872 | tf_op jit(solution)/shard_map/ppermute | solution.py:440
  65.6 1.8 %collective-permute-done.10 = bf16[1,2,8,32,256]{4,3,2,1,0:T(8,128)(2,1)} collective-permute-done((bf16[1,2,8,32,256]{4,3,2,1,0:T(8,128)(2,1)}, bf16[1,2,8,32,256]{4,3,2,1,0:T(8,128)(2,1)}, u32[]{:S(2)}, u32[]{:S(2)}) %collective-permute-start.10) | collective-permute-done | bytes 262176 | tf_op jit(solution)/shard_map/ppermute | solution.py:440
  68.5 2.1 %collective-permute-start.11 = (bf16[4,8,32,256]{3,2,1,0:T(8,128)(2,1)S(1)}, bf16[4,8,32,256]{3,2,1,0:T(8,128)(2,1)S(1)}, u32[]{:S(2)}, u32[]{:S(2)}) collective-permute-start(bf16[4,8,32,256]{3,2,1,0:T(8,128)(2,1)S(1)} %pad_maximum_fusion.3.held), channel_id=1, source_target_pairs={{0,1},{1,0},{2,3},{3,2},{4,5},{5,4},{6,7},{7,6},{8,9},{9,8},{10,11... | collective-permute-start | bytes 1572872 | tf_op jit(solution)/shard_map/ppermute | solution.py:440
  70.7 5.0 %collective-permute-done.5.far = bf16[2,8,64,256]{3,2,1,0:T(8,128)(2,1)S(1)} collective-permute-done((bf16[2,8,64,256]{3,2,1,0:T(8,128)(2,1)S(1)}, bf16[2,8,64,256]{3,2,1,0:T(8,128)(2,1)S(1)}, u32[]{:S(2)}, u32[]{:S(2)}) %collective-permute-start.5) | collective-permute-done | bytes 524320 | tf_op jit(solution)/shard_map/ppermute | solution.py:440
  75.9 1.4 shard_map.86.by_channel
  77.3 5.1 %collective-permute-done.11.across = bf16[4,8,32,256]{3,2,1,0:T(8,128)(2,1)S(1)} collective-permute-done((bf16[4,8,32,256]{3,2,1,0:T(8,128)(2,1)S(1)}, bf16[4,8,32,256]{3,2,1,0:T(8,128)(2,1)S(1)}, u32[]{:S(2)}, u32[]{:S(2)}) %collective-permute-start.11) | collective-permute-done | bytes 524320 | tf_op jit(solution)/shard_map/ppermute | solution.py:440
  82.8 1.6 %collective-permute-start.12 = (bf16[2,8,64,256]{3,2,1,0:T(8,128)(2,1)S(1)}, bf16[2,8,64,256]{3,2,1,0:T(8,128)(2,1)S(1)}, u32[]{:S(2)}, u32[]{:S(2)}) collective-permute-start(bf16[2,8,64,256]{3,2,1,0:T(8,128)(2,1)S(1)} %get-tuple-element.52), channel_id=1, source_target_pairs={{0,16},{8,24},{16,0},{24,8},{1,17},{9,25},{17,1},{25,9},{2,18},{10... | collective-permute-start | bytes 1572872 | tf_op jit(solution)/shard_map/ppermute | solution.py:440
  84.5 1.8 %collective-permute-start.16 = (bf16[4,8,32,256]{3,2,1,0:T(8,128)(2,1)S(1)}, bf16[4,8,32,256]{3,2,1,0:T(8,128)(2,1)S(1)}, u32[]{:S(2)}, u32[]{:S(2)}) collective-permute-start(bf16[4,8,32,256]{3,2,1,0:T(8,128)(2,1)S(1)} %get-tuple-element.57.held), channel_id=1, source_target_pairs={{0,1},{1,0},{2,3},{3,2},{4,5},{5,4},{6,7},{7,6},{8,9},{9,8},{10,11... | collective-permute-start | bytes 1572872 | tf_op jit(solution)/shard_map/ppermute | solution.py:440
  86.3 5.3 %shard_map.87.refs_0_ = bf16[4,2,512,128]{3,2,1,0:T(8,128)(2,1)S(1)} custom-call(bf16[8,64,256]{2,1,0:T(8,128)(2,1)S(1)} %get-tuple-element.42.here, bf16[2,8,64,256]{3,2,1,0:T(8,128)(2,1)S(1)} %collective-permute-done.6.near, bf16[2,8,64,256]{3,2,1,0:T(8,128)(2,1)S(1)} %collective-permute-done.5.far, bf16[8,512,256]{2,1,0:T(8,128)(2,1)S(1)} %shard_map.86.by_channel), custom_call_target="tpu_custom_call" | custom-call | flops 603979776 | bytes 4194304 | tf_op jit(solution)/shard_map/pallas_call | solution.py:311
  91.7 4.2 %collective-permute-done.12.far = bf16[2,8,64,256]{3,2,1,0:T(8,128)(2,1)S(1)} collective-permute-done((bf16[2,8,64,256]{3,2,1,0:T(8,128)(2,1)S(1)}, bf16[2,8,64,256]{3,2,1,0:T(8,128)(2,1)S(1)}, u32[]{:S(2)}, u32[]{:S(2)}) %collective-permute-start.12) | collective-permute-done | bytes 524320 | tf_op jit(solution)/shard_map/ppermute | solution.py:440
  96.0 1.3 collective-permute-done.16.across
  99.8 5.5 %shard_map.89.refs_1_ = bf16[4,2,512,128]{3,2,1,0:T(8,128)(2,1)S(1)} custom-call(bf16[8,64,256]{2,1,0:T(8,128)(2,1)S(1)} %get-tuple-element.50.here, bf16[2,8,64,256]{3,2,1,0:T(8,128)(2,1)S(1)} %collective-permute-done.13.near, bf16[2,8,64,256]{3,2,1,0:T(8,128)(2,1)S(1)} %collective-permute-done.12.far, bf16[8,512,256]{2,1,0:T(8,128)(2,1)S(1)} %shard_map.86.by_channel), custom_call_target="tpu_custom_call" | custom-call | flops 603979776 | bytes 4194304 | tf_op jit(solution)/shard_map/pallas_call | solution.py:311
  105.3 5.6 %collective-permute-done.17.far = bf16[2,8,64,256]{3,2,1,0:T(8,128)(2,1)S(1)} collective-permute-done((bf16[2,8,64,256]{3,2,1,0:T(8,128)(2,1)S(1)}, bf16[2,8,64,256]{3,2,1,0:T(8,128)(2,1)S(1)}, u32[]{:S(2)}, u32[]{:S(2)}) %collective-permute-start.17) | collective-permute-done | bytes 524320 | tf_op jit(solution)/shard_map/ppermute | solution.py:440
  113.1 5.3 %shard_map.91.refs_2_ = bf16[4,2,512,128]{3,2,1,0:T(8,128)(2,1)S(1)} custom-call(bf16[8,64,256]{2,1,0:T(8,128)(2,1)S(1)} %get-tuple-element.59.here, bf16[2,8,64,256]{3,2,1,0:T(8,128)(2,1)S(1)} %collective-permute-done.18.near, bf16[2,8,64,256]{3,2,1,0:T(8,128)(2,1)S(1)} %collective-permute-done.17.far, bf16[8,512,256]{2,1,0:T(8,128)(2,1)S(1)} %shard_map.86.by_channel), custom_call_target="tpu_custom_call" | custom-call | flops 603979776 | bytes 4194304 | tf_op jit(solution)/shard_map/pallas_call | solution.py:311
  118.5 7.4 %collective-permute-done.20.far = bf16[2,8,64,256]{3,2,1,0:T(8,128)(2,1)S(1)} collective-permute-done((bf16[2,8,64,256]{3,2,1,0:T(8,128)(2,1)S(1)}, bf16[2,8,64,256]{3,2,1,0:T(8,128)(2,1)S(1)}, u32[]{:S(2)}, u32[]{:S(2)}) %collective-permute-start.20) | collective-permute-done | bytes 524320 | tf_op jit(solution)/shard_map/ppermute | solution.py:440
  126.0 1.9 %collective-permute-done.21.near = bf16[2,8,64,256]{3,2,1,0:T(8,128)(2,1)S(1)} collective-permute-done((bf16[2,8,64,256]{3,2,1,0:T(8,128)(2,1)S(1)}, bf16[2,8,64,256]{3,2,1,0:T(8,128)(2,1)S(1)}, u32[]{:S(2)}, u32[]{:S(2)}) %collective-permute-start.21) | collective-permute-done | bytes 524320 | tf_op jit(solution)/shard_map/ppermute | solution.py:440
  127.9 5.3 %shard_map.93.refs_3_ = bf16[4,2,512,128]{3,2,1,0:T(8,128)(2,1)S(1)} custom-call(bf16[8,64,256]{2,1,0:T(8,128)(2,1)S(1)} %get-tuple-element.65.here, bf16[2,8,64,256]{3,2,1,0:T(8,128)(2,1)S(1)} %collective-permute-done.21.near, bf16[2,8,64,256]{3,2,1,0:T(8,128)(2,1)S(1)} %collective-permute-done.20.far, bf16[8,512,256]{2,1,0:T(8,128)(2,1)S(1)} %shard_map.86.by_channel), custom_call_target="tpu_custom_call" | custom-call | flops 603979776 | bytes 4194304 | tf_op jit(solution)/shard_map/pallas_call | solution.py:311
  133.2 9.9 %shard_map.94 = f32[64,32,2048]{2,1,0:T(8,128)} custom-call(bf16[4,2,512,128]{3,2,1,0:T(8,128)(2,1)S(1)} %shard_map.87.refs_0_, bf16[4,2,512,128]{3,2,1,0:T(8,128)(2,1)S(1)} %shard_map.89.refs_1_, bf16[4,2,512,128]{3,2,1,0:T(8,128)(2,1)S(1)} %shard_map.91.refs_2_, bf16[4,2,512,128]{3,2,1,0:T(8,128)(2,1)S(1)} %shard_map.93.refs_3_, ...), custom_call_target="tpu_custom_call" | custom-call | flops 4294967296 | bytes 16777216 | tf_op jit(solution)/shard_map/pallas_call | solution.py:361
  (72 shorter events, 13.9 us)
Async XLA Ops:
  0.0 17.1 %copy-start.5 = (bf16[32]{0:T(256)(128)(2,1)S(1)}, bf16[32]{0:T(256)(128)(2,1)}, u32[]{:S(2)}) copy-start(bf16[32]{0:T(256)(128)(2,1)} %param.9) | copy-start | bytes 196
  0.0 17.2 %copy-start.2 = (f32[512,272]{1,0:T(8,128)S(1)}, f32[512,272]{1,0:T(8,128)}, u32[]{:S(2)}) copy-start(f32[512,272]{1,0:T(8,128)} %constant.33.clone.angles) | copy-start | bytes 1671172
  0.0 27.1 %copy-start.4 = (s32[32]{0:T(128)S(1)}, s32[32]{0:T(128)}, u32[]{:S(2)}) copy-start(s32[32]{0:T(128)} %param.10) | copy-start | bytes 388
  10.6 23.4 %copy-start.7 = (s32[8]{0:T(128)S(1)}, s32[8]{0:T(128)}, u32[]{:S(2)}) copy-start(s32[8]{0:T(128)} %constant.34.clone) | copy-start | bytes 100
  10.6 30.8 %copy-start.6 = (s32[256]{0:T(256)S(1)}, s32[256]{0:T(256)}, u32[]{:S(2)}) copy-start(s32[256]{0:T(256)} %param.11) | copy-start | bytes 3076
  10.6 16.5 %collective-permute-start = (bf16[8,16,1024]{2,1,0:T(8,128)(2,1)}, bf16[8,16,1024]{2,1,0:T(8,128)(2,1)S(1)}, u32[]{:S(2)}, u32[]{:S(2)}) collective-permute-start(bf16[8,16,1024]{2,1,0:T(8,128)(2,1)} %get-tuple-element.38), channel_id=1, source_target_pairs={{0,1},{1,2},{2,3},{3,4},{4,5},{5,6},{6,7},{8,9},{9,10},{10,11},{11... | collective-permute-start | bytes 786440 | tf_op jit(solution)/shard_map/ppermute | solution.py:453
  15.6 11.5 %collective-permute-start.1 = (bf16[8,16,1024]{2,1,0:T(8,128)(2,1)}, bf16[8,16,1024]{2,1,0:T(8,128)(2,1)S(1)}, u32[]{:S(2)}, u32[]{:S(2)}) collective-permute-start(bf16[8,16,1024]{2,1,0:T(8,128)(2,1)} %get-tuple-element.40), channel_id=1, source_target_pairs={{1,0},{2,1},{3,2},{4,3},{5,4},{6,5},{7,6},{9,8},{10,9},{11,10},{12... | collective-permute-start | bytes 786440 | tf_op jit(solution)/shard_map/ppermute | solution.py:454
  18.5 1.4 copy-start
  27.1 1.2 copy-start.1
  29.5 10.9 %collective-permute-start.2 = (bf16[1,1,8,32,256]{4,3,2,1,0:T(8,128)(2,1)S(1)}, bf16[1,1,8,32,256]{4,3,2,1,0:T(8,128)(2,1)S(1)}, u32[]{:S(2)}, u32[]{:S(2)}) collective-permute-start(bf16[1,1,8,32,256]{4,3,2,1,0:T(8,128)(2,1)S(1)} %get-tuple-element.41), channel_id=1, source_target_pairs={{0,4},{1,5},{2,6},{3,7},{4,0},{5,1},{6,2},{7,3},{8,12},{9,13},{10,... | collective-permute-start | bytes 393224 | tf_op jit(solution)/shard_map/ppermute | solution.py:440
  34.0 17.2 %collective-permute-start.7 = (bf16[8,32,1024]{2,1,0:T(8,128)(2,1)S(1)}, bf16[8,32,1024]{2,1,0:T(8,128)(2,1)S(1)}, u32[]{:S(2)}, u32[]{:S(2)}) collective-permute-start(bf16[8,32,1024]{2,1,0:T(8,128)(2,1)S(1)} %get-tuple-element.45.here), channel_id=1, source_target_pairs={{0,16},{8,24},{16,0},{24,8},{1,17},{9,25},{17,1},{25,9},{2,18},{10... | collective-permute-start | bytes 1572872 | tf_op jit(solution)/shard_map/ppermute | solution.py:440
  40.5 10.6 %collective-permute-start.3 = (bf16[1,2,8,32,256]{4,3,2,1,0:T(8,128)(2,1)S(1)}, bf16[1,2,8,32,256]{4,3,2,1,0:T(8,128)(2,1)S(1)}, u32[]{:S(2)}, u32[]{:S(2)}) collective-permute-start(bf16[1,2,8,32,256]{4,3,2,1,0:T(8,128)(2,1)S(1)} %constant_dynamic-update-slice_fusion), channel_id=1, source_target_pairs={{0,2},{1,3},{2,0},{3,1},{4,6},{5,7},{6,4},{7,5},{8,10},{9,11},{10,... | collective-permute-start | bytes 786440 | tf_op jit(solution)/shard_map/ppermute | solution.py:440
  41.5 10.8 %collective-permute-start.9 = (bf16[1,1,8,32,256]{4,3,2,1,0:T(8,128)(2,1)S(1)}, bf16[1,1,8,32,256]{4,3,2,1,0:T(8,128)(2,1)S(1)}, u32[]{:S(2)}, u32[]{:S(2)}) collective-permute-start(bf16[1,1,8,32,256]{4,3,2,1,0:T(8,128)(2,1)S(1)} %get-tuple-element.47), channel_id=1, source_target_pairs={{0,4},{1,5},{2,6},{3,7},{4,0},{5,1},{6,2},{7,3},{8,12},{9,13},{10,... | collective-permute-start | bytes 393224 | tf_op jit(solution)/shard_map/ppermute | solution.py:440
  51.1 12.5 %collective-permute-start.4 = (bf16[4,8,32,256]{3,2,1,0:T(8,128)(2,1)S(1)}, bf16[4,8,32,256]{3,2,1,0:T(8,128)(2,1)S(1)}, u32[]{:S(2)}, u32[]{:S(2)}) collective-permute-start(bf16[4,8,32,256]{3,2,1,0:T(8,128)(2,1)S(1)} %pad_maximum_fusion.1.held), channel_id=1, source_target_pairs={{0,1},{1,0},{2,3},{3,2},{4,5},{5,4},{6,7},{7,6},{8,9},{9,8},{10,11... | collective-permute-start | bytes 1572872 | tf_op jit(solution)/shard_map/ppermute | solution.py:440
  52.3 23.6 %collective-permute-start.8 = (bf16[2,8,32,1024]{3,2,1,0:T(8,128)(2,1)}, bf16[2,8,32,1024]{3,2,1,0:T(8,128)(2,1)S(1)}, u32[]{:S(2)}, u32[]{:S(2)}) collective-permute-start(bf16[2,8,32,1024]{3,2,1,0:T(8,128)(2,1)} %pad_maximum_fusion), channel_id=1, source_target_pairs={{0,8},{8,0},{16,24},{24,16},{1,9},{9,1},{17,25},{25,17},{2,10},{10... | collective-permute-start | bytes 3145736 | tf_op jit(solution)/shard_map/ppermute | solution.py:440
  53.0 14.5 %collective-permute-start.10 = (bf16[1,2,8,32,256]{4,3,2,1,0:T(8,128)(2,1)}, bf16[1,2,8,32,256]{4,3,2,1,0:T(8,128)(2,1)}, u32[]{:S(2)}, u32[]{:S(2)}) collective-permute-start(bf16[1,2,8,32,256]{4,3,2,1,0:T(8,128)(2,1)} %constant_dynamic-update-slice_fusion.2), channel_id=1, source_target_pairs={{0,2},{1,3},{2,0},{3,1},{4,6},{5,7},{6,4},{7,5},{8,10},{9,11},{10,... | collective-permute-start | bytes 786440 | tf_op jit(solution)/shard_map/ppermute | solution.py:440
  54.8 15.8 %collective-permute-start.14 = (bf16[2,1,8,32,256]{4,3,2,1,0:T(8,128)(2,1)S(1)}, bf16[2,1,8,32,256]{4,3,2,1,0:T(8,128)(2,1)S(1)}, u32[]{:S(2)}, u32[]{:S(2)}) collective-permute-start(bf16[2,1,8,32,256]{4,3,2,1,0:T(8,128)(2,1)S(1)} %get-tuple-element.55), channel_id=1, source_target_pairs={{0,4},{1,5},{2,6},{3,7},{4,0},{5,1},{6,2},{7,3},{8,12},{9,13},{10,... | collective-permute-start | bytes 786440 | tf_op jit(solution)/shard_map/ppermute | solution.py:440
  64.1 11.7 %collective-permute-start.5 = (bf16[2,8,64,256]{3,2,1,0:T(8,128)(2,1)S(1)}, bf16[2,8,64,256]{3,2,1,0:T(8,128)(2,1)S(1)}, u32[]{:S(2)}, u32[]{:S(2)}) collective-permute-start(bf16[2,8,64,256]{3,2,1,0:T(8,128)(2,1)S(1)} %get-tuple-element.44), channel_id=1, source_target_pairs={{0,16},{8,24},{16,0},{24,8},{1,17},{9,25},{17,1},{25,9},{2,18},{10... | collective-permute-start | bytes 1572872 | tf_op jit(solution)/shard_map/ppermute | solution.py:440
  68.5 13.9 %collective-permute-start.11 = (bf16[4,8,32,256]{3,2,1,0:T(8,128)(2,1)S(1)}, bf16[4,8,32,256]{3,2,1,0:T(8,128)(2,1)S(1)}, u32[]{:S(2)}, u32[]{:S(2)}) collective-permute-start(bf16[4,8,32,256]{3,2,1,0:T(8,128)(2,1)S(1)} %pad_maximum_fusion.3.held), channel_id=1, source_target_pairs={{0,1},{1,0},{2,3},{3,2},{4,5},{5,4},{6,7},{7,6},{8,9},{9,8},{10,11... | collective-permute-start | bytes 1572872 | tf_op jit(solution)/shard_map/ppermute | solution.py:440
  70.6 13.8 %collective-permute-start.15 = (bf16[2,2,8,32,256]{4,3,2,1,0:T(8,128)(2,1)S(1)}, bf16[2,2,8,32,256]{4,3,2,1,0:T(8,128)(2,1)S(1)}, u32[]{:S(2)}, u32[]{:S(2)}) collective-permute-start(bf16[2,2,8,32,256]{4,3,2,1,0:T(8,128)(2,1)S(1)} %pad_maximum_fusion.5), channel_id=1, source_target_pairs={{0,2},{1,3},{2,0},{3,1},{4,6},{5,7},{6,4},{7,5},{8,10},{9,11},{10,... | collective-permute-start | bytes 1572872 | tf_op jit(solution)/shard_map/ppermute | solution.py:440
  75.8 10.5 %collective-permute-start.6 = (bf16[2,8,64,256]{3,2,1,0:T(8,128)(2,1)S(1)}, bf16[2,8,64,256]{3,2,1,0:T(8,128)(2,1)S(1)}, u32[]{:S(2)}, u32[]{:S(2)}) collective-permute-start(bf16[2,8,64,256]{3,2,1,0:T(8,128)(2,1)S(1)} %pad_maximum_fusion.2), channel_id=1, source_target_pairs={{0,8},{8,0},{16,24},{24,16},{1,9},{9,1},{17,25},{25,17},{2,10},{10... | collective-permute-start | bytes 1572872 | tf_op jit(solution)/shard_map/ppermute | solution.py:440
  82.8 13.0 %collective-permute-start.12 = (bf16[2,8,64,256]{3,2,1,0:T(8,128)(2,1)S(1)}, bf16[2,8,64,256]{3,2,1,0:T(8,128)(2,1)S(1)}, u32[]{:S(2)}, u32[]{:S(2)}) collective-permute-start(bf16[2,8,64,256]{3,2,1,0:T(8,128)(2,1)S(1)} %get-tuple-element.52), channel_id=1, source_target_pairs={{0,16},{8,24},{16,0},{24,8},{1,17},{9,25},{17,1},{25,9},{2,18},{10... | collective-permute-start | bytes 1572872 | tf_op jit(solution)/shard_map/ppermute | solution.py:440
  84.5 12.8 %collective-permute-start.16 = (bf16[4,8,32,256]{3,2,1,0:T(8,128)(2,1)S(1)}, bf16[4,8,32,256]{3,2,1,0:T(8,128)(2,1)S(1)}, u32[]{:S(2)}, u32[]{:S(2)}) collective-permute-start(bf16[4,8,32,256]{3,2,1,0:T(8,128)(2,1)S(1)} %get-tuple-element.57.held), channel_id=1, source_target_pairs={{0,1},{1,0},{2,3},{3,2},{4,5},{5,4},{6,7},{7,6},{8,9},{9,8},{10,11... | collective-permute-start | bytes 1572872 | tf_op jit(solution)/shard_map/ppermute | solution.py:440
  95.9 3.8 %collective-permute-start.13 = (bf16[2,8,64,256]{3,2,1,0:T(8,128)(2,1)S(1)}, bf16[2,8,64,256]{3,2,1,0:T(8,128)(2,1)S(1)}, u32[]{:S(2)}, u32[]{:S(2)}) collective-permute-start(bf16[2,8,64,256]{3,2,1,0:T(8,128)(2,1)S(1)} %pad_maximum_fusion.4), channel_id=1, source_target_pairs={{0,8},{8,0},{16,24},{24,16},{1,9},{9,1},{17,25},{25,17},{2,10},{10... | collective-permute-start | bytes 1572872 | tf_op jit(solution)/shard_map/ppermute | solution.py:440
  97.7 13.1 %collective-permute-start.17 = (bf16[2,8,64,256]{3,2,1,0:T(8,128)(2,1)S(1)}, bf16[2,8,64,256]{3,2,1,0:T(8,128)(2,1)S(1)}, u32[]{:S(2)}, u32[]{:S(2)}) collective-permute-start(bf16[2,8,64,256]{3,2,1,0:T(8,128)(2,1)S(1)} %get-tuple-element.61), channel_id=1, source_target_pairs={{0,16},{8,24},{16,0},{24,8},{1,17},{9,25},{17,1},{25,9},{2,18},{10... | collective-permute-start | bytes 1572872 | tf_op jit(solution)/shard_map/ppermute | solution.py:440
  98.5 13.5 %collective-permute-start.19 = (bf16[4,8,32,256]{3,2,1,0:T(8,128)(2,1)S(1)}, bf16[4,8,32,256]{3,2,1,0:T(8,128)(2,1)S(1)}, u32[]{:S(2)}, u32[]{:S(2)}) collective-permute-start(bf16[4,8,32,256]{3,2,1,0:T(8,128)(2,1)S(1)} %get-tuple-element.63.held), channel_id=1, source_target_pairs={{0,1},{1,0},{2,3},{3,2},{4,5},{5,4},{6,7},{7,6},{8,9},{9,8},{10,11... | collective-permute-start | bytes 1572872 | tf_op jit(solution)/shard_map/ppermute | solution.py:440
  110.9 2.2 %collective-permute-start.18 = (bf16[2,8,64,256]{3,2,1,0:T(8,128)(2,1)S(1)}, bf16[2,8,64,256]{3,2,1,0:T(8,128)(2,1)S(1)}, u32[]{:S(2)}, u32[]{:S(2)}) collective-permute-start(bf16[2,8,64,256]{3,2,1,0:T(8,128)(2,1)S(1)} %pad_maximum_fusion.7), channel_id=1, source_target_pairs={{0,8},{8,0},{16,24},{24,16},{1,9},{9,1},{17,25},{25,17},{2,10},{10... | collective-permute-start | bytes 1572872 | tf_op jit(solution)/shard_map/ppermute | solution.py:440
  112.5 13.3 %collective-permute-start.20 = (bf16[2,8,64,256]{3,2,1,0:T(8,128)(2,1)S(1)}, bf16[2,8,64,256]{3,2,1,0:T(8,128)(2,1)S(1)}, u32[]{:S(2)}, u32[]{:S(2)}) collective-permute-start(bf16[2,8,64,256]{3,2,1,0:T(8,128)(2,1)S(1)} %get-tuple-element.67), channel_id=1, source_target_pairs={{0,16},{8,24},{16,0},{24,8},{1,17},{9,25},{17,1},{25,9},{2,18},{10... | collective-permute-start | bytes 1572872 | tf_op jit(solution)/shard_map/ppermute | solution.py:440
  118.4 14.8 %copy-start.3 = (f32[2,512]{1,0:T(2,128)S(1)}, f32[2,512]{1,0:T(2,128)}, u32[]{:S(2)}) copy-start(f32[2,512]{1,0:T(2,128)} %constant.35.clone.refs_5_) | copy-start | bytes 12292
  125.9 2.0 %collective-permute-start.21 = (bf16[2,8,64,256]{3,2,1,0:T(8,128)(2,1)S(1)}, bf16[2,8,64,256]{3,2,1,0:T(8,128)(2,1)S(1)}, u32[]{:S(2)}, u32[]{:S(2)}) collective-permute-start(bf16[2,8,64,256]{3,2,1,0:T(8,128)(2,1)S(1)} %pad_maximum_fusion.9), channel_id=1, source_target_pairs={{0,8},{8,0},{16,24},{24,16},{1,9},{9,1},{17,25},{25,17},{2,10},{10... | collective-permute-start | bytes 1572872 | tf_op jit(solution)/shard_map/ppermute | solution.py:440
where the time goes:
time: 143 us
  waiting for transfers between devices  56.6 us (40%)
  Pallas kernels  47.6 us (33%)
  starting transfers between devices  31.3 us (22%)
  local copies, waits for them, and re-layouts  4.36 us (3%)
  other arithmetic  3.02 us (2%)
    ppermute x20, waiting for transfers between devices, swapped(): lax.ppermute(value, axis, [(i, i ^ step) for i in range(lax.axis_size(axi...  49.5 us
    ppermute x20, starting transfers between devices, swapped(): lax.ppermute(value, axis, [(i, i ^ step) for i in range(lax.axis_size(axi...  24.8 us
    pallas_call x4, Pallas kernels, cross(): pl.pallas_call(cross_kernel, grid=(1,), in_specs=[pl.BlockSpec(a.shape, f...  21.5 us
    pallas_call x1, Pallas kernels, transform(): pl.pallas_call(transform_kernel, grid=(steps,), in_specs=[pl.BlockSpec((r...  10.6 us
    pallas_call x1, Pallas kernels, lagged(): pl.pallas_call(functools.partial(lag_kernel, scaling), grid=(groups,), in...  9.94 us
    ppermute x1, waiting for transfers between devices, per_device(): left = lax.ppermute(tail, 'chan', [(i, i + 1) for i in range(blocks - 1)])  7.02 us
    ppermute x1, starting transfers between devices, per_device(): left = lax.ppermute(tail, 'chan', [(i, i + 1) for i in range(blocks - 1)])  4.99 us
    unnamed x18, local copies, waits for them, and re-layouts  3.29 us
  transfers between devices with their start and end apart: 22, of which 13 were waited for; matrix products, arithmetic and copies ran while one was open for 3% of the time, Pallas kernels for 14%

commit v1 on v0

--- a/solution.py
+++ b/solution.py
@@ -493,14 +493,13 @@
         across = swapped(held, "chan", 1)
         if at > 1:
             finish(at - 2)
-        if at:
-            across = after(across, stacked[-1] if stacked else by_channel)
+            across = after(across, stacked[-1])
         here, near, far = pick(held, across, selector, groups)
         picked.append((here, near, swapped(far, "win", 2)))
 
     def finish(at):
         here, near, far = picked[at]
-        if stacked:
+        if at == chunks - 1:
             far = after(far, stacked[-1])
         near = swapped(jnp.stack([near, far[1]]), "win", 1)
         stacked.append(cross(here, near, far, by_channel, CHUNKS[at][0]))

time: 143 us -> 147 us (1.028); the launches traced: 143 us -> 145 us
  waiting for transfers between devices: 56.6 us -> 60.2 us
  other arithmetic: 3.02 us -> 1.03 us
  starting transfers between devices: 31.3 us -> 33.1 us
    ppermute x20, waiting for transfers between devices: 49.5 us -> 53.2 us  [swapped(): lax.ppermute(value, axis, [(i, i ^ step) for i in range(lax.axis_size(axi...]
    ppermute x20, starting transfers between devices: 24.8 us -> 26.6 us  [swapped(): lax.ppermute(value, axis, [(i, i ^ step) for i in range(lax.axis_size(axi...]
  transfers between devices with their start and end apart: 22 -> 22, of which waited for: 13 -> 11; matrix products, arithmetic and copies ran while one was open for 3% -> 1% of each run, Pallas kernels for 14% -> 14%
where the time goes in v1:
time: 147 us; the launch traced here: 145 us
  waiting for transfers between devices  60.2 us (41%)
  Pallas kernels  47.6 us (32%)
  starting transfers between devices  33.1 us (23%)
  local copies, waits for them, and re-layouts  3.03 us (2%)
    ppermute x20, waiting for transfers between devices, swapped(): lax.ppermute(value, axis, [(i, i ^ step) for i in range(lax.axis_size(axi...  53.2 us
    ppermute x20, starting transfers between devices, swapped(): lax.ppermute(value, axis, [(i, i ^ step) for i in range(lax.axis_size(axi...  26.6 us
    pallas_call x4, Pallas kernels, cross(): pl.pallas_call(cross_kernel, grid=(1,), in_specs=[pl.BlockSpec(a.shape, f...  21.5 us
    pallas_call x1, Pallas kernels, transform(): pl.pallas_call(transform_kernel, grid=(steps,), in_specs=[pl.BlockSpec((r...  10.6 us
    pallas_call x1, Pallas kernels, lagged(): pl.pallas_call(functools.partial(lag_kernel, scaling), grid=(groups,), in...  9.94 us
    ppermute x1, waiting for transfers between devices, per_device(): left = lax.ppermute(tail, 'chan', [(i, i + 1) for i in range(blocks - 1)])  7.04 us
    ppermute x1, starting transfers between devices, per_device(): left = lax.ppermute(tail, 'chan', [(i, i + 1) for i in range(blocks - 1)])  4.99 us
  transfers between devices with their start and end apart: 22, of which 11 were waited for; matrix products, arithmetic and copies ran while one was open for 1% of the time, Pallas kernels for 14%

profile of v1, /device:TPU:0, one launch (start us, length us, event | category | flops | bytes accessed | tf_op | source)
XLA Modules:
  0.0 145.4 jit_solution(7240699224056289356)
XLA Ops:
  0.0 10.6 %shard_map.82 = (f32[8,32,1024]{2,1,0:T(8,128)}, bf16[8,16,1024]{2,1,0:T(8,128)(2,1)}, bf16[8,16,1024]{2,1,0:T(8,128)(2,1)}) custom-call(bf16[256,7680]{1,0:T(8,128)(2,1)} %bitcast.28, bf16[256,7680]{1,0:T(8,128)(2,1)} %bitcast.29, bf16[256,7680]{1,0:T(8,128)(2,1)} %bitcast.30, bf16[256,7680]{1,0:T(8,128)(2,1)} %bitcast.31, ...), custom_call_target="tpu_custom_call" | custom-call | flops 4026531840 | bytes 3932160 | tf_op jit(solution)/shard_map/pallas_call | solution.py:97
  10.6 5.0 %collective-permute-start = (bf16[8,16,1024]{2,1,0:T(8,128)(2,1)}, bf16[8,16,1024]{2,1,0:T(8,128)(2,1)S(1)}, u32[]{:S(2)}, u32[]{:S(2)}) collective-permute-start(bf16[8,16,1024]{2,1,0:T(8,128)(2,1)} %get-tuple-element.35), channel_id=1, source_target_pairs={{0,1},{1,2},{2,3},{3,4},{4,5},{5,6},{6,7},{8,9},{9,10},{10,11},{11... | collective-permute-start | bytes 786440 | tf_op jit(solution)/shard_map/ppermute | solution.py:453
  15.6 1.5 %collective-permute-start.1 = (bf16[8,16,1024]{2,1,0:T(8,128)(2,1)}, bf16[8,16,1024]{2,1,0:T(8,128)(2,1)S(1)}, u32[]{:S(2)}, u32[]{:S(2)}) collective-permute-start(bf16[8,16,1024]{2,1,0:T(8,128)(2,1)} %get-tuple-element.37), channel_id=1, source_target_pairs={{1,0},{2,1},{3,2},{4,3},{5,4},{6,5},{7,6},{9,8},{10,9},{11,10},{12... | collective-permute-start | bytes 786440 | tf_op jit(solution)/shard_map/ppermute | solution.py:454
  20.0 7.0 %collective-permute-done.left = bf16[8,16,1024]{2,1,0:T(8,128)(2,1)S(1)} collective-permute-done((bf16[8,16,1024]{2,1,0:T(8,128)(2,1)}, bf16[8,16,1024]{2,1,0:T(8,128)(2,1)S(1)}, u32[]{:S(2)}, u32[]{:S(2)}) %collective-permute-start) | collective-permute-done | bytes 262176 | tf_op jit(solution)/shard_map/ppermute | solution.py:453
  29.5 4.5 %collective-permute-start.2 = (bf16[1,1,8,32,256]{4,3,2,1,0:T(8,128)(2,1)S(1)}, bf16[1,1,8,32,256]{4,3,2,1,0:T(8,128)(2,1)S(1)}, u32[]{:S(2)}, u32[]{:S(2)}) collective-permute-start(bf16[1,1,8,32,256]{4,3,2,1,0:T(8,128)(2,1)S(1)} %get-tuple-element.38), channel_id=1, source_target_pairs={{0,4},{1,5},{2,6},{3,7},{4,0},{5,1},{6,2},{7,3},{8,12},{9,13},{10,... | collective-permute-start | bytes 393224 | tf_op jit(solution)/shard_map/ppermute | solution.py:440
  34.0 1.5 %collective-permute-start.7 = (bf16[8,32,1024]{2,1,0:T(8,128)(2,1)S(1)}, bf16[8,32,1024]{2,1,0:T(8,128)(2,1)S(1)}, u32[]{:S(2)}, u32[]{:S(2)}) collective-permute-start(bf16[8,32,1024]{2,1,0:T(8,128)(2,1)S(1)} %get-tuple-element.42.here), channel_id=1, source_target_pairs={{0,16},{8,24},{16,0},{24,8},{1,17},{9,25},{17,1},{25,9},{2,18},{10... | collective-permute-start | bytes 1572872 | tf_op jit(solution)/shard_map/ppermute | solution.py:440
  35.5 5.0 %collective-permute-done.2 = bf16[1,1,8,32,256]{4,3,2,1,0:T(8,128)(2,1)S(1)} collective-permute-done((bf16[1,1,8,32,256]{4,3,2,1,0:T(8,128)(2,1)S(1)}, bf16[1,1,8,32,256]{4,3,2,1,0:T(8,128)(2,1)S(1)}, u32[]{:S(2)}, u32[]{:S(2)}) %collective-permute-start.2) | collective-permute-done | bytes 131104 | tf_op jit(solution)/shard_map/ppermute | solution.py:440
  41.4 3.4 %collective-permute-start.9 = (bf16[1,1,8,32,256]{4,3,2,1,0:T(8,128)(2,1)S(1)}, bf16[1,1,8,32,256]{4,3,2,1,0:T(8,128)(2,1)S(1)}, u32[]{:S(2)}, u32[]{:S(2)}) collective-permute-start(bf16[1,1,8,32,256]{4,3,2,1,0:T(8,128)(2,1)S(1)} %get-tuple-element.44), channel_id=1, source_target_pairs={{0,4},{1,5},{2,6},{3,7},{4,0},{5,1},{6,2},{7,3},{8,12},{9,13},{10,... | collective-permute-start | bytes 393224 | tf_op jit(solution)/shard_map/ppermute | solution.py:440
  44.9 6.2 %collective-permute-done.3 = bf16[1,2,8,32,256]{4,3,2,1,0:T(8,128)(2,1)S(1)} collective-permute-done((bf16[1,2,8,32,256]{4,3,2,1,0:T(8,128)(2,1)S(1)}, bf16[1,2,8,32,256]{4,3,2,1,0:T(8,128)(2,1)S(1)}, u32[]{:S(2)}, u32[]{:S(2)}) %collective-permute-start.3) | collective-permute-done | bytes 262176 | tf_op jit(solution)/shard_map/ppermute | solution.py:440
  51.2 2.2 %collective-permute-start.14 = (bf16[2,1,8,32,256]{4,3,2,1,0:T(8,128)(2,1)S(1)}, bf16[2,1,8,32,256]{4,3,2,1,0:T(8,128)(2,1)S(1)}, u32[]{:S(2)}, u32[]{:S(2)}) collective-permute-start(bf16[2,1,8,32,256]{4,3,2,1,0:T(8,128)(2,1)S(1)} %get-tuple-element.50), channel_id=1, source_target_pairs={{0,4},{1,5},{2,6},{3,7},{4,0},{5,1},{6,2},{7,3},{8,12},{9,13},{10,... | collective-permute-start | bytes 786440 | tf_op jit(solution)/shard_map/ppermute | solution.py:440
  53.7 2.5 %collective-permute-start.10 = (bf16[1,2,8,32,256]{4,3,2,1,0:T(8,128)(2,1)S(1)}, bf16[1,2,8,32,256]{4,3,2,1,0:T(8,128)(2,1)S(1)}, u32[]{:S(2)}, u32[]{:S(2)}) collective-permute-start(bf16[1,2,8,32,256]{4,3,2,1,0:T(8,128)(2,1)S(1)} %constant_dynamic-update-slice_fusion.2), channel_id=1, source_target_pairs={{0,2},{1,3},{2,0},{3,1},{4,6},{5,7},{6,4},{7,5},{8,10},{9,11},{10,... | collective-permute-start | bytes 786440 | tf_op jit(solution)/shard_map/ppermute | solution.py:440
  56.3 7.3 %collective-permute-done.4.across = bf16[4,8,32,256]{3,2,1,0:T(8,128)(2,1)S(1)} collective-permute-done((bf16[4,8,32,256]{3,2,1,0:T(8,128)(2,1)S(1)}, bf16[4,8,32,256]{3,2,1,0:T(8,128)(2,1)S(1)}, u32[]{:S(2)}, u32[]{:S(2)}) %collective-permute-start.4) | collective-permute-done | bytes 524320 | tf_op jit(solution)/shard_map/ppermute | solution.py:440
  64.0 1.6 %collective-permute-start.5 = (bf16[2,8,64,256]{3,2,1,0:T(8,128)(2,1)S(1)}, bf16[2,8,64,256]{3,2,1,0:T(8,128)(2,1)S(1)}, u32[]{:S(2)}, u32[]{:S(2)}) collective-permute-start(bf16[2,8,64,256]{3,2,1,0:T(8,128)(2,1)S(1)} %get-tuple-element.41), channel_id=1, source_target_pairs={{0,16},{8,24},{16,0},{24,8},{1,17},{9,25},{17,1},{25,9},{2,18},{10... | collective-permute-start | bytes 1572872 | tf_op jit(solution)/shard_map/ppermute | solution.py:440
  65.9 1.7 %collective-permute-start.11 = (bf16[4,8,32,256]{3,2,1,0:T(8,128)(2,1)S(1)}, bf16[4,8,32,256]{3,2,1,0:T(8,128)(2,1)S(1)}, u32[]{:S(2)}, u32[]{:S(2)}) collective-permute-start(bf16[4,8,32,256]{3,2,1,0:T(8,128)(2,1)S(1)} %pad_maximum_fusion.3.held), channel_id=1, source_target_pairs={{0,1},{1,0},{2,3},{3,2},{4,5},{5,4},{6,7},{7,6},{8,9},{9,8},{10,11... | collective-permute-start | bytes 1572872 | tf_op jit(solution)/shard_map/ppermute | solution.py:440
  67.7 7.8 %collective-permute-done.5.far = bf16[2,8,64,256]{3,2,1,0:T(8,128)(2,1)S(1)} collective-permute-done((bf16[2,8,64,256]{3,2,1,0:T(8,128)(2,1)S(1)}, bf16[2,8,64,256]{3,2,1,0:T(8,128)(2,1)S(1)}, u32[]{:S(2)}, u32[]{:S(2)}) %collective-permute-start.5) | collective-permute-done | bytes 524320 | tf_op jit(solution)/shard_map/ppermute | solution.py:440
  75.7 2.0 %collective-permute-done.15 = bf16[2,2,8,32,256]{4,3,2,1,0:T(8,128)(2,1)S(1)} collective-permute-done((bf16[2,2,8,32,256]{4,3,2,1,0:T(8,128)(2,1)S(1)}, bf16[2,2,8,32,256]{4,3,2,1,0:T(8,128)(2,1)S(1)}, u32[]{:S(2)}, u32[]{:S(2)}) %collective-permute-start.15) | collective-permute-done | bytes 524320 | tf_op jit(solution)/shard_map/ppermute | solution.py:440
  77.8 2.5 %collective-permute-done.11.across = bf16[4,8,32,256]{3,2,1,0:T(8,128)(2,1)S(1)} collective-permute-done((bf16[4,8,32,256]{3,2,1,0:T(8,128)(2,1)S(1)}, bf16[4,8,32,256]{3,2,1,0:T(8,128)(2,1)S(1)}, u32[]{:S(2)}, u32[]{:S(2)}) %collective-permute-start.11) | collective-permute-done | bytes 524320 | tf_op jit(solution)/shard_map/ppermute | solution.py:440
  80.8 1.7 %collective-permute-start.16 = (bf16[4,8,32,256]{3,2,1,0:T(8,128)(2,1)S(1)}, bf16[4,8,32,256]{3,2,1,0:T(8,128)(2,1)S(1)}, u32[]{:S(2)}, u32[]{:S(2)}) collective-permute-start(bf16[4,8,32,256]{3,2,1,0:T(8,128)(2,1)S(1)} %pad_maximum_fusion.6.held), channel_id=1, source_target_pairs={{0,1},{1,0},{2,3},{3,2},{4,5},{5,4},{6,7},{7,6},{8,9},{9,8},{10,11... | collective-permute-start | bytes 1572872 | tf_op jit(solution)/shard_map/ppermute | solution.py:440
  82.5 1.5 %collective-permute-start.12 = (bf16[2,8,64,256]{3,2,1,0:T(8,128)(2,1)S(1)}, bf16[2,8,64,256]{3,2,1,0:T(8,128)(2,1)S(1)}, u32[]{:S(2)}, u32[]{:S(2)}) collective-permute-start(bf16[2,8,64,256]{3,2,1,0:T(8,128)(2,1)S(1)} %get-tuple-element.48), channel_id=1, source_target_pairs={{0,16},{8,24},{16,0},{24,8},{1,17},{9,25},{17,1},{25,9},{2,18},{10... | collective-permute-start | bytes 1572872 | tf_op jit(solution)/shard_map/ppermute | solution.py:440
  84.0 1.4 shard_map.86.by_channel
  85.4 5.3 %shard_map.87.refs_0_ = bf16[4,2,512,128]{3,2,1,0:T(8,128)(2,1)S(1)} custom-call(bf16[8,64,256]{2,1,0:T(8,128)(2,1)S(1)} %get-tuple-element.39.here, bf16[2,8,64,256]{3,2,1,0:T(8,128)(2,1)S(1)} %collective-permute-done.6.near, bf16[2,8,64,256]{3,2,1,0:T(8,128)(2,1)S(1)} %collective-permute-done.5.far, bf16[8,512,256]{2,1,0:T(8,128)(2,1)S(1)} %shard_map.86.by_channel), custom_call_target="tpu_custom_call" | custom-call | flops 603979776 | bytes 4194304 | tf_op jit(solution)/shard_map/pallas_call | solution.py:311
  90.7 3.7 %collective-permute-done.16.across = bf16[4,8,32,256]{3,2,1,0:T(8,128)(2,1)S(1)} collective-permute-done((bf16[4,8,32,256]{3,2,1,0:T(8,128)(2,1)S(1)}, bf16[4,8,32,256]{3,2,1,0:T(8,128)(2,1)S(1)}, u32[]{:S(2)}, u32[]{:S(2)}) %collective-permute-start.16) | collective-permute-done | bytes 524320 | tf_op jit(solution)/shard_map/ppermute | solution.py:440
  94.8 1.5 %collective-permute-start.17 = (bf16[2,8,64,256]{3,2,1,0:T(8,128)(2,1)S(1)}, bf16[2,8,64,256]{3,2,1,0:T(8,128)(2,1)S(1)}, u32[]{:S(2)}, u32[]{:S(2)}) collective-permute-start(bf16[2,8,64,256]{3,2,1,0:T(8,128)(2,1)S(1)} %get-tuple-element.56), channel_id=1, source_target_pairs={{0,16},{8,24},{16,0},{24,8},{1,17},{9,25},{17,1},{25,9},{2,18},{10... | collective-permute-start | bytes 1572872 | tf_op jit(solution)/shard_map/ppermute | solution.py:440
  96.5 1.8 %collective-permute-start.19 = (bf16[4,8,32,256]{3,2,1,0:T(8,128)(2,1)S(1)}, bf16[4,8,32,256]{3,2,1,0:T(8,128)(2,1)S(1)}, u32[]{:S(2)}, u32[]{:S(2)}) collective-permute-start(bf16[4,8,32,256]{3,2,1,0:T(8,128)(2,1)S(1)} %pad_maximum_fusion.8.held), channel_id=1, source_target_pairs={{0,1},{1,0},{2,3},{3,2},{4,5},{5,4},{6,7},{7,6},{8,9},{9,8},{10,11... | collective-permute-start | bytes 1572872 | tf_op jit(solution)/shard_map/ppermute | solution.py:440
  98.3 9.2 %collective-permute-done.17.far = bf16[2,8,64,256]{3,2,1,0:T(8,128)(2,1)S(1)} collective-permute-done((bf16[2,8,64,256]{3,2,1,0:T(8,128)(2,1)S(1)}, bf16[2,8,64,256]{3,2,1,0:T(8,128)(2,1)S(1)}, u32[]{:S(2)}, u32[]{:S(2)}) %collective-permute-start.17) | collective-permute-done | bytes 524320 | tf_op jit(solution)/shard_map/ppermute | solution.py:440
  107.7 5.5 %shard_map.89.refs_1_ = bf16[4,2,512,128]{3,2,1,0:T(8,128)(2,1)S(1)} custom-call(bf16[8,64,256]{2,1,0:T(8,128)(2,1)S(1)} %get-tuple-element.46.here, bf16[2,8,64,256]{3,2,1,0:T(8,128)(2,1)S(1)} %collective-permute-done.13.near, bf16[2,8,64,256]{3,2,1,0:T(8,128)(2,1)S(1)} %collective-permute-done.12.far, bf16[8,512,256]{2,1,0:T(8,128)(2,1)S(1)} %shard_map.86.by_channel), custom_call_target="tpu_custom_call" | custom-call | flops 603979776 | bytes 4194304 | tf_op jit(solution)/shard_map/pallas_call | solution.py:311
  113.7 1.5 %collective-permute-start.20 = (bf16[2,8,64,256]{3,2,1,0:T(8,128)(2,1)S(1)}, bf16[2,8,64,256]{3,2,1,0:T(8,128)(2,1)S(1)}, u32[]{:S(2)}, u32[]{:S(2)}) collective-permute-start(bf16[2,8,64,256]{3,2,1,0:T(8,128)(2,1)S(1)} %get-tuple-element.61), channel_id=1, source_target_pairs={{0,16},{8,24},{16,0},{24,8},{1,17},{9,25},{17,1},{25,9},{2,18},{10... | collective-permute-start | bytes 1572872 | tf_op jit(solution)/shard_map/ppermute | solution.py:440
  115.2 5.3 %shard_map.91.refs_2_ = bf16[4,2,512,128]{3,2,1,0:T(8,128)(2,1)S(1)} custom-call(bf16[8,64,256]{2,1,0:T(8,128)(2,1)S(1)} %get-tuple-element.54.here, bf16[2,8,64,256]{3,2,1,0:T(8,128)(2,1)S(1)} %collective-permute-done.18.near, bf16[2,8,64,256]{3,2,1,0:T(8,128)(2,1)S(1)} %collective-permute-done.17.far, bf16[8,512,256]{2,1,0:T(8,128)(2,1)S(1)} %shard_map.86.by_channel), custom_call_target="tpu_custom_call" | custom-call | flops 603979776 | bytes 4194304 | tf_op jit(solution)/shard_map/pallas_call | solution.py:311
  120.5 7.6 %collective-permute-done.20.far = bf16[2,8,64,256]{3,2,1,0:T(8,128)(2,1)S(1)} collective-permute-done((bf16[2,8,64,256]{3,2,1,0:T(8,128)(2,1)S(1)}, bf16[2,8,64,256]{3,2,1,0:T(8,128)(2,1)S(1)}, u32[]{:S(2)}, u32[]{:S(2)}) %collective-permute-start.20) | collective-permute-done | bytes 524320 | tf_op jit(solution)/shard_map/ppermute | solution.py:440
  128.2 1.9 %collective-permute-done.21.near = bf16[2,8,64,256]{3,2,1,0:T(8,128)(2,1)S(1)} collective-permute-done((bf16[2,8,64,256]{3,2,1,0:T(8,128)(2,1)S(1)}, bf16[2,8,64,256]{3,2,1,0:T(8,128)(2,1)S(1)}, u32[]{:S(2)}, u32[]{:S(2)}) %collective-permute-start.21) | collective-permute-done | bytes 524320 | tf_op jit(solution)/shard_map/ppermute | solution.py:440
  130.1 5.3 %shard_map.93.refs_3_ = bf16[4,2,512,128]{3,2,1,0:T(8,128)(2,1)S(1)} custom-call(bf16[8,64,256]{2,1,0:T(8,128)(2,1)S(1)} %get-tuple-element.59.here, bf16[2,8,64,256]{3,2,1,0:T(8,128)(2,1)S(1)} %collective-permute-done.21.near, bf16[2,8,64,256]{3,2,1,0:T(8,128)(2,1)S(1)} %collective-permute-done.20.far, bf16[8,512,256]{2,1,0:T(8,128)(2,1)S(1)} %shard_map.86.by_channel), custom_call_target="tpu_custom_call" | custom-call | flops 603979776 | bytes 4194304 | tf_op jit(solution)/shard_map/pallas_call | solution.py:311
  135.5 9.9 %shard_map.94 = f32[64,32,2048]{2,1,0:T(8,128)} custom-call(bf16[4,2,512,128]{3,2,1,0:T(8,128)(2,1)S(1)} %shard_map.87.refs_0_, bf16[4,2,512,128]{3,2,1,0:T(8,128)(2,1)S(1)} %shard_map.89.refs_1_, bf16[4,2,512,128]{3,2,1,0:T(8,128)(2,1)S(1)} %shard_map.91.refs_2_, bf16[4,2,512,128]{3,2,1,0:T(8,128)(2,1)S(1)} %shard_map.93.refs_3_, ...), custom_call_target="tpu_custom_call" | custom-call | flops 4294967296 | bytes 16777216 | tf_op jit(solution)/shard_map/pallas_call | solution.py:361
  (73 shorter events, 9.6 us)
Async XLA Ops:
  0.0 17.1 %copy-start.5 = (bf16[32]{0:T(256)(128)(2,1)S(1)}, bf16[32]{0:T(256)(128)(2,1)}, u32[]{:S(2)}) copy-start(bf16[32]{0:T(256)(128)(2,1)} %param.9) | copy-start | bytes 196
  0.0 17.2 %copy-start.2 = (f32[512,272]{1,0:T(8,128)S(1)}, f32[512,272]{1,0:T(8,128)}, u32[]{:S(2)}) copy-start(f32[512,272]{1,0:T(8,128)} %constant.33.clone.angles) | copy-start | bytes 1671172
  0.0 27.0 %copy-start.4 = (s32[32]{0:T(128)S(1)}, s32[32]{0:T(128)}, u32[]{:S(2)}) copy-start(s32[32]{0:T(128)} %param.10) | copy-start | bytes 388
  10.6 23.4 %copy-start.7 = (s32[8]{0:T(128)S(1)}, s32[8]{0:T(128)}, u32[]{:S(2)}) copy-start(s32[8]{0:T(128)} %constant.34.clone) | copy-start | bytes 100
  10.6 30.8 %copy-start.6 = (s32[256]{0:T(256)S(1)}, s32[256]{0:T(256)}, u32[]{:S(2)}) copy-start(s32[256]{0:T(256)} %param.11) | copy-start | bytes 3076
  10.6 16.5 %collective-permute-start = (bf16[8,16,1024]{2,1,0:T(8,128)(2,1)}, bf16[8,16,1024]{2,1,0:T(8,128)(2,1)S(1)}, u32[]{:S(2)}, u32[]{:S(2)}) collective-permute-start(bf16[8,16,1024]{2,1,0:T(8,128)(2,1)} %get-tuple-element.35), channel_id=1, source_target_pairs={{0,1},{1,2},{2,3},{3,4},{4,5},{5,6},{6,7},{8,9},{9,10},{10,11},{11... | collective-permute-start | bytes 786440 | tf_op jit(solution)/shard_map/ppermute | solution.py:453
  15.6 11.5 %collective-permute-start.1 = (bf16[8,16,1024]{2,1,0:T(8,128)(2,1)}, bf16[8,16,1024]{2,1,0:T(8,128)(2,1)S(1)}, u32[]{:S(2)}, u32[]{:S(2)}) collective-permute-start(bf16[8,16,1024]{2,1,0:T(8,128)(2,1)} %get-tuple-element.37), channel_id=1, source_target_pairs={{1,0},{2,1},{3,2},{4,3},{5,4},{6,5},{7,6},{9,8},{10,9},{11,10},{12... | collective-permute-start | bytes 786440 | tf_op jit(solution)/shard_map/ppermute | solution.py:454
  18.5 1.4 copy-start
  27.0 1.2 copy-start.1
  29.5 10.9 %collective-permute-start.2 = (bf16[1,1,8,32,256]{4,3,2,1,0:T(8,128)(2,1)S(1)}, bf16[1,1,8,32,256]{4,3,2,1,0:T(8,128)(2,1)S(1)}, u32[]{:S(2)}, u32[]{:S(2)}) collective-permute-start(bf16[1,1,8,32,256]{4,3,2,1,0:T(8,128)(2,1)S(1)} %get-tuple-element.38), channel_id=1, source_target_pairs={{0,4},{1,5},{2,6},{3,7},{4,0},{5,1},{6,2},{7,3},{8,12},{9,13},{10,... | collective-permute-start | bytes 393224 | tf_op jit(solution)/shard_map/ppermute | solution.py:440
  34.0 17.2 %collective-permute-start.7 = (bf16[8,32,1024]{2,1,0:T(8,128)(2,1)S(1)}, bf16[8,32,1024]{2,1,0:T(8,128)(2,1)S(1)}, u32[]{:S(2)}, u32[]{:S(2)}) collective-permute-start(bf16[8,32,1024]{2,1,0:T(8,128)(2,1)S(1)} %get-tuple-element.42.here), channel_id=1, source_target_pairs={{0,16},{8,24},{16,0},{24,8},{1,17},{9,25},{17,1},{25,9},{2,18},{10... | collective-permute-start | bytes 1572872 | tf_op jit(solution)/shard_map/ppermute | solution.py:440
  40.5 10.6 %collective-permute-start.3 = (bf16[1,2,8,32,256]{4,3,2,1,0:T(8,128)(2,1)S(1)}, bf16[1,2,8,32,256]{4,3,2,1,0:T(8,128)(2,1)S(1)}, u32[]{:S(2)}, u32[]{:S(2)}) collective-permute-start(bf16[1,2,8,32,256]{4,3,2,1,0:T(8,128)(2,1)S(1)} %constant_dynamic-update-slice_fusion), channel_id=1, source_target_pairs={{0,2},{1,3},{2,0},{3,1},{4,6},{5,7},{6,4},{7,5},{8,10},{9,11},{10,... | collective-permute-start | bytes 786440 | tf_op jit(solution)/shard_map/ppermute | solution.py:440
  41.4 9.8 %collective-permute-start.9 = (bf16[1,1,8,32,256]{4,3,2,1,0:T(8,128)(2,1)S(1)}, bf16[1,1,8,32,256]{4,3,2,1,0:T(8,128)(2,1)S(1)}, u32[]{:S(2)}, u32[]{:S(2)}) collective-permute-start(bf16[1,1,8,32,256]{4,3,2,1,0:T(8,128)(2,1)S(1)} %get-tuple-element.44), channel_id=1, source_target_pairs={{0,4},{1,5},{2,6},{3,7},{4,0},{5,1},{6,2},{7,3},{8,12},{9,13},{10,... | collective-permute-start | bytes 393224 | tf_op jit(solution)/shard_map/ppermute | solution.py:440
  51.1 12.5 %collective-permute-start.4 = (bf16[4,8,32,256]{3,2,1,0:T(8,128)(2,1)S(1)}, bf16[4,8,32,256]{3,2,1,0:T(8,128)(2,1)S(1)}, u32[]{:S(2)}, u32[]{:S(2)}) collective-permute-start(bf16[4,8,32,256]{3,2,1,0:T(8,128)(2,1)S(1)} %pad_maximum_fusion.1.held), channel_id=1, source_target_pairs={{0,1},{1,0},{2,3},{3,2},{4,5},{5,4},{6,7},{7,6},{8,9},{9,8},{10,11... | collective-permute-start | bytes 1572872 | tf_op jit(solution)/shard_map/ppermute | solution.py:440
  51.2 14.3 %collective-permute-start.14 = (bf16[2,1,8,32,256]{4,3,2,1,0:T(8,128)(2,1)S(1)}, bf16[2,1,8,32,256]{4,3,2,1,0:T(8,128)(2,1)S(1)}, u32[]{:S(2)}, u32[]{:S(2)}) collective-permute-start(bf16[2,1,8,32,256]{4,3,2,1,0:T(8,128)(2,1)S(1)} %get-tuple-element.50), channel_id=1, source_target_pairs={{0,4},{1,5},{2,6},{3,7},{4,0},{5,1},{6,2},{7,3},{8,12},{9,13},{10,... | collective-permute-start | bytes 786440 | tf_op jit(solution)/shard_map/ppermute | solution.py:440
  53.7 12.1 %collective-permute-start.10 = (bf16[1,2,8,32,256]{4,3,2,1,0:T(8,128)(2,1)S(1)}, bf16[1,2,8,32,256]{4,3,2,1,0:T(8,128)(2,1)S(1)}, u32[]{:S(2)}, u32[]{:S(2)}) collective-permute-start(bf16[1,2,8,32,256]{4,3,2,1,0:T(8,128)(2,1)S(1)} %constant_dynamic-update-slice_fusion.2), channel_id=1, source_target_pairs={{0,2},{1,3},{2,0},{3,1},{4,6},{5,7},{6,4},{7,5},{8,10},{9,11},{10,... | collective-permute-start | bytes 786440 | tf_op jit(solution)/shard_map/ppermute | solution.py:440
  64.0 11.5 %collective-permute-start.5 = (bf16[2,8,64,256]{3,2,1,0:T(8,128)(2,1)S(1)}, bf16[2,8,64,256]{3,2,1,0:T(8,128)(2,1)S(1)}, u32[]{:S(2)}, u32[]{:S(2)}) collective-permute-start(bf16[2,8,64,256]{3,2,1,0:T(8,128)(2,1)S(1)} %get-tuple-element.41), channel_id=1, source_target_pairs={{0,16},{8,24},{16,0},{24,8},{1,17},{9,25},{17,1},{25,9},{2,18},{10... | collective-permute-start | bytes 1572872 | tf_op jit(solution)/shard_map/ppermute | solution.py:440
  65.6 12.1 %collective-permute-start.15 = (bf16[2,2,8,32,256]{4,3,2,1,0:T(8,128)(2,1)S(1)}, bf16[2,2,8,32,256]{4,3,2,1,0:T(8,128)(2,1)S(1)}, u32[]{:S(2)}, u32[]{:S(2)}) collective-permute-start(bf16[2,2,8,32,256]{4,3,2,1,0:T(8,128)(2,1)S(1)} %pad_maximum_fusion.5), channel_id=1, source_target_pairs={{0,2},{1,3},{2,0},{3,1},{4,6},{5,7},{6,4},{7,5},{8,10},{9,11},{10,... | collective-permute-start | bytes 1572872 | tf_op jit(solution)/shard_map/ppermute | solution.py:440
  65.8 18.2 %collective-permute-start.8 = (bf16[2,8,32,1024]{3,2,1,0:T(8,128)(2,1)S(1)}, bf16[2,8,32,1024]{3,2,1,0:T(8,128)(2,1)S(1)}, u32[]{:S(2)}, u32[]{:S(2)}) collective-permute-start(bf16[2,8,32,1024]{3,2,1,0:T(8,128)(2,1)S(1)} %pad_maximum_fusion), channel_id=1, source_target_pairs={{0,8},{8,0},{16,24},{24,16},{1,9},{9,1},{17,25},{25,17},{2,10},{10... | collective-permute-start | bytes 3145736 | tf_op jit(solution)/shard_map/ppermute | solution.py:440
  65.9 14.4 %collective-permute-start.11 = (bf16[4,8,32,256]{3,2,1,0:T(8,128)(2,1)S(1)}, bf16[4,8,32,256]{3,2,1,0:T(8,128)(2,1)S(1)}, u32[]{:S(2)}, u32[]{:S(2)}) collective-permute-start(bf16[4,8,32,256]{3,2,1,0:T(8,128)(2,1)S(1)} %pad_maximum_fusion.3.held), channel_id=1, source_target_pairs={{0,1},{1,0},{2,3},{3,2},{4,5},{5,4},{6,7},{7,6},{8,9},{9,8},{10,11... | collective-permute-start | bytes 1572872 | tf_op jit(solution)/shard_map/ppermute | solution.py:440
  75.6 9.7 %collective-permute-start.6 = (bf16[2,8,64,256]{3,2,1,0:T(8,128)(2,1)S(1)}, bf16[2,8,64,256]{3,2,1,0:T(8,128)(2,1)S(1)}, u32[]{:S(2)}, u32[]{:S(2)}) collective-permute-start(bf16[2,8,64,256]{3,2,1,0:T(8,128)(2,1)S(1)} %pad_maximum_fusion.2), channel_id=1, source_target_pairs={{0,8},{8,0},{16,24},{24,16},{1,9},{9,1},{17,25},{25,17},{2,10},{10... | collective-permute-start | bytes 1572872 | tf_op jit(solution)/shard_map/ppermute | solution.py:440
  80.8 13.6 %collective-permute-start.16 = (bf16[4,8,32,256]{3,2,1,0:T(8,128)(2,1)S(1)}, bf16[4,8,32,256]{3,2,1,0:T(8,128)(2,1)S(1)}, u32[]{:S(2)}, u32[]{:S(2)}) collective-permute-start(bf16[4,8,32,256]{3,2,1,0:T(8,128)(2,1)S(1)} %pad_maximum_fusion.6.held), channel_id=1, source_target_pairs={{0,1},{1,0},{2,3},{3,2},{4,5},{5,4},{6,7},{7,6},{8,9},{9,8},{10,11... | collective-permute-start | bytes 1572872 | tf_op jit(solution)/shard_map/ppermute | solution.py:440
  82.5 13.8 %collective-permute-start.12 = (bf16[2,8,64,256]{3,2,1,0:T(8,128)(2,1)S(1)}, bf16[2,8,64,256]{3,2,1,0:T(8,128)(2,1)S(1)}, u32[]{:S(2)}, u32[]{:S(2)}) collective-permute-start(bf16[2,8,64,256]{3,2,1,0:T(8,128)(2,1)S(1)} %get-tuple-element.48), channel_id=1, source_target_pairs={{0,16},{8,24},{16,0},{24,8},{1,17},{9,25},{17,1},{25,9},{2,18},{10... | collective-permute-start | bytes 1572872 | tf_op jit(solution)/shard_map/ppermute | solution.py:440
  94.8 12.7 %collective-permute-start.17 = (bf16[2,8,64,256]{3,2,1,0:T(8,128)(2,1)S(1)}, bf16[2,8,64,256]{3,2,1,0:T(8,128)(2,1)S(1)}, u32[]{:S(2)}, u32[]{:S(2)}) collective-permute-start(bf16[2,8,64,256]{3,2,1,0:T(8,128)(2,1)S(1)} %get-tuple-element.56), channel_id=1, source_target_pairs={{0,16},{8,24},{16,0},{24,8},{1,17},{9,25},{17,1},{25,9},{2,18},{10... | collective-permute-start | bytes 1572872 | tf_op jit(solution)/shard_map/ppermute | solution.py:440
  96.4 11.3 %collective-permute-start.13 = (bf16[2,8,64,256]{3,2,1,0:T(8,128)(2,1)S(1)}, bf16[2,8,64,256]{3,2,1,0:T(8,128)(2,1)S(1)}, u32[]{:S(2)}, u32[]{:S(2)}) collective-permute-start(bf16[2,8,64,256]{3,2,1,0:T(8,128)(2,1)S(1)} %pad_maximum_fusion.4), channel_id=1, source_target_pairs={{0,8},{8,0},{16,24},{24,16},{1,9},{9,1},{17,25},{25,17},{2,10},{10... | collective-permute-start | bytes 1572872 | tf_op jit(solution)/shard_map/ppermute | solution.py:440
  96.5 16.7 %collective-permute-start.19 = (bf16[4,8,32,256]{3,2,1,0:T(8,128)(2,1)S(1)}, bf16[4,8,32,256]{3,2,1,0:T(8,128)(2,1)S(1)}, u32[]{:S(2)}, u32[]{:S(2)}) collective-permute-start(bf16[4,8,32,256]{3,2,1,0:T(8,128)(2,1)S(1)} %pad_maximum_fusion.8.held), channel_id=1, source_target_pairs={{0,1},{1,0},{2,3},{3,2},{4,5},{5,4},{6,7},{7,6},{8,9},{9,8},{10,11... | collective-permute-start | bytes 1572872 | tf_op jit(solution)/shard_map/ppermute | solution.py:440
  107.6 7.5 %collective-permute-start.18 = (bf16[2,8,64,256]{3,2,1,0:T(8,128)(2,1)S(1)}, bf16[2,8,64,256]{3,2,1,0:T(8,128)(2,1)S(1)}, u32[]{:S(2)}, u32[]{:S(2)}) collective-permute-start(bf16[2,8,64,256]{3,2,1,0:T(8,128)(2,1)S(1)} %pad_maximum_fusion.7), channel_id=1, source_target_pairs={{0,8},{8,0},{16,24},{24,16},{1,9},{9,1},{17,25},{25,17},{2,10},{10... | collective-permute-start | bytes 1572872 | tf_op jit(solution)/shard_map/ppermute | solution.py:440
  113.7 14.4 %collective-permute-start.20 = (bf16[2,8,64,256]{3,2,1,0:T(8,128)(2,1)S(1)}, bf16[2,8,64,256]{3,2,1,0:T(8,128)(2,1)S(1)}, u32[]{:S(2)}, u32[]{:S(2)}) collective-permute-start(bf16[2,8,64,256]{3,2,1,0:T(8,128)(2,1)S(1)} %get-tuple-element.61), channel_id=1, source_target_pairs={{0,16},{8,24},{16,0},{24,8},{1,17},{9,25},{17,1},{25,9},{2,18},{10... | collective-permute-start | bytes 1572872 | tf_op jit(solution)/shard_map/ppermute | solution.py:440
  120.5 15.0 %copy-start.3 = (f32[2,512]{1,0:T(2,128)S(1)}, f32[2,512]{1,0:T(2,128)}, u32[]{:S(2)}) copy-start(f32[2,512]{1,0:T(2,128)} %constant.35.clone.refs_5_) | copy-start | bytes 12292
  128.2 2.0 %collective-permute-start.21 = (bf16[2,8,64,256]{3,2,1,0:T(8,128)(2,1)S(1)}, bf16[2,8,64,256]{3,2,1,0:T(8,128)(2,1)S(1)}, u32[]{:S(2)}, u32[]{:S(2)}) collective-permute-start(bf16[2,8,64,256]{3,2,1,0:T(8,128)(2,1)S(1)} %pad_maximum_fusion.9), channel_id=1, source_target_pairs={{0,8},{8,0},{16,24},{24,16},{1,9},{9,1},{17,25},{25,17},{2,10},{10... | collective-permute-start | bytes 1572872 | tf_op jit(solution)/shard_map/ppermute | solution.py:440

commit v2 on v0

--- a/solution.py
+++ b/solution.py
@@ -19,7 +19,7 @@
 STEP = 640
 FINE = 32
 CHUNKS = tuple((start, 128) for start in range(0, F, 128))
-Z_GROUPS = ((0, 1), (1, 2), (2, 4))
+Z_GROUPS = ((0, 1), (1, 3), (3, 4))
 GROUP = 16
 LAG_FINE = 128
 LAG_ROWS = 8
@@ -483,8 +483,8 @@
                 held = jnp.concatenate([held, received], axis=1)
                 if step == blocks // 2:
                     first_held.append(held)
-                    if len(gathered) > 1:
-                        held = after(held, picked[0][0])
+                    if gathered:
+                        held = after(held, picked[0][0] if picked else gathered[0])
             step //= 2
         gathered.extend(jnp.concatenate([held[i], received[i]], axis=0) for i in range(part.shape[0]))
 
@@ -493,8 +493,7 @@
         across = swapped(held, "chan", 1)
         if at > 1:
             finish(at - 2)
-        if at:
-            across = after(across, stacked[-1] if stacked else by_channel)
+        across = after(across, (stacked[-1] if stacked else by_channel) if at else gathered[1])
         here, near, far = pick(held, across, selector, groups)
         picked.append((here, near, swapped(far, "win", 2)))
 
@@ -508,7 +507,7 @@
     first_held = []
     for part in parts:
         gather(after(part, [first_held[-1]] + [own_far] * (len(first_held) > 1)) if first_held else part)
-        if len(gathered) == 2:
+        if len(gathered) > 1 and not picked:
             exchange(0)
     for at in range(1, chunks):
         exchange(at)

time: 143 us -> 151 us (1.056)
  waiting for transfers between devices: 56.6 us -> 65.1 us
  starting transfers between devices: 31.3 us -> 33.8 us
  other arithmetic: 3.02 us -> 1 us
    ppermute x20, waiting for transfers between devices: 49.5 us -> 58.1 us  [swapped(): lax.ppermute(value, axis, [(i, i ^ step) for i in range(lax.axis_size(axi...]
    ppermute x20, starting transfers between devices: 24.8 us -> 27.3 us  [swapped(): lax.ppermute(value, axis, [(i, i ^ step) for i in range(lax.axis_size(axi...]
  transfers between devices with their start and end apart: 22 -> 22, of which waited for: 13 -> 13; matrix products, arithmetic and copies ran while one was open for 3% -> 1% of each run, Pallas kernels for 14% -> 14%
where the time goes in v2:
time: 151 us
  waiting for transfers between devices  65.1 us (43%)
  Pallas kernels  47.6 us (32%)
  starting transfers between devices  33.8 us (22%)
  local copies, waits for them, and re-layouts  3.05 us (2%)
    ppermute x20, waiting for transfers between devices, swapped(): lax.ppermute(value, axis, [(i, i ^ step) for i in range(lax.axis_size(axi...  58.1 us
    ppermute x20, starting transfers between devices, swapped(): lax.ppermute(value, axis, [(i, i ^ step) for i in range(lax.axis_size(axi...  27.3 us
    pallas_call x4, Pallas kernels, cross(): pl.pallas_call(cross_kernel, grid=(1,), in_specs=[pl.BlockSpec(a.shape, f...  21.5 us
    pallas_call x1, Pallas kernels, transform(): pl.pallas_call(transform_kernel, grid=(steps,), in_specs=[pl.BlockSpec((r...  10.6 us
    pallas_call x1, Pallas kernels, lagged(): pl.pallas_call(functools.partial(lag_kernel, scaling), grid=(groups,), in...  9.95 us
    ppermute x1, waiting for transfers between devices, per_device(): left = lax.ppermute(tail, 'chan', [(i, i + 1) for i in range(blocks - 1)])  7.01 us
    ppermute x1, starting transfers between devices, per_device(): left = lax.ppermute(tail, 'chan', [(i, i + 1) for i in range(blocks - 1)])  4.98 us
  transfers between devices with their start and end apart: 22, of which 13 were waited for; matrix products, arithmetic and copies ran while one was open for 1% of the time, Pallas kernels for 14%

profile of v2, /device:TPU:0, one launch (start us, length us, event | category | flops | bytes accessed | tf_op | source)
XLA Modules:
  0.0 151.0 jit_solution(17343670568717697550)
XLA Ops:
  0.0 10.6 %shard_map.82 = (f32[8,32,1024]{2,1,0:T(8,128)}, bf16[8,16,1024]{2,1,0:T(8,128)(2,1)}, bf16[8,16,1024]{2,1,0:T(8,128)(2,1)}) custom-call(bf16[256,7680]{1,0:T(8,128)(2,1)} %bitcast.28, bf16[256,7680]{1,0:T(8,128)(2,1)} %bitcast.29, bf16[256,7680]{1,0:T(8,128)(2,1)} %bitcast.30, bf16[256,7680]{1,0:T(8,128)(2,1)} %bitcast.31, ...), custom_call_target="tpu_custom_call" | custom-call | flops 4026531840 | bytes 3932160 | tf_op jit(solution)/shard_map/pallas_call | solution.py:97
  10.6 5.0 %collective-permute-start = (bf16[8,16,1024]{2,1,0:T(8,128)(2,1)}, bf16[8,16,1024]{2,1,0:T(8,128)(2,1)S(1)}, u32[]{:S(2)}, u32[]{:S(2)}) collective-permute-start(bf16[8,16,1024]{2,1,0:T(8,128)(2,1)} %get-tuple-element.40), channel_id=1, source_target_pairs={{0,1},{1,2},{2,3},{3,4},{4,5},{5,6},{6,7},{8,9},{9,10},{10,11},{11... | collective-permute-start | bytes 786440 | tf_op jit(solution)/shard_map/ppermute | solution.py:453
  15.6 1.5 collective-permute-start.1
  17.4 1.3 shard_map.83.refs_4_
  18.7 1.3 copy-done
  20.0 7.0 %collective-permute-done.left = bf16[8,16,1024]{2,1,0:T(8,128)(2,1)S(1)} collective-permute-done((bf16[8,16,1024]{2,1,0:T(8,128)(2,1)}, bf16[8,16,1024]{2,1,0:T(8,128)(2,1)S(1)}, u32[]{:S(2)}, u32[]{:S(2)}) %collective-permute-start) | collective-permute-done | bytes 262176 | tf_op jit(solution)/shard_map/ppermute | solution.py:453
  27.0 1.2 copy-done.1
  28.3 1.2 shard_map.84
  29.5 4.5 %collective-permute-start.2 = (bf16[1,1,8,32,256]{4,3,2,1,0:T(8,128)(2,1)S(1)}, bf16[1,1,8,32,256]{4,3,2,1,0:T(8,128)(2,1)S(1)}, u32[]{:S(2)}, u32[]{:S(2)}) collective-permute-start(bf16[1,1,8,32,256]{4,3,2,1,0:T(8,128)(2,1)S(1)} %get-tuple-element.43), channel_id=1, source_target_pairs={{0,4},{1,5},{2,6},{3,7},{4,0},{5,1},{6,2},{7,3},{8,12},{9,13},{10,... | collective-permute-start | bytes 393224 | tf_op jit(solution)/shard_map/ppermute | solution.py:440
  34.1 6.3 %collective-permute-done.2 = bf16[1,1,8,32,256]{4,3,2,1,0:T(8,128)(2,1)S(1)} collective-permute-done((bf16[1,1,8,32,256]{4,3,2,1,0:T(8,128)(2,1)S(1)}, bf16[1,1,8,32,256]{4,3,2,1,0:T(8,128)(2,1)S(1)}, u32[]{:S(2)}, u32[]{:S(2)}) %collective-permute-start.2) | collective-permute-done | bytes 131104 | tf_op jit(solution)/shard_map/ppermute | solution.py:440
  40.6 4.1 %collective-permute-start.3 = (bf16[1,2,8,32,256]{4,3,2,1,0:T(8,128)(2,1)S(1)}, bf16[1,2,8,32,256]{4,3,2,1,0:T(8,128)(2,1)S(1)}, u32[]{:S(2)}, u32[]{:S(2)}) collective-permute-start(bf16[1,2,8,32,256]{4,3,2,1,0:T(8,128)(2,1)S(1)} %constant_dynamic-update-slice_fusion), channel_id=1, source_target_pairs={{0,2},{1,3},{2,0},{3,1},{4,6},{5,7},{6,4},{7,5},{8,10},{9,11},{10,... | collective-permute-start | bytes 786440 | tf_op jit(solution)/shard_map/ppermute | solution.py:440
  44.9 1.5 collective-permute-start.9
  46.4 8.5 %collective-permute-done.5 = bf16[2,1,8,32,256]{4,3,2,1,0:T(8,128)(2,1)S(1)} collective-permute-done((bf16[2,1,8,32,256]{4,3,2,1,0:T(8,128)(2,1)S(1)}, bf16[2,1,8,32,256]{4,3,2,1,0:T(8,128)(2,1)S(1)}, u32[]{:S(2)}, u32[]{:S(2)}) %collective-permute-start.5) | collective-permute-done | bytes 262176 | tf_op jit(solution)/shard_map/ppermute | solution.py:440
  55.3 3.0 %collective-permute-start.4 = (bf16[4,8,32,256]{3,2,1,0:T(8,128)(2,1)S(1)}, bf16[4,8,32,256]{3,2,1,0:T(8,128)(2,1)S(1)}, u32[]{:S(2)}, u32[]{:S(2)}) collective-permute-start(bf16[4,8,32,256]{3,2,1,0:T(8,128)(2,1)S(1)} %pad_maximum_fusion.1.held), channel_id=1, source_target_pairs={{0,1},{1,0},{2,3},{3,2},{4,5},{5,4},{6,7},{7,6},{8,9},{9,8},{10,11... | collective-permute-start | bytes 1572872 | tf_op jit(solution)/shard_map/ppermute | solution.py:440
  58.4 8.9 %collective-permute-done.6 = bf16[2,2,8,32,256]{4,3,2,1,0:T(8,128)(2,1)S(1)} collective-permute-done((bf16[2,2,8,32,256]{4,3,2,1,0:T(8,128)(2,1)S(1)}, bf16[2,2,8,32,256]{4,3,2,1,0:T(8,128)(2,1)S(1)}, u32[]{:S(2)}, u32[]{:S(2)}) %collective-permute-start.6) | collective-permute-done | bytes 524320 | tf_op jit(solution)/shard_map/ppermute | solution.py:440
  67.5 1.4 collective-permute-done.4.across
  69.5 1.7 %collective-permute-start.11 = (bf16[4,8,32,256]{3,2,1,0:T(8,128)(2,1)S(1)}, bf16[4,8,32,256]{3,2,1,0:T(8,128)(2,1)S(1)}, u32[]{:S(2)}, u32[]{:S(2)}) collective-permute-start(bf16[4,8,32,256]{3,2,1,0:T(8,128)(2,1)S(1)} %pad_maximum_fusion.2.held), channel_id=1, source_target_pairs={{0,1},{1,0},{2,3},{3,2},{4,5},{5,4},{6,7},{7,6},{8,9},{9,8},{10,11... | collective-permute-start | bytes 1572872 | tf_op jit(solution)/shard_map/ppermute | solution.py:440
  71.2 9.9 %collective-permute-done.7.far = bf16[2,8,64,256]{3,2,1,0:T(8,128)(2,1)S(1)} collective-permute-done((bf16[2,8,64,256]{3,2,1,0:T(8,128)(2,1)S(1)}, bf16[2,8,64,256]{3,2,1,0:T(8,128)(2,1)S(1)}, u32[]{:S(2)}, u32[]{:S(2)}) %collective-permute-start.7) | collective-permute-done | bytes 524320 | tf_op jit(solution)/shard_map/ppermute | solution.py:440
  81.3 1.4 shard_map.86.by_channel
  83.6 1.5 %collective-permute-start.14 = (bf16[4,8,32,256]{3,2,1,0:T(8,128)(2,1)S(1)}, bf16[4,8,32,256]{3,2,1,0:T(8,128)(2,1)S(1)}, u32[]{:S(2)}, u32[]{:S(2)}) collective-permute-start(bf16[4,8,32,256]{3,2,1,0:T(8,128)(2,1)S(1)} %pad_maximum_fusion.5.held), channel_id=1, source_target_pairs={{0,1},{1,0},{2,3},{3,2},{4,5},{5,4},{6,7},{7,6},{8,9},{9,8},{10,11... | collective-permute-start | bytes 1572872 | tf_op jit(solution)/shard_map/ppermute | solution.py:440
  85.1 6.7 %collective-permute-start.17 = (bf16[1,1,8,32,256]{4,3,2,1,0:T(8,128)(2,1)S(1)}, bf16[1,1,8,32,256]{4,3,2,1,0:T(8,128)(2,1)S(1)}, u32[]{:S(2)}, u32[]{:S(2)}) collective-permute-start(bf16[1,1,8,32,256]{4,3,2,1,0:T(8,128)(2,1)S(1)} %get-tuple-element.65), channel_id=1, source_target_pairs={{0,4},{1,5},{2,6},{3,7},{4,0},{5,1},{6,2},{7,3},{8,12},{9,13},{10,... | collective-permute-start | bytes 393224 | tf_op jit(solution)/shard_map/ppermute | solution.py:440
  91.7 6.4 %collective-permute-done.17 = bf16[1,1,8,32,256]{4,3,2,1,0:T(8,128)(2,1)S(1)} collective-permute-done((bf16[1,1,8,32,256]{4,3,2,1,0:T(8,128)(2,1)S(1)}, bf16[1,1,8,32,256]{4,3,2,1,0:T(8,128)(2,1)S(1)}, u32[]{:S(2)}, u32[]{:S(2)}) %collective-permute-start.17) | collective-permute-done | bytes 131104 | tf_op jit(solution)/shard_map/ppermute | solution.py:440
  98.3 5.3 %shard_map.87.refs_0_ = bf16[4,2,512,128]{3,2,1,0:T(8,128)(2,1)S(1)} custom-call(bf16[8,64,256]{2,1,0:T(8,128)(2,1)S(1)} %get-tuple-element.48.here, bf16[2,8,64,256]{3,2,1,0:T(8,128)(2,1)S(1)} %collective-permute-done.8.near, bf16[2,8,64,256]{3,2,1,0:T(8,128)(2,1)S(1)} %collective-permute-done.7.far, bf16[8,512,256]{2,1,0:T(8,128)(2,1)S(1)} %shard_map.86.by_channel), custom_call_target="tpu_custom_call" | custom-call | flops 603979776 | bytes 4194304 | tf_op jit(solution)/shard_map/pallas_call | solution.py:311
  104.2 1.8 %collective-permute-start.15 = (bf16[2,8,64,256]{3,2,1,0:T(8,128)(2,1)S(1)}, bf16[2,8,64,256]{3,2,1,0:T(8,128)(2,1)S(1)}, u32[]{:S(2)}, u32[]{:S(2)}) collective-permute-start(bf16[2,8,64,256]{3,2,1,0:T(8,128)(2,1)S(1)} %get-tuple-element.62), channel_id=1, source_target_pairs={{0,16},{8,24},{16,0},{24,8},{1,17},{9,25},{17,1},{25,9},{2,18},{10... | collective-permute-start | bytes 1572872 | tf_op jit(solution)/shard_map/ppermute | solution.py:440
  107.0 5.5 %shard_map.89.refs_1_ = bf16[4,2,512,128]{3,2,1,0:T(8,128)(2,1)S(1)} custom-call(bf16[8,64,256]{2,1,0:T(8,128)(2,1)S(1)} %get-tuple-element.54.here, bf16[2,8,64,256]{3,2,1,0:T(8,128)(2,1)S(1)} %collective-permute-done.13.near, bf16[2,8,64,256]{3,2,1,0:T(8,128)(2,1)S(1)} %collective-permute-done.12.far, bf16[8,512,256]{2,1,0:T(8,128)(2,1)S(1)} %shard_map.86.by_channel), custom_call_target="tpu_custom_call" | custom-call | flops 603979776 | bytes 4194304 | tf_op jit(solution)/shard_map/pallas_call | solution.py:311
  112.6 6.1 %collective-permute-done.15.far = bf16[2,8,64,256]{3,2,1,0:T(8,128)(2,1)S(1)} collective-permute-done((bf16[2,8,64,256]{3,2,1,0:T(8,128)(2,1)S(1)}, bf16[2,8,64,256]{3,2,1,0:T(8,128)(2,1)S(1)}, u32[]{:S(2)}, u32[]{:S(2)}) %collective-permute-start.15) | collective-permute-done | bytes 524320 | tf_op jit(solution)/shard_map/ppermute | solution.py:440
  118.8 1.4 collective-permute-done.19.across
  121.5 5.3 %shard_map.91.refs_2_ = bf16[4,2,512,128]{3,2,1,0:T(8,128)(2,1)S(1)} custom-call(bf16[8,64,256]{2,1,0:T(8,128)(2,1)S(1)} %get-tuple-element.60.here, bf16[2,8,64,256]{3,2,1,0:T(8,128)(2,1)S(1)} %collective-permute-done.16.near, bf16[2,8,64,256]{3,2,1,0:T(8,128)(2,1)S(1)} %collective-permute-done.15.far, bf16[8,512,256]{2,1,0:T(8,128)(2,1)S(1)} %shard_map.86.by_channel), custom_call_target="tpu_custom_call" | custom-call | flops 603979776 | bytes 4194304 | tf_op jit(solution)/shard_map/pallas_call | solution.py:311
  126.8 6.8 %collective-permute-done.20.far = bf16[2,8,64,256]{3,2,1,0:T(8,128)(2,1)S(1)} collective-permute-done((bf16[2,8,64,256]{3,2,1,0:T(8,128)(2,1)S(1)}, bf16[2,8,64,256]{3,2,1,0:T(8,128)(2,1)S(1)}, u32[]{:S(2)}, u32[]{:S(2)}) %collective-permute-start.20) | collective-permute-done | bytes 524320 | tf_op jit(solution)/shard_map/ppermute | solution.py:440
  133.8 1.9 %collective-permute-done.21.near = bf16[2,8,64,256]{3,2,1,0:T(8,128)(2,1)S(1)} collective-permute-done((bf16[2,8,64,256]{3,2,1,0:T(8,128)(2,1)S(1)}, bf16[2,8,64,256]{3,2,1,0:T(8,128)(2,1)S(1)}, u32[]{:S(2)}, u32[]{:S(2)}) %collective-permute-start.21) | collective-permute-done | bytes 524320 | tf_op jit(solution)/shard_map/ppermute | solution.py:440
  135.7 5.3 %shard_map.93.refs_3_ = bf16[4,2,512,128]{3,2,1,0:T(8,128)(2,1)S(1)} custom-call(bf16[8,64,256]{2,1,0:T(8,128)(2,1)S(1)} %get-tuple-element.69.here, bf16[2,8,64,256]{3,2,1,0:T(8,128)(2,1)S(1)} %collective-permute-done.21.near, bf16[2,8,64,256]{3,2,1,0:T(8,128)(2,1)S(1)} %collective-permute-done.20.far, bf16[8,512,256]{2,1,0:T(8,128)(2,1)S(1)} %shard_map.86.by_channel), custom_call_target="tpu_custom_call" | custom-call | flops 603979776 | bytes 4194304 | tf_op jit(solution)/shard_map/pallas_call | solution.py:311
  141.0 9.9 %shard_map.94 = f32[64,32,2048]{2,1,0:T(8,128)} custom-call(bf16[4,2,512,128]{3,2,1,0:T(8,128)(2,1)S(1)} %shard_map.87.refs_0_, bf16[4,2,512,128]{3,2,1,0:T(8,128)(2,1)S(1)} %shard_map.89.refs_1_, bf16[4,2,512,128]{3,2,1,0:T(8,128)(2,1)S(1)} %shard_map.91.refs_2_, bf16[4,2,512,128]{3,2,1,0:T(8,128)(2,1)S(1)} %shard_map.93.refs_3_, ...), custom_call_target="tpu_custom_call" | custom-call | flops 4294967296 | bytes 16777216 | tf_op jit(solution)/shard_map/pallas_call | solution.py:361
  (73 shorter events, 6.3 us)
Async XLA Ops:
  0.0 17.1 %copy-start.5 = (bf16[32]{0:T(256)(128)(2,1)S(1)}, bf16[32]{0:T(256)(128)(2,1)}, u32[]{:S(2)}) copy-start(bf16[32]{0:T(256)(128)(2,1)} %param.9) | copy-start | bytes 196
  0.0 17.4 %copy-start.2 = (f32[512,272]{1,0:T(8,128)S(1)}, f32[512,272]{1,0:T(8,128)}, u32[]{:S(2)}) copy-start(f32[512,272]{1,0:T(8,128)} %constant.33.clone.angles) | copy-start | bytes 1671172
  0.0 20.0 %copy-start.7 = (s32[8]{0:T(128)S(1)}, s32[8]{0:T(128)}, u32[]{:S(2)}) copy-start(s32[8]{0:T(128)} %constant.34.clone) | copy-start | bytes 100
  0.0 27.0 %copy-start.4 = (s32[32]{0:T(128)S(1)}, s32[32]{0:T(128)}, u32[]{:S(2)}) copy-start(s32[32]{0:T(128)} %param.10) | copy-start | bytes 388
  10.6 23.5 %copy-start.6 = (s32[256]{0:T(256)S(1)}, s32[256]{0:T(256)}, u32[]{:S(2)}) copy-start(s32[256]{0:T(256)} %param.11) | copy-start | bytes 3076
  10.6 16.5 %collective-permute-start = (bf16[8,16,1024]{2,1,0:T(8,128)(2,1)}, bf16[8,16,1024]{2,1,0:T(8,128)(2,1)S(1)}, u32[]{:S(2)}, u32[]{:S(2)}) collective-permute-start(bf16[8,16,1024]{2,1,0:T(8,128)(2,1)} %get-tuple-element.40), channel_id=1, source_target_pairs={{0,1},{1,2},{2,3},{3,4},{4,5},{5,6},{6,7},{8,9},{9,10},{10,11},{11... | collective-permute-start | bytes 786440 | tf_op jit(solution)/shard_map/ppermute | solution.py:453
  15.6 11.5 %collective-permute-start.1 = (bf16[8,16,1024]{2,1,0:T(8,128)(2,1)}, bf16[8,16,1024]{2,1,0:T(8,128)(2,1)S(1)}, u32[]{:S(2)}, u32[]{:S(2)}) collective-permute-start(bf16[8,16,1024]{2,1,0:T(8,128)(2,1)} %get-tuple-element.42), channel_id=1, source_target_pairs={{1,0},{2,1},{3,2},{4,3},{5,4},{6,5},{7,6},{9,8},{10,9},{11,10},{12... | collective-permute-start | bytes 786440 | tf_op jit(solution)/shard_map/ppermute | solution.py:454
  18.7 1.4 copy-start
  27.0 1.2 copy-start.1
  29.5 10.9 %collective-permute-start.2 = (bf16[1,1,8,32,256]{4,3,2,1,0:T(8,128)(2,1)S(1)}, bf16[1,1,8,32,256]{4,3,2,1,0:T(8,128)(2,1)S(1)}, u32[]{:S(2)}, u32[]{:S(2)}) collective-permute-start(bf16[1,1,8,32,256]{4,3,2,1,0:T(8,128)(2,1)S(1)} %get-tuple-element.43), channel_id=1, source_target_pairs={{0,4},{1,5},{2,6},{3,7},{4,0},{5,1},{6,2},{7,3},{8,12},{9,13},{10,... | collective-permute-start | bytes 393224 | tf_op jit(solution)/shard_map/ppermute | solution.py:440
  40.5 14.4 %collective-permute-start.5 = (bf16[2,1,8,32,256]{4,3,2,1,0:T(8,128)(2,1)S(1)}, bf16[2,1,8,32,256]{4,3,2,1,0:T(8,128)(2,1)S(1)}, u32[]{:S(2)}, u32[]{:S(2)}) collective-permute-start(bf16[2,1,8,32,256]{4,3,2,1,0:T(8,128)(2,1)S(1)} %get-tuple-element.45), channel_id=1, source_target_pairs={{0,4},{1,5},{2,6},{3,7},{4,0},{5,1},{6,2},{7,3},{8,12},{9,13},{10,... | collective-permute-start | bytes 786440 | tf_op jit(solution)/shard_map/ppermute | solution.py:440
  40.6 14.4 %collective-permute-start.3 = (bf16[1,2,8,32,256]{4,3,2,1,0:T(8,128)(2,1)S(1)}, bf16[1,2,8,32,256]{4,3,2,1,0:T(8,128)(2,1)S(1)}, u32[]{:S(2)}, u32[]{:S(2)}) collective-permute-start(bf16[1,2,8,32,256]{4,3,2,1,0:T(8,128)(2,1)S(1)} %constant_dynamic-update-slice_fusion), channel_id=1, source_target_pairs={{0,2},{1,3},{2,0},{3,1},{4,6},{5,7},{6,4},{7,5},{8,10},{9,11},{10,... | collective-permute-start | bytes 786440 | tf_op jit(solution)/shard_map/ppermute | solution.py:440
  44.9 13.3 %collective-permute-start.9 = (bf16[8,32,1024]{2,1,0:T(8,128)(2,1)S(1)}, bf16[8,32,1024]{2,1,0:T(8,128)(2,1)S(1)}, u32[]{:S(2)}, u32[]{:S(2)}) collective-permute-start(bf16[8,32,1024]{2,1,0:T(8,128)(2,1)S(1)} %get-tuple-element.51.here), channel_id=1, source_target_pairs={{0,16},{8,24},{16,0},{24,8},{1,17},{9,25},{17,1},{25,9},{2,18},{10... | collective-permute-start | bytes 1572872 | tf_op jit(solution)/shard_map/ppermute | solution.py:440
  55.1 12.3 %collective-permute-start.6 = (bf16[2,2,8,32,256]{4,3,2,1,0:T(8,128)(2,1)S(1)}, bf16[2,2,8,32,256]{4,3,2,1,0:T(8,128)(2,1)S(1)}, u32[]{:S(2)}, u32[]{:S(2)}) collective-permute-start(bf16[2,2,8,32,256]{4,3,2,1,0:T(8,128)(2,1)S(1)} %constant_dynamic-update-slice_fusion.2), channel_id=1, source_target_pairs={{0,2},{1,3},{2,0},{3,1},{4,6},{5,7},{6,4},{7,5},{8,10},{9,11},{10,... | collective-permute-start | bytes 1572872 | tf_op jit(solution)/shard_map/ppermute | solution.py:440
  55.3 13.6 %collective-permute-start.4 = (bf16[4,8,32,256]{3,2,1,0:T(8,128)(2,1)S(1)}, bf16[4,8,32,256]{3,2,1,0:T(8,128)(2,1)S(1)}, u32[]{:S(2)}, u32[]{:S(2)}) collective-permute-start(bf16[4,8,32,256]{3,2,1,0:T(8,128)(2,1)S(1)} %pad_maximum_fusion.1.held), channel_id=1, source_target_pairs={{0,1},{1,0},{2,3},{3,2},{4,5},{5,4},{6,7},{7,6},{8,9},{9,8},{10,11... | collective-permute-start | bytes 1572872 | tf_op jit(solution)/shard_map/ppermute | solution.py:440
  58.3 23.0 %collective-permute-start.10 = (bf16[2,8,32,1024]{3,2,1,0:T(8,128)(2,1)S(1)}, bf16[2,8,32,1024]{3,2,1,0:T(8,128)(2,1)S(1)}, u32[]{:S(2)}, u32[]{:S(2)}) collective-permute-start(bf16[2,8,32,1024]{3,2,1,0:T(8,128)(2,1)S(1)} %pad_maximum_fusion), channel_id=1, source_target_pairs={{0,8},{8,0},{16,24},{24,16},{1,9},{9,1},{17,25},{25,17},{2,10},{10... | collective-permute-start | bytes 3145736 | tf_op jit(solution)/shard_map/ppermute | solution.py:440
  69.3 11.8 %collective-permute-start.7 = (bf16[2,8,64,256]{3,2,1,0:T(8,128)(2,1)S(1)}, bf16[2,8,64,256]{3,2,1,0:T(8,128)(2,1)S(1)}, u32[]{:S(2)}, u32[]{:S(2)}) collective-permute-start(bf16[2,8,64,256]{3,2,1,0:T(8,128)(2,1)S(1)} %get-tuple-element.50), channel_id=1, source_target_pairs={{0,16},{8,24},{16,0},{24,8},{1,17},{9,25},{17,1},{25,9},{2,18},{10... | collective-permute-start | bytes 1572872 | tf_op jit(solution)/shard_map/ppermute | solution.py:440
  69.5 13.2 %collective-permute-start.11 = (bf16[4,8,32,256]{3,2,1,0:T(8,128)(2,1)S(1)}, bf16[4,8,32,256]{3,2,1,0:T(8,128)(2,1)S(1)}, u32[]{:S(2)}, u32[]{:S(2)}) collective-permute-start(bf16[4,8,32,256]{3,2,1,0:T(8,128)(2,1)S(1)} %pad_maximum_fusion.2.held), channel_id=1, source_target_pairs={{0,1},{1,0},{2,3},{3,2},{4,5},{5,4},{6,7},{7,6},{8,9},{9,8},{10,11... | collective-permute-start | bytes 1572872 | tf_op jit(solution)/shard_map/ppermute | solution.py:440
  81.2 17.0 %collective-permute-start.8 = (bf16[2,8,64,256]{3,2,1,0:T(8,128)(2,1)S(1)}, bf16[2,8,64,256]{3,2,1,0:T(8,128)(2,1)S(1)}, u32[]{:S(2)}, u32[]{:S(2)}) collective-permute-start(bf16[2,8,64,256]{3,2,1,0:T(8,128)(2,1)S(1)} %pad_maximum_fusion.3), channel_id=1, source_target_pairs={{0,8},{8,0},{16,24},{24,16},{1,9},{9,1},{17,25},{25,17},{2,10},{10... | collective-permute-start | bytes 1572872 | tf_op jit(solution)/shard_map/ppermute | solution.py:440
  83.2 20.4 %collective-permute-start.12 = (bf16[2,8,64,256]{3,2,1,0:T(8,128)(2,1)S(1)}, bf16[2,8,64,256]{3,2,1,0:T(8,128)(2,1)S(1)}, u32[]{:S(2)}, u32[]{:S(2)}) collective-permute-start(bf16[2,8,64,256]{3,2,1,0:T(8,128)(2,1)S(1)} %get-tuple-element.56), channel_id=1, source_target_pairs={{0,16},{8,24},{16,0},{24,8},{1,17},{9,25},{17,1},{25,9},{2,18},{10... | collective-permute-start | bytes 1572872 | tf_op jit(solution)/shard_map/ppermute | solution.py:440
  83.6 20.2 %collective-permute-start.14 = (bf16[4,8,32,256]{3,2,1,0:T(8,128)(2,1)S(1)}, bf16[4,8,32,256]{3,2,1,0:T(8,128)(2,1)S(1)}, u32[]{:S(2)}, u32[]{:S(2)}) collective-permute-start(bf16[4,8,32,256]{3,2,1,0:T(8,128)(2,1)S(1)} %pad_maximum_fusion.5.held), channel_id=1, source_target_pairs={{0,1},{1,0},{2,3},{3,2},{4,5},{5,4},{6,7},{7,6},{8,9},{9,8},{10,11... | collective-permute-start | bytes 1572872 | tf_op jit(solution)/shard_map/ppermute | solution.py:440
  85.1 13.1 %collective-permute-start.17 = (bf16[1,1,8,32,256]{4,3,2,1,0:T(8,128)(2,1)S(1)}, bf16[1,1,8,32,256]{4,3,2,1,0:T(8,128)(2,1)S(1)}, u32[]{:S(2)}, u32[]{:S(2)}) collective-permute-start(bf16[1,1,8,32,256]{4,3,2,1,0:T(8,128)(2,1)S(1)} %get-tuple-element.65), channel_id=1, source_target_pairs={{0,4},{1,5},{2,6},{3,7},{4,0},{5,1},{6,2},{7,3},{8,12},{9,13},{10,... | collective-permute-start | bytes 393224 | tf_op jit(solution)/shard_map/ppermute | solution.py:440
  98.2 8.1 %collective-permute-start.18 = (bf16[1,2,8,32,256]{4,3,2,1,0:T(8,128)(2,1)S(1)}, bf16[1,2,8,32,256]{4,3,2,1,0:T(8,128)(2,1)S(1)}, u32[]{:S(2)}, u32[]{:S(2)}) collective-permute-start(bf16[1,2,8,32,256]{4,3,2,1,0:T(8,128)(2,1)S(1)} %pad_maximum_fusion.9), channel_id=1, source_target_pairs={{0,2},{1,3},{2,0},{3,1},{4,6},{5,7},{6,4},{7,5},{8,10},{9,11},{10,... | collective-permute-start | bytes 786440 | tf_op jit(solution)/shard_map/ppermute | solution.py:440
  103.7 3.3 %collective-permute-start.13 = (bf16[2,8,64,256]{3,2,1,0:T(8,128)(2,1)S(1)}, bf16[2,8,64,256]{3,2,1,0:T(8,128)(2,1)S(1)}, u32[]{:S(2)}, u32[]{:S(2)}) collective-permute-start(bf16[2,8,64,256]{3,2,1,0:T(8,128)(2,1)S(1)} %pad_maximum_fusion.4), channel_id=1, source_target_pairs={{0,8},{8,0},{16,24},{24,16},{1,9},{9,1},{17,25},{25,17},{2,10},{10... | collective-permute-start | bytes 1572872 | tf_op jit(solution)/shard_map/ppermute | solution.py:440
  104.2 14.4 %collective-permute-start.15 = (bf16[2,8,64,256]{3,2,1,0:T(8,128)(2,1)S(1)}, bf16[2,8,64,256]{3,2,1,0:T(8,128)(2,1)S(1)}, u32[]{:S(2)}, u32[]{:S(2)}) collective-permute-start(bf16[2,8,64,256]{3,2,1,0:T(8,128)(2,1)S(1)} %get-tuple-element.62), channel_id=1, source_target_pairs={{0,16},{8,24},{16,0},{24,8},{1,17},{9,25},{17,1},{25,9},{2,18},{10... | collective-permute-start | bytes 1572872 | tf_op jit(solution)/shard_map/ppermute | solution.py:440
  106.4 13.8 %collective-permute-start.19 = (bf16[4,8,32,256]{3,2,1,0:T(8,128)(2,1)S(1)}, bf16[4,8,32,256]{3,2,1,0:T(8,128)(2,1)S(1)}, u32[]{:S(2)}, u32[]{:S(2)}) collective-permute-start(bf16[4,8,32,256]{3,2,1,0:T(8,128)(2,1)S(1)} %pad_maximum_fusion.7.held), channel_id=1, source_target_pairs={{0,1},{1,0},{2,3},{3,2},{4,5},{5,4},{6,7},{7,6},{8,9},{9,8},{10,11... | collective-permute-start | bytes 1572872 | tf_op jit(solution)/shard_map/ppermute | solution.py:440
  118.7 2.8 %collective-permute-start.16 = (bf16[2,8,64,256]{3,2,1,0:T(8,128)(2,1)S(1)}, bf16[2,8,64,256]{3,2,1,0:T(8,128)(2,1)S(1)}, u32[]{:S(2)}, u32[]{:S(2)}) collective-permute-start(bf16[2,8,64,256]{3,2,1,0:T(8,128)(2,1)S(1)} %pad_maximum_fusion.6), channel_id=1, source_target_pairs={{0,8},{8,0},{16,24},{24,16},{1,9},{9,1},{17,25},{25,17},{2,10},{10... | collective-permute-start | bytes 1572872 | tf_op jit(solution)/shard_map/ppermute | solution.py:440
  120.6 13.0 %collective-permute-start.20 = (bf16[2,8,64,256]{3,2,1,0:T(8,128)(2,1)S(1)}, bf16[2,8,64,256]{3,2,1,0:T(8,128)(2,1)S(1)}, u32[]{:S(2)}, u32[]{:S(2)}) collective-permute-start(bf16[2,8,64,256]{3,2,1,0:T(8,128)(2,1)S(1)} %get-tuple-element.71), channel_id=1, source_target_pairs={{0,16},{8,24},{16,0},{24,8},{1,17},{9,25},{17,1},{25,9},{2,18},{10... | collective-permute-start | bytes 1572872 | tf_op jit(solution)/shard_map/ppermute | solution.py:440
  126.8 14.2 %copy-start.3 = (f32[2,512]{1,0:T(2,128)S(1)}, f32[2,512]{1,0:T(2,128)}, u32[]{:S(2)}) copy-start(f32[2,512]{1,0:T(2,128)} %constant.35.clone.refs_5_) | copy-start | bytes 12292
  133.7 2.0 %collective-permute-start.21 = (bf16[2,8,64,256]{3,2,1,0:T(8,128)(2,1)S(1)}, bf16[2,8,64,256]{3,2,1,0:T(8,128)(2,1)S(1)}, u32[]{:S(2)}, u32[]{:S(2)}) collective-permute-start(bf16[2,8,64,256]{3,2,1,0:T(8,128)(2,1)S(1)} %pad_maximum_fusion.8), channel_id=1, source_target_pairs={{0,8},{8,0},{16,24},{24,16},{1,9},{9,1},{17,25},{25,17},{2,10},{10... | collective-permute-start | bytes 1572872 | tf_op jit(solution)/shard_map/ppermute | solution.py:440

commit v3 on v0

--- a/solution.py
+++ b/solution.py
@@ -493,8 +493,7 @@
         across = swapped(held, "chan", 1)
         if at > 1:
             finish(at - 2)
-        if at:
-            across = after(across, stacked[-1] if stacked else by_channel)
+        across = after(across, (stacked[-1] if stacked else by_channel) if at else gathered[1])
         here, near, far = pick(held, across, selector, groups)
         picked.append((here, near, swapped(far, "win", 2)))
 
@@ -507,7 +506,7 @@
 
     first_held = []
     for part in parts:
-        gather(after(part, [first_held[-1]] + [own_far] * (len(first_held) > 1)) if first_held else part)
+        gather(after(part, [first_held[-1], own_far]) if len(first_held) > 1 else part)
         if len(gathered) == 2:
             exchange(0)
     for at in range(1, chunks):

time: 143 us -> 142 us (level)
  starting transfers between devices: 31.3 us -> 24.5 us
  waiting for transfers between devices: 56.6 us -> 62.2 us
    ppermute x20, starting transfers between devices: 24.8 us -> 18 us  [swapped(): lax.ppermute(value, axis, [(i, i ^ step) for i in range(lax.axis_size(axi...]
    ppermute x20, waiting for transfers between devices: 49.5 us -> 55.2 us  [swapped(): lax.ppermute(value, axis, [(i, i ^ step) for i in range(lax.axis_size(axi...]
  transfers between devices with their start and end apart: 22 -> 22, of which waited for: 13 -> 14; matrix products, arithmetic and copies ran while one was open for 3% -> 3% of each run, Pallas kernels for 14% -> 14%
where the time goes in v3:
time: 142 us
  waiting for transfers between devices  62.2 us (44%)
  Pallas kernels  47.6 us (34%)
  starting transfers between devices  24.5 us (17%)
  local copies, waits for them, and re-layouts  4.35 us (3%)
  other arithmetic  3.02 us (2%)
    ppermute x20, waiting for transfers between devices, swapped(): lax.ppermute(value, axis, [(i, i ^ step) for i in range(lax.axis_size(axi...  55.2 us
    pallas_call x4, Pallas kernels, cross(): pl.pallas_call(cross_kernel, grid=(1,), in_specs=[pl.BlockSpec(a.shape, f...  21.5 us
    ppermute x20, starting transfers between devices, swapped(): lax.ppermute(value, axis, [(i, i ^ step) for i in range(lax.axis_size(axi...  18 us
    pallas_call x1, Pallas kernels, transform(): pl.pallas_call(transform_kernel, grid=(steps,), in_specs=[pl.BlockSpec((r...  10.6 us
    pallas_call x1, Pallas kernels, lagged(): pl.pallas_call(functools.partial(lag_kernel, scaling), grid=(groups,), in...  9.94 us
    ppermute x1, waiting for transfers between devices, per_device(): left = lax.ppermute(tail, 'chan', [(i, i + 1) for i in range(blocks - 1)])  7 us
    ppermute x1, starting transfers between devices, per_device(): left = lax.ppermute(tail, 'chan', [(i, i + 1) for i in range(blocks - 1)])  4.98 us
    unnamed x18, local copies, waits for them, and re-layouts  3.29 us
  transfers between devices with their start and end apart: 22, of which 14 were waited for; matrix products, arithmetic and copies ran while one was open for 3% of the time, Pallas kernels for 14%

profile of v3, /device:TPU:0, one launch (start us, length us, event | category | flops | bytes accessed | tf_op | source)
XLA Modules:
  0.0 142.1 jit_solution(5631115749985260434)
XLA Ops:
  0.0 10.6 %shard_map.82 = (f32[8,32,1024]{2,1,0:T(8,128)}, bf16[8,16,1024]{2,1,0:T(8,128)(2,1)}, bf16[8,16,1024]{2,1,0:T(8,128)(2,1)}) custom-call(bf16[256,7680]{1,0:T(8,128)(2,1)} %bitcast.28, bf16[256,7680]{1,0:T(8,128)(2,1)} %bitcast.29, bf16[256,7680]{1,0:T(8,128)(2,1)} %bitcast.30, bf16[256,7680]{1,0:T(8,128)(2,1)} %bitcast.31, ...), custom_call_target="tpu_custom_call" | custom-call | flops 4026531840 | bytes 3932160 | tf_op jit(solution)/shard_map/pallas_call | solution.py:97
  10.6 5.0 %collective-permute-start = (bf16[8,16,1024]{2,1,0:T(8,128)(2,1)}, bf16[8,16,1024]{2,1,0:T(8,128)(2,1)S(1)}, u32[]{:S(2)}, u32[]{:S(2)}) collective-permute-start(bf16[8,16,1024]{2,1,0:T(8,128)(2,1)} %get-tuple-element.38), channel_id=1, source_target_pairs={{0,1},{1,2},{2,3},{3,4},{4,5},{5,6},{6,7},{8,9},{9,10},{10,11},{11... | collective-permute-start | bytes 786440 | tf_op jit(solution)/shard_map/ppermute | solution.py:453
  15.6 1.5 %collective-permute-start.1 = (bf16[8,16,1024]{2,1,0:T(8,128)(2,1)}, bf16[8,16,1024]{2,1,0:T(8,128)(2,1)S(1)}, u32[]{:S(2)}, u32[]{:S(2)}) collective-permute-start(bf16[8,16,1024]{2,1,0:T(8,128)(2,1)} %get-tuple-element.40), channel_id=1, source_target_pairs={{1,0},{2,1},{3,2},{4,3},{5,4},{6,5},{7,6},{9,8},{10,9},{11,10},{12... | collective-permute-start | bytes 786440 | tf_op jit(solution)/shard_map/ppermute | solution.py:454
  17.4 1.3 shard_map.83.refs_4_
  18.7 1.4 copy-done
  20.0 7.0 %collective-permute-done.left = bf16[8,16,1024]{2,1,0:T(8,128)(2,1)S(1)} collective-permute-done((bf16[8,16,1024]{2,1,0:T(8,128)(2,1)}, bf16[8,16,1024]{2,1,0:T(8,128)(2,1)S(1)}, u32[]{:S(2)}, u32[]{:S(2)}) %collective-permute-start) | collective-permute-done | bytes 262176 | tf_op jit(solution)/shard_map/ppermute | solution.py:453
  28.3 1.3 shard_map.84
  29.5 4.4 %collective-permute-start.2 = (bf16[1,1,8,32,256]{4,3,2,1,0:T(8,128)(2,1)S(1)}, bf16[1,1,8,32,256]{4,3,2,1,0:T(8,128)(2,1)S(1)}, u32[]{:S(2)}, u32[]{:S(2)}) collective-permute-start(bf16[1,1,8,32,256]{4,3,2,1,0:T(8,128)(2,1)S(1)} %get-tuple-element.41), channel_id=1, source_target_pairs={{0,4},{1,5},{2,6},{3,7},{4,0},{5,1},{6,2},{7,3},{8,12},{9,13},{10,... | collective-permute-start | bytes 393224 | tf_op jit(solution)/shard_map/ppermute | solution.py:440
  34.2 1.6 %collective-permute-start.9 = (bf16[8,32,1024]{2,1,0:T(8,128)(2,1)S(1)}, bf16[8,32,1024]{2,1,0:T(8,128)(2,1)S(1)}, u32[]{:S(2)}, u32[]{:S(2)}) collective-permute-start(bf16[8,32,1024]{2,1,0:T(8,128)(2,1)S(1)} %get-tuple-element.47.here), channel_id=1, source_target_pairs={{0,16},{8,24},{16,0},{24,8},{1,17},{9,25},{17,1},{25,9},{2,18},{10... | collective-permute-start | bytes 1572872 | tf_op jit(solution)/shard_map/ppermute | solution.py:440
  35.7 8.2 %collective-permute-done.2 = bf16[1,1,8,32,256]{4,3,2,1,0:T(8,128)(2,1)S(1)} collective-permute-done((bf16[1,1,8,32,256]{4,3,2,1,0:T(8,128)(2,1)S(1)}, bf16[1,1,8,32,256]{4,3,2,1,0:T(8,128)(2,1)S(1)}, u32[]{:S(2)}, u32[]{:S(2)}) %collective-permute-start.2) | collective-permute-done | bytes 131104 | tf_op jit(solution)/shard_map/ppermute | solution.py:440
  44.9 1.3 collective-permute-done.5
  47.5 5.7 %collective-permute-done.3 = bf16[1,2,8,32,256]{4,3,2,1,0:T(8,128)(2,1)S(1)} collective-permute-done((bf16[1,2,8,32,256]{4,3,2,1,0:T(8,128)(2,1)S(1)}, bf16[1,2,8,32,256]{4,3,2,1,0:T(8,128)(2,1)S(1)}, u32[]{:S(2)}, u32[]{:S(2)}) %collective-permute-start.3) | collective-permute-done | bytes 262176 | tf_op jit(solution)/shard_map/ppermute | solution.py:440
  54.9 1.3 collective-permute-start.14
  58.5 5.7 %collective-permute-done.4.across = bf16[4,8,32,256]{3,2,1,0:T(8,128)(2,1)S(1)} collective-permute-done((bf16[4,8,32,256]{3,2,1,0:T(8,128)(2,1)S(1)}, bf16[4,8,32,256]{3,2,1,0:T(8,128)(2,1)S(1)}, u32[]{:S(2)}, u32[]{:S(2)}) %collective-permute-start.4) | collective-permute-done | bytes 524320 | tf_op jit(solution)/shard_map/ppermute | solution.py:440
  64.7 1.9 %collective-permute-start.7 = (bf16[2,8,64,256]{3,2,1,0:T(8,128)(2,1)S(1)}, bf16[2,8,64,256]{3,2,1,0:T(8,128)(2,1)S(1)}, u32[]{:S(2)}, u32[]{:S(2)}) collective-permute-start(bf16[2,8,64,256]{3,2,1,0:T(8,128)(2,1)S(1)} %get-tuple-element.46), channel_id=1, source_target_pairs={{0,16},{8,24},{16,0},{24,8},{1,17},{9,25},{17,1},{25,9},{2,18},{10... | collective-permute-start | bytes 1572872 | tf_op jit(solution)/shard_map/ppermute | solution.py:440
  66.9 3.3 %collective-permute-done.14 = bf16[2,1,8,32,256]{4,3,2,1,0:T(8,128)(2,1)S(1)} collective-permute-done((bf16[2,1,8,32,256]{4,3,2,1,0:T(8,128)(2,1)S(1)}, bf16[2,1,8,32,256]{4,3,2,1,0:T(8,128)(2,1)S(1)}, u32[]{:S(2)}, u32[]{:S(2)}) %collective-permute-start.14) | collective-permute-done | bytes 262176 | tf_op jit(solution)/shard_map/ppermute | solution.py:440
  70.4 4.4 %collective-permute-done.7.far = bf16[2,8,64,256]{3,2,1,0:T(8,128)(2,1)S(1)} collective-permute-done((bf16[2,8,64,256]{3,2,1,0:T(8,128)(2,1)S(1)}, bf16[2,8,64,256]{3,2,1,0:T(8,128)(2,1)S(1)}, u32[]{:S(2)}, u32[]{:S(2)}) %collective-permute-start.7) | collective-permute-done | bytes 524320 | tf_op jit(solution)/shard_map/ppermute | solution.py:440
  75.0 1.4 shard_map.86.by_channel
  76.8 1.6 %collective-permute-start.12 = (bf16[2,8,64,256]{3,2,1,0:T(8,128)(2,1)S(1)}, bf16[2,8,64,256]{3,2,1,0:T(8,128)(2,1)S(1)}, u32[]{:S(2)}, u32[]{:S(2)}) collective-permute-start(bf16[2,8,64,256]{3,2,1,0:T(8,128)(2,1)S(1)} %get-tuple-element.52), channel_id=1, source_target_pairs={{0,16},{8,24},{16,0},{24,8},{1,17},{9,25},{17,1},{25,9},{2,18},{10... | collective-permute-start | bytes 1572872 | tf_op jit(solution)/shard_map/ppermute | solution.py:440
  78.3 5.8 %collective-permute-done.15 = bf16[2,2,8,32,256]{4,3,2,1,0:T(8,128)(2,1)S(1)} collective-permute-done((bf16[2,2,8,32,256]{4,3,2,1,0:T(8,128)(2,1)S(1)}, bf16[2,2,8,32,256]{4,3,2,1,0:T(8,128)(2,1)S(1)}, u32[]{:S(2)}, u32[]{:S(2)}) %collective-permute-start.15) | collective-permute-done | bytes 524320 | tf_op jit(solution)/shard_map/ppermute | solution.py:440
  84.3 1.7 %collective-permute-start.16 = (bf16[4,8,32,256]{3,2,1,0:T(8,128)(2,1)S(1)}, bf16[4,8,32,256]{3,2,1,0:T(8,128)(2,1)S(1)}, u32[]{:S(2)}, u32[]{:S(2)}) collective-permute-start(bf16[4,8,32,256]{3,2,1,0:T(8,128)(2,1)S(1)} %get-tuple-element.57.held), channel_id=1, source_target_pairs={{0,1},{1,0},{2,3},{3,2},{4,5},{5,4},{6,7},{7,6},{8,9},{9,8},{10,11... | collective-permute-start | bytes 1572872 | tf_op jit(solution)/shard_map/ppermute | solution.py:440
  86.0 5.3 %shard_map.87.refs_0_ = bf16[4,2,512,128]{3,2,1,0:T(8,128)(2,1)S(1)} custom-call(bf16[8,64,256]{2,1,0:T(8,128)(2,1)S(1)} %get-tuple-element.44.here, bf16[2,8,64,256]{3,2,1,0:T(8,128)(2,1)S(1)} %collective-permute-done.8.near, bf16[2,8,64,256]{3,2,1,0:T(8,128)(2,1)S(1)} %collective-permute-done.7.far, bf16[8,512,256]{2,1,0:T(8,128)(2,1)S(1)} %shard_map.86.by_channel), custom_call_target="tpu_custom_call" | custom-call | flops 603979776 | bytes 4194304 | tf_op jit(solution)/shard_map/pallas_call | solution.py:311
  91.4 5.8 %collective-permute-done.16.across = bf16[4,8,32,256]{3,2,1,0:T(8,128)(2,1)S(1)} collective-permute-done((bf16[4,8,32,256]{3,2,1,0:T(8,128)(2,1)S(1)}, bf16[4,8,32,256]{3,2,1,0:T(8,128)(2,1)S(1)}, u32[]{:S(2)}, u32[]{:S(2)}) %collective-permute-start.16) | collective-permute-done | bytes 524320 | tf_op jit(solution)/shard_map/ppermute | solution.py:440
  97.7 1.5 %collective-permute-start.17 = (bf16[2,8,64,256]{3,2,1,0:T(8,128)(2,1)S(1)}, bf16[2,8,64,256]{3,2,1,0:T(8,128)(2,1)S(1)}, u32[]{:S(2)}, u32[]{:S(2)}) collective-permute-start(bf16[2,8,64,256]{3,2,1,0:T(8,128)(2,1)S(1)} %get-tuple-element.61), channel_id=1, source_target_pairs={{0,16},{8,24},{16,0},{24,8},{1,17},{9,25},{17,1},{25,9},{2,18},{10... | collective-permute-start | bytes 1572872 | tf_op jit(solution)/shard_map/ppermute | solution.py:440
  99.2 1.5 %collective-permute-start.19 = (bf16[4,8,32,256]{3,2,1,0:T(8,128)(2,1)S(1)}, bf16[4,8,32,256]{3,2,1,0:T(8,128)(2,1)S(1)}, u32[]{:S(2)}, u32[]{:S(2)}) collective-permute-start(bf16[4,8,32,256]{3,2,1,0:T(8,128)(2,1)S(1)} %get-tuple-element.63.held), channel_id=1, source_target_pairs={{0,1},{1,0},{2,3},{3,2},{4,5},{5,4},{6,7},{7,6},{8,9},{9,8},{10,11... | collective-permute-start | bytes 1572872 | tf_op jit(solution)/shard_map/ppermute | solution.py:440
  100.7 5.5 %shard_map.89.refs_1_ = bf16[4,2,512,128]{3,2,1,0:T(8,128)(2,1)S(1)} custom-call(bf16[8,64,256]{2,1,0:T(8,128)(2,1)S(1)} %get-tuple-element.50.here, bf16[2,8,64,256]{3,2,1,0:T(8,128)(2,1)S(1)} %collective-permute-done.13.near, bf16[2,8,64,256]{3,2,1,0:T(8,128)(2,1)S(1)} %collective-permute-done.12.far, bf16[8,512,256]{2,1,0:T(8,128)(2,1)S(1)} %shard_map.86.by_channel), custom_call_target="tpu_custom_call" | custom-call | flops 603979776 | bytes 4194304 | tf_op jit(solution)/shard_map/pallas_call | solution.py:311
  106.2 3.5 %collective-permute-done.17.far = bf16[2,8,64,256]{3,2,1,0:T(8,128)(2,1)S(1)} collective-permute-done((bf16[2,8,64,256]{3,2,1,0:T(8,128)(2,1)S(1)}, bf16[2,8,64,256]{3,2,1,0:T(8,128)(2,1)S(1)}, u32[]{:S(2)}, u32[]{:S(2)}) %collective-permute-start.17) | collective-permute-done | bytes 524320 | tf_op jit(solution)/shard_map/ppermute | solution.py:440
  112.0 5.3 %shard_map.91.refs_2_ = bf16[4,2,512,128]{3,2,1,0:T(8,128)(2,1)S(1)} custom-call(bf16[8,64,256]{2,1,0:T(8,128)(2,1)S(1)} %get-tuple-element.59.here, bf16[2,8,64,256]{3,2,1,0:T(8,128)(2,1)S(1)} %collective-permute-done.18.near, bf16[2,8,64,256]{3,2,1,0:T(8,128)(2,1)S(1)} %collective-permute-done.17.far, bf16[8,512,256]{2,1,0:T(8,128)(2,1)S(1)} %shard_map.86.by_channel), custom_call_target="tpu_custom_call" | custom-call | flops 603979776 | bytes 4194304 | tf_op jit(solution)/shard_map/pallas_call | solution.py:311
  117.3 7.4 %collective-permute-done.20.far = bf16[2,8,64,256]{3,2,1,0:T(8,128)(2,1)S(1)} collective-permute-done((bf16[2,8,64,256]{3,2,1,0:T(8,128)(2,1)S(1)}, bf16[2,8,64,256]{3,2,1,0:T(8,128)(2,1)S(1)}, u32[]{:S(2)}, u32[]{:S(2)}) %collective-permute-start.20) | collective-permute-done | bytes 524320 | tf_op jit(solution)/shard_map/ppermute | solution.py:440
  124.9 1.9 %collective-permute-done.21.near = bf16[2,8,64,256]{3,2,1,0:T(8,128)(2,1)S(1)} collective-permute-done((bf16[2,8,64,256]{3,2,1,0:T(8,128)(2,1)S(1)}, bf16[2,8,64,256]{3,2,1,0:T(8,128)(2,1)S(1)}, u32[]{:S(2)}, u32[]{:S(2)}) %collective-permute-start.21) | collective-permute-done | bytes 524320 | tf_op jit(solution)/shard_map/ppermute | solution.py:440
  126.8 5.3 %shard_map.93.refs_3_ = bf16[4,2,512,128]{3,2,1,0:T(8,128)(2,1)S(1)} custom-call(bf16[8,64,256]{2,1,0:T(8,128)(2,1)S(1)} %get-tuple-element.65.here, bf16[2,8,64,256]{3,2,1,0:T(8,128)(2,1)S(1)} %collective-permute-done.21.near, bf16[2,8,64,256]{3,2,1,0:T(8,128)(2,1)S(1)} %collective-permute-done.20.far, bf16[8,512,256]{2,1,0:T(8,128)(2,1)S(1)} %shard_map.86.by_channel), custom_call_target="tpu_custom_call" | custom-call | flops 603979776 | bytes 4194304 | tf_op jit(solution)/shard_map/pallas_call | solution.py:311
  132.1 9.9 %shard_map.94 = f32[64,32,2048]{2,1,0:T(8,128)} custom-call(bf16[4,2,512,128]{3,2,1,0:T(8,128)(2,1)S(1)} %shard_map.87.refs_0_, bf16[4,2,512,128]{3,2,1,0:T(8,128)(2,1)S(1)} %shard_map.89.refs_1_, bf16[4,2,512,128]{3,2,1,0:T(8,128)(2,1)S(1)} %shard_map.91.refs_2_, bf16[4,2,512,128]{3,2,1,0:T(8,128)(2,1)S(1)} %shard_map.93.refs_3_, ...), custom_call_target="tpu_custom_call" | custom-call | flops 4294967296 | bytes 16777216 | tf_op jit(solution)/shard_map/pallas_call | solution.py:361
  (72 shorter events, 12.5 us)
Async XLA Ops:
  0.0 17.1 %copy-start.5 = (bf16[32]{0:T(256)(128)(2,1)S(1)}, bf16[32]{0:T(256)(128)(2,1)}, u32[]{:S(2)}) copy-start(bf16[32]{0:T(256)(128)(2,1)} %param.9) | copy-start | bytes 196
  0.0 17.4 %copy-start.2 = (f32[512,272]{1,0:T(8,128)S(1)}, f32[512,272]{1,0:T(8,128)}, u32[]{:S(2)}) copy-start(f32[512,272]{1,0:T(8,128)} %constant.33.clone.angles) | copy-start | bytes 1671172
  0.0 20.0 %copy-start.7 = (s32[8]{0:T(128)S(1)}, s32[8]{0:T(128)}, u32[]{:S(2)}) copy-start(s32[8]{0:T(128)} %constant.34.clone) | copy-start | bytes 100
  0.0 27.0 %copy-start.4 = (s32[32]{0:T(128)S(1)}, s32[32]{0:T(128)}, u32[]{:S(2)}) copy-start(s32[32]{0:T(128)} %param.10) | copy-start | bytes 388
  10.6 23.5 %copy-start.6 = (s32[256]{0:T(256)S(1)}, s32[256]{0:T(256)}, u32[]{:S(2)}) copy-start(s32[256]{0:T(256)} %param.11) | copy-start | bytes 3076
  10.6 16.5 %collective-permute-start = (bf16[8,16,1024]{2,1,0:T(8,128)(2,1)}, bf16[8,16,1024]{2,1,0:T(8,128)(2,1)S(1)}, u32[]{:S(2)}, u32[]{:S(2)}) collective-permute-start(bf16[8,16,1024]{2,1,0:T(8,128)(2,1)} %get-tuple-element.38), channel_id=1, source_target_pairs={{0,1},{1,2},{2,3},{3,4},{4,5},{5,6},{6,7},{8,9},{9,10},{10,11},{11... | collective-permute-start | bytes 786440 | tf_op jit(solution)/shard_map/ppermute | solution.py:453
  15.6 11.5 %collective-permute-start.1 = (bf16[8,16,1024]{2,1,0:T(8,128)(2,1)}, bf16[8,16,1024]{2,1,0:T(8,128)(2,1)S(1)}, u32[]{:S(2)}, u32[]{:S(2)}) collective-permute-start(bf16[8,16,1024]{2,1,0:T(8,128)(2,1)} %get-tuple-element.40), channel_id=1, source_target_pairs={{1,0},{2,1},{3,2},{4,3},{5,4},{6,5},{7,6},{9,8},{10,9},{11,10},{12... | collective-permute-start | bytes 786440 | tf_op jit(solution)/shard_map/ppermute | solution.py:454
  18.7 1.4 copy-start
  27.0 1.2 copy-start.1
  29.5 14.4 %collective-permute-start.2 = (bf16[1,1,8,32,256]{4,3,2,1,0:T(8,128)(2,1)S(1)}, bf16[1,1,8,32,256]{4,3,2,1,0:T(8,128)(2,1)S(1)}, u32[]{:S(2)}, u32[]{:S(2)}) collective-permute-start(bf16[1,1,8,32,256]{4,3,2,1,0:T(8,128)(2,1)S(1)} %get-tuple-element.41), channel_id=1, source_target_pairs={{0,4},{1,5},{2,6},{3,7},{4,0},{5,1},{6,2},{7,3},{8,12},{9,13},{10,... | collective-permute-start | bytes 393224 | tf_op jit(solution)/shard_map/ppermute | solution.py:440
  34.1 12.0 %collective-permute-start.5 = (bf16[1,1,8,32,256]{4,3,2,1,0:T(8,128)(2,1)S(1)}, bf16[1,1,8,32,256]{4,3,2,1,0:T(8,128)(2,1)S(1)}, u32[]{:S(2)}, u32[]{:S(2)}) collective-permute-start(bf16[1,1,8,32,256]{4,3,2,1,0:T(8,128)(2,1)S(1)} %get-tuple-element.42), channel_id=1, source_target_pairs={{0,4},{1,5},{2,6},{3,7},{4,0},{5,1},{6,2},{7,3},{8,12},{9,13},{10,... | collective-permute-start | bytes 393224 | tf_op jit(solution)/shard_map/ppermute | solution.py:440
  34.2 19.4 %collective-permute-start.9 = (bf16[8,32,1024]{2,1,0:T(8,128)(2,1)S(1)}, bf16[8,32,1024]{2,1,0:T(8,128)(2,1)S(1)}, u32[]{:S(2)}, u32[]{:S(2)}) collective-permute-start(bf16[8,32,1024]{2,1,0:T(8,128)(2,1)S(1)} %get-tuple-element.47.here), channel_id=1, source_target_pairs={{0,16},{8,24},{16,0},{24,8},{1,17},{9,25},{17,1},{25,9},{2,18},{10... | collective-permute-start | bytes 1572872 | tf_op jit(solution)/shard_map/ppermute | solution.py:440
  43.9 9.3 %collective-permute-start.3 = (bf16[1,2,8,32,256]{4,3,2,1,0:T(8,128)(2,1)S(1)}, bf16[1,2,8,32,256]{4,3,2,1,0:T(8,128)(2,1)S(1)}, u32[]{:S(2)}, u32[]{:S(2)}) collective-permute-start(bf16[1,2,8,32,256]{4,3,2,1,0:T(8,128)(2,1)S(1)} %constant_dynamic-update-slice_fusion), channel_id=1, source_target_pairs={{0,2},{1,3},{2,0},{3,1},{4,6},{5,7},{6,4},{7,5},{8,10},{9,11},{10,... | collective-permute-start | bytes 786440 | tf_op jit(solution)/shard_map/ppermute | solution.py:440
  46.8 10.6 %collective-permute-start.6 = (bf16[1,2,8,32,256]{4,3,2,1,0:T(8,128)(2,1)}, bf16[1,2,8,32,256]{4,3,2,1,0:T(8,128)(2,1)}, u32[]{:S(2)}, u32[]{:S(2)}) collective-permute-start(bf16[1,2,8,32,256]{4,3,2,1,0:T(8,128)(2,1)} %constant_dynamic-update-slice_fusion.2), channel_id=1, source_target_pairs={{0,2},{1,3},{2,0},{3,1},{4,6},{5,7},{6,4},{7,5},{8,10},{9,11},{10,... | collective-permute-start | bytes 786440 | tf_op jit(solution)/shard_map/ppermute | solution.py:440
  53.3 11.0 %collective-permute-start.4 = (bf16[4,8,32,256]{3,2,1,0:T(8,128)(2,1)S(1)}, bf16[4,8,32,256]{3,2,1,0:T(8,128)(2,1)S(1)}, u32[]{:S(2)}, u32[]{:S(2)}) collective-permute-start(bf16[4,8,32,256]{3,2,1,0:T(8,128)(2,1)S(1)} %pad_maximum_fusion.1.held), channel_id=1, source_target_pairs={{0,1},{1,0},{2,3},{3,2},{4,5},{5,4},{6,7},{7,6},{8,9},{9,8},{10,11... | collective-permute-start | bytes 1572872 | tf_op jit(solution)/shard_map/ppermute | solution.py:440
  54.7 20.3 %collective-permute-start.10 = (bf16[2,8,32,1024]{3,2,1,0:T(8,128)(2,1)}, bf16[2,8,32,1024]{3,2,1,0:T(8,128)(2,1)S(1)}, u32[]{:S(2)}, u32[]{:S(2)}) collective-permute-start(bf16[2,8,32,1024]{3,2,1,0:T(8,128)(2,1)} %pad_maximum_fusion), channel_id=1, source_target_pairs={{0,8},{8,0},{16,24},{24,16},{1,9},{9,1},{17,25},{25,17},{2,10},{10... | collective-permute-start | bytes 3145736 | tf_op jit(solution)/shard_map/ppermute | solution.py:440
  54.9 15.3 %collective-permute-start.14 = (bf16[2,1,8,32,256]{4,3,2,1,0:T(8,128)(2,1)S(1)}, bf16[2,1,8,32,256]{4,3,2,1,0:T(8,128)(2,1)S(1)}, u32[]{:S(2)}, u32[]{:S(2)}) collective-permute-start(bf16[2,1,8,32,256]{4,3,2,1,0:T(8,128)(2,1)S(1)} %get-tuple-element.55), channel_id=1, source_target_pairs={{0,4},{1,5},{2,6},{3,7},{4,0},{5,1},{6,2},{7,3},{8,12},{9,13},{10,... | collective-permute-start | bytes 786440 | tf_op jit(solution)/shard_map/ppermute | solution.py:440
  64.7 10.1 %collective-permute-start.7 = (bf16[2,8,64,256]{3,2,1,0:T(8,128)(2,1)S(1)}, bf16[2,8,64,256]{3,2,1,0:T(8,128)(2,1)S(1)}, u32[]{:S(2)}, u32[]{:S(2)}) collective-permute-start(bf16[2,8,64,256]{3,2,1,0:T(8,128)(2,1)S(1)} %get-tuple-element.46), channel_id=1, source_target_pairs={{0,16},{8,24},{16,0},{24,8},{1,17},{9,25},{17,1},{25,9},{2,18},{10... | collective-permute-start | bytes 1572872 | tf_op jit(solution)/shard_map/ppermute | solution.py:440
  66.7 9.7 %collective-permute-start.11 = (bf16[4,8,32,256]{3,2,1,0:T(8,128)(2,1)S(1)}, bf16[4,8,32,256]{3,2,1,0:T(8,128)(2,1)S(1)}, u32[]{:S(2)}, u32[]{:S(2)}) collective-permute-start(bf16[4,8,32,256]{3,2,1,0:T(8,128)(2,1)S(1)} %pad_maximum_fusion.2.held), channel_id=1, source_target_pairs={{0,1},{1,0},{2,3},{3,2},{4,5},{5,4},{6,7},{7,6},{8,9},{9,8},{10,11... | collective-permute-start | bytes 1572872 | tf_op jit(solution)/shard_map/ppermute | solution.py:440
  70.3 13.8 %collective-permute-start.15 = (bf16[2,2,8,32,256]{4,3,2,1,0:T(8,128)(2,1)S(1)}, bf16[2,2,8,32,256]{4,3,2,1,0:T(8,128)(2,1)S(1)}, u32[]{:S(2)}, u32[]{:S(2)}) collective-permute-start(bf16[2,2,8,32,256]{4,3,2,1,0:T(8,128)(2,1)S(1)} %pad_maximum_fusion.5), channel_id=1, source_target_pairs={{0,2},{1,3},{2,0},{3,1},{4,6},{5,7},{6,4},{7,5},{8,10},{9,11},{10,... | collective-permute-start | bytes 1572872 | tf_op jit(solution)/shard_map/ppermute | solution.py:440
  74.9 11.1 %collective-permute-start.8 = (bf16[2,8,64,256]{3,2,1,0:T(8,128)(2,1)S(1)}, bf16[2,8,64,256]{3,2,1,0:T(8,128)(2,1)S(1)}, u32[]{:S(2)}, u32[]{:S(2)}) collective-permute-start(bf16[2,8,64,256]{3,2,1,0:T(8,128)(2,1)S(1)} %pad_maximum_fusion.3), channel_id=1, source_target_pairs={{0,8},{8,0},{16,24},{24,16},{1,9},{9,1},{17,25},{25,17},{2,10},{10... | collective-permute-start | bytes 1572872 | tf_op jit(solution)/shard_map/ppermute | solution.py:440
  76.8 14.5 %collective-permute-start.12 = (bf16[2,8,64,256]{3,2,1,0:T(8,128)(2,1)S(1)}, bf16[2,8,64,256]{3,2,1,0:T(8,128)(2,1)S(1)}, u32[]{:S(2)}, u32[]{:S(2)}) collective-permute-start(bf16[2,8,64,256]{3,2,1,0:T(8,128)(2,1)S(1)} %get-tuple-element.52), channel_id=1, source_target_pairs={{0,16},{8,24},{16,0},{24,8},{1,17},{9,25},{17,1},{25,9},{2,18},{10... | collective-permute-start | bytes 1572872 | tf_op jit(solution)/shard_map/ppermute | solution.py:440
  84.3 13.0 %collective-permute-start.16 = (bf16[4,8,32,256]{3,2,1,0:T(8,128)(2,1)S(1)}, bf16[4,8,32,256]{3,2,1,0:T(8,128)(2,1)S(1)}, u32[]{:S(2)}, u32[]{:S(2)}) collective-permute-start(bf16[4,8,32,256]{3,2,1,0:T(8,128)(2,1)S(1)} %get-tuple-element.57.held), channel_id=1, source_target_pairs={{0,1},{1,0},{2,3},{3,2},{4,5},{5,4},{6,7},{7,6},{8,9},{9,8},{10,11... | collective-permute-start | bytes 1572872 | tf_op jit(solution)/shard_map/ppermute | solution.py:440
  91.4 9.3 %collective-permute-start.13 = (bf16[2,8,64,256]{3,2,1,0:T(8,128)(2,1)S(1)}, bf16[2,8,64,256]{3,2,1,0:T(8,128)(2,1)S(1)}, u32[]{:S(2)}, u32[]{:S(2)}) collective-permute-start(bf16[2,8,64,256]{3,2,1,0:T(8,128)(2,1)S(1)} %pad_maximum_fusion.4), channel_id=1, source_target_pairs={{0,8},{8,0},{16,24},{24,16},{1,9},{9,1},{17,25},{25,17},{2,10},{10... | collective-permute-start | bytes 1572872 | tf_op jit(solution)/shard_map/ppermute | solution.py:440
  97.7 12.1 %collective-permute-start.17 = (bf16[2,8,64,256]{3,2,1,0:T(8,128)(2,1)S(1)}, bf16[2,8,64,256]{3,2,1,0:T(8,128)(2,1)S(1)}, u32[]{:S(2)}, u32[]{:S(2)}) collective-permute-start(bf16[2,8,64,256]{3,2,1,0:T(8,128)(2,1)S(1)} %get-tuple-element.61), channel_id=1, source_target_pairs={{0,16},{8,24},{16,0},{24,8},{1,17},{9,25},{17,1},{25,9},{2,18},{10... | collective-permute-start | bytes 1572872 | tf_op jit(solution)/shard_map/ppermute | solution.py:440
  99.2 11.7 %collective-permute-start.19 = (bf16[4,8,32,256]{3,2,1,0:T(8,128)(2,1)S(1)}, bf16[4,8,32,256]{3,2,1,0:T(8,128)(2,1)S(1)}, u32[]{:S(2)}, u32[]{:S(2)}) collective-permute-start(bf16[4,8,32,256]{3,2,1,0:T(8,128)(2,1)S(1)} %get-tuple-element.63.held), channel_id=1, source_target_pairs={{0,1},{1,0},{2,3},{3,2},{4,5},{5,4},{6,7},{7,6},{8,9},{9,8},{10,11... | collective-permute-start | bytes 1572872 | tf_op jit(solution)/shard_map/ppermute | solution.py:440
  109.8 2.2 %collective-permute-start.18 = (bf16[2,8,64,256]{3,2,1,0:T(8,128)(2,1)S(1)}, bf16[2,8,64,256]{3,2,1,0:T(8,128)(2,1)S(1)}, u32[]{:S(2)}, u32[]{:S(2)}) collective-permute-start(bf16[2,8,64,256]{3,2,1,0:T(8,128)(2,1)S(1)} %pad_maximum_fusion.7), channel_id=1, source_target_pairs={{0,8},{8,0},{16,24},{24,16},{1,9},{9,1},{17,25},{25,17},{2,10},{10... | collective-permute-start | bytes 1572872 | tf_op jit(solution)/shard_map/ppermute | solution.py:440
  111.3 13.5 %collective-permute-start.20 = (bf16[2,8,64,256]{3,2,1,0:T(8,128)(2,1)S(1)}, bf16[2,8,64,256]{3,2,1,0:T(8,128)(2,1)S(1)}, u32[]{:S(2)}, u32[]{:S(2)}) collective-permute-start(bf16[2,8,64,256]{3,2,1,0:T(8,128)(2,1)S(1)} %get-tuple-element.67), channel_id=1, source_target_pairs={{0,16},{8,24},{16,0},{24,8},{1,17},{9,25},{17,1},{25,9},{2,18},{10... | collective-permute-start | bytes 1572872 | tf_op jit(solution)/shard_map/ppermute | solution.py:440
  117.3 14.8 %copy-start.3 = (f32[2,512]{1,0:T(2,128)S(1)}, f32[2,512]{1,0:T(2,128)}, u32[]{:S(2)}) copy-start(f32[2,512]{1,0:T(2,128)} %constant.35.clone.refs_5_) | copy-start | bytes 12292
  124.8 2.0 %collective-permute-start.21 = (bf16[2,8,64,256]{3,2,1,0:T(8,128)(2,1)S(1)}, bf16[2,8,64,256]{3,2,1,0:T(8,128)(2,1)S(1)}, u32[]{:S(2)}, u32[]{:S(2)}) collective-permute-start(bf16[2,8,64,256]{3,2,1,0:T(8,128)(2,1)S(1)} %pad_maximum_fusion.9), channel_id=1, source_target_pairs={{0,8},{8,0},{16,24},{24,16},{1,9},{9,1},{17,25},{25,17},{2,10},{10... | collective-permute-start | bytes 1572872 | tf_op jit(solution)/shard_map/ppermute | solution.py:440

commit v4 on v3

--- a/solution.py
+++ b/solution.py
@@ -483,8 +483,8 @@
                 held = jnp.concatenate([held, received], axis=1)
                 if step == blocks // 2:
                     first_held.append(held)
-                    if len(gathered) > 1:
-                        held = after(held, picked[0][0])
+                    if gathered:
+                        held = after(held, picked[0][0] if picked else own_far)
             step //= 2
         gathered.extend(jnp.concatenate([held[i], received[i]], axis=0) for i in range(part.shape[0]))
 
@@ -506,7 +506,7 @@
 
     first_held = []
     for part in parts:
-        gather(after(part, [first_held[-1], own_far]) if len(first_held) > 1 else part)
+        gather(after(part, first_held[-1]) if len(first_held) > 1 else part)
         if len(gathered) == 2:
             exchange(0)
     for at in range(1, chunks):

time: 142 us -> 142 us (level)
  starting transfers between devices: 24.5 us -> 26.7 us
  waiting for transfers between devices: 62.2 us -> 60.2 us
    ppermute x20, starting transfers between devices: 18 us -> 20.2 us  [swapped(): lax.ppermute(value, axis, [(i, i ^ step) for i in range(lax.axis_size(axi...]
    ppermute x20, waiting for transfers between devices: 55.2 us -> 53.2 us  [swapped(): lax.ppermute(value, axis, [(i, i ^ step) for i in range(lax.axis_size(axi...]
  transfers between devices with their start and end apart: 22 -> 22, of which waited for: 14 -> 15; matrix products, arithmetic and copies ran while one was open for 3% -> 3% of each run, Pallas kernels for 14% -> 14%
where the time goes in v4:
time: 142 us
  waiting for transfers between devices  60.2 us (42%)
  Pallas kernels  47.6 us (34%)
  starting transfers between devices  26.7 us (19%)
  local copies, waits for them, and re-layouts  4.35 us (3%)
  other arithmetic  3.02 us (2%)
    ppermute x20, waiting for transfers between devices, swapped(): lax.ppermute(value, axis, [(i, i ^ step) for i in range(lax.axis_size(axi...  53.2 us
    pallas_call x4, Pallas kernels, cross(): pl.pallas_call(cross_kernel, grid=(1,), in_specs=[pl.BlockSpec(a.shape, f...  21.5 us
    ppermute x20, starting transfers between devices, swapped(): lax.ppermute(value, axis, [(i, i ^ step) for i in range(lax.axis_size(axi...  20.2 us
    pallas_call x1, Pallas kernels, transform(): pl.pallas_call(transform_kernel, grid=(steps,), in_specs=[pl.BlockSpec((r...  10.6 us
    pallas_call x1, Pallas kernels, lagged(): pl.pallas_call(functools.partial(lag_kernel, scaling), grid=(groups,), in...  9.94 us
    ppermute x1, waiting for transfers between devices, per_device(): left = lax.ppermute(tail, 'chan', [(i, i + 1) for i in range(blocks - 1)])  7 us
    ppermute x1, starting transfers between devices, per_device(): left = lax.ppermute(tail, 'chan', [(i, i + 1) for i in range(blocks - 1)])  4.98 us
    unnamed x18, local copies, waits for them, and re-layouts  3.29 us
  transfers between devices with their start and end apart: 22, of which 15 were waited for; matrix products, arithmetic and copies ran while one was open for 3% of the time, Pallas kernels for 14%

profile of v4, /device:TPU:0, one launch (start us, length us, event | category | flops | bytes accessed | tf_op | source)
XLA Modules:
  0.0 142.2 jit_solution(3086380075895103391)
XLA Ops:
  0.0 10.6 %shard_map.82 = (f32[8,32,1024]{2,1,0:T(8,128)}, bf16[8,16,1024]{2,1,0:T(8,128)(2,1)}, bf16[8,16,1024]{2,1,0:T(8,128)(2,1)}) custom-call(bf16[256,7680]{1,0:T(8,128)(2,1)} %bitcast.28, bf16[256,7680]{1,0:T(8,128)(2,1)} %bitcast.29, bf16[256,7680]{1,0:T(8,128)(2,1)} %bitcast.30, bf16[256,7680]{1,0:T(8,128)(2,1)} %bitcast.31, ...), custom_call_target="tpu_custom_call" | custom-call | flops 4026531840 | bytes 3932160 | tf_op jit(solution)/shard_map/pallas_call | solution.py:97
  10.6 5.0 %collective-permute-start = (bf16[8,16,1024]{2,1,0:T(8,128)(2,1)}, bf16[8,16,1024]{2,1,0:T(8,128)(2,1)S(1)}, u32[]{:S(2)}, u32[]{:S(2)}) collective-permute-start(bf16[8,16,1024]{2,1,0:T(8,128)(2,1)} %get-tuple-element.39), channel_id=1, source_target_pairs={{0,1},{1,2},{2,3},{3,4},{4,5},{5,6},{6,7},{8,9},{9,10},{10,11},{11... | collective-permute-start | bytes 786440 | tf_op jit(solution)/shard_map/ppermute | solution.py:453
  15.6 1.5 %collective-permute-start.1 = (bf16[8,16,1024]{2,1,0:T(8,128)(2,1)}, bf16[8,16,1024]{2,1,0:T(8,128)(2,1)S(1)}, u32[]{:S(2)}, u32[]{:S(2)}) collective-permute-start(bf16[8,16,1024]{2,1,0:T(8,128)(2,1)} %get-tuple-element.41), channel_id=1, source_target_pairs={{1,0},{2,1},{3,2},{4,3},{5,4},{6,5},{7,6},{9,8},{10,9},{11,10},{12... | collective-permute-start | bytes 786440 | tf_op jit(solution)/shard_map/ppermute | solution.py:454
  18.7 1.4 copy-done
  20.0 7.0 %collective-permute-done.left = bf16[8,16,1024]{2,1,0:T(8,128)(2,1)S(1)} collective-permute-done((bf16[8,16,1024]{2,1,0:T(8,128)(2,1)}, bf16[8,16,1024]{2,1,0:T(8,128)(2,1)S(1)}, u32[]{:S(2)}, u32[]{:S(2)}) %collective-permute-start) | collective-permute-done | bytes 262176 | tf_op jit(solution)/shard_map/ppermute | solution.py:453
  29.5 4.4 %collective-permute-start.2 = (bf16[1,1,8,32,256]{4,3,2,1,0:T(8,128)(2,1)S(1)}, bf16[1,1,8,32,256]{4,3,2,1,0:T(8,128)(2,1)S(1)}, u32[]{:S(2)}, u32[]{:S(2)}) collective-permute-start(bf16[1,1,8,32,256]{4,3,2,1,0:T(8,128)(2,1)S(1)} %get-tuple-element.42), channel_id=1, source_target_pairs={{0,4},{1,5},{2,6},{3,7},{4,0},{5,1},{6,2},{7,3},{8,12},{9,13},{10,... | collective-permute-start | bytes 393224 | tf_op jit(solution)/shard_map/ppermute | solution.py:440
  34.2 1.6 %collective-permute-start.6 = (bf16[8,32,1024]{2,1,0:T(8,128)(2,1)S(1)}, bf16[8,32,1024]{2,1,0:T(8,128)(2,1)S(1)}, u32[]{:S(2)}, u32[]{:S(2)}) collective-permute-start(bf16[8,32,1024]{2,1,0:T(8,128)(2,1)S(1)} %get-tuple-element.44.here), channel_id=1, source_target_pairs={{0,16},{8,24},{16,0},{24,8},{1,17},{9,25},{17,1},{25,9},{2,18},{10... | collective-permute-start | bytes 1572872 | tf_op jit(solution)/shard_map/ppermute | solution.py:440
  35.7 8.2 %collective-permute-done.2 = bf16[1,1,8,32,256]{4,3,2,1,0:T(8,128)(2,1)S(1)} collective-permute-done((bf16[1,1,8,32,256]{4,3,2,1,0:T(8,128)(2,1)S(1)}, bf16[1,1,8,32,256]{4,3,2,1,0:T(8,128)(2,1)S(1)}, u32[]{:S(2)}, u32[]{:S(2)}) %collective-permute-start.2) | collective-permute-done | bytes 131104 | tf_op jit(solution)/shard_map/ppermute | solution.py:440
  44.9 1.3 collective-permute-done.5
  46.8 4.9 %collective-permute-done.3 = bf16[1,2,8,32,256]{4,3,2,1,0:T(8,128)(2,1)S(1)} collective-permute-done((bf16[1,2,8,32,256]{4,3,2,1,0:T(8,128)(2,1)S(1)}, bf16[1,2,8,32,256]{4,3,2,1,0:T(8,128)(2,1)S(1)}, u32[]{:S(2)}, u32[]{:S(2)}) %collective-permute-start.3) | collective-permute-done | bytes 262176 | tf_op jit(solution)/shard_map/ppermute | solution.py:440
  53.9 3.6 %collective-permute-start.14 = (bf16[2,1,8,32,256]{4,3,2,1,0:T(8,128)(2,1)S(1)}, bf16[2,1,8,32,256]{4,3,2,1,0:T(8,128)(2,1)S(1)}, u32[]{:S(2)}, u32[]{:S(2)}) collective-permute-start(bf16[2,1,8,32,256]{4,3,2,1,0:T(8,128)(2,1)S(1)} %get-tuple-element.57), channel_id=1, source_target_pairs={{0,4},{1,5},{2,6},{3,7},{4,0},{5,1},{6,2},{7,3},{8,12},{9,13},{10,... | collective-permute-start | bytes 786440 | tf_op jit(solution)/shard_map/ppermute | solution.py:440
  57.4 2.7 %collective-permute-done.7 = bf16[1,2,8,32,256]{4,3,2,1,0:T(8,128)(2,1)} collective-permute-done((bf16[1,2,8,32,256]{4,3,2,1,0:T(8,128)(2,1)}, bf16[1,2,8,32,256]{4,3,2,1,0:T(8,128)(2,1)}, u32[]{:S(2)}, u32[]{:S(2)}) %collective-permute-start.7) | collective-permute-done | bytes 262176 | tf_op jit(solution)/shard_map/ppermute | solution.py:440
  61.2 3.1 %collective-permute-done.4.across = bf16[4,8,32,256]{3,2,1,0:T(8,128)(2,1)S(1)} collective-permute-done((bf16[4,8,32,256]{3,2,1,0:T(8,128)(2,1)S(1)}, bf16[4,8,32,256]{3,2,1,0:T(8,128)(2,1)S(1)}, u32[]{:S(2)}, u32[]{:S(2)}) %collective-permute-start.4) | collective-permute-done | bytes 524320 | tf_op jit(solution)/shard_map/ppermute | solution.py:440
  64.7 1.6 %collective-permute-start.8 = (bf16[2,8,64,256]{3,2,1,0:T(8,128)(2,1)S(1)}, bf16[2,8,64,256]{3,2,1,0:T(8,128)(2,1)S(1)}, u32[]{:S(2)}, u32[]{:S(2)}) collective-permute-start(bf16[2,8,64,256]{3,2,1,0:T(8,128)(2,1)S(1)} %get-tuple-element.49), channel_id=1, source_target_pairs={{0,16},{8,24},{16,0},{24,8},{1,17},{9,25},{17,1},{25,9},{2,18},{10... | collective-permute-start | bytes 1572872 | tf_op jit(solution)/shard_map/ppermute | solution.py:440
  66.6 3.5 %collective-permute-done.14 = bf16[2,1,8,32,256]{4,3,2,1,0:T(8,128)(2,1)S(1)} collective-permute-done((bf16[2,1,8,32,256]{4,3,2,1,0:T(8,128)(2,1)S(1)}, bf16[2,1,8,32,256]{4,3,2,1,0:T(8,128)(2,1)S(1)}, u32[]{:S(2)}, u32[]{:S(2)}) %collective-permute-start.14) | collective-permute-done | bytes 262176 | tf_op jit(solution)/shard_map/ppermute | solution.py:440
  70.2 6.0 %collective-permute-done.8.far = bf16[2,8,64,256]{3,2,1,0:T(8,128)(2,1)S(1)} collective-permute-done((bf16[2,8,64,256]{3,2,1,0:T(8,128)(2,1)S(1)}, bf16[2,8,64,256]{3,2,1,0:T(8,128)(2,1)S(1)}, u32[]{:S(2)}, u32[]{:S(2)}) %collective-permute-start.8) | collective-permute-done | bytes 524320 | tf_op jit(solution)/shard_map/ppermute | solution.py:440
  76.5 1.4 shard_map.86.by_channel
  78.3 1.6 %collective-permute-start.12 = (bf16[2,8,64,256]{3,2,1,0:T(8,128)(2,1)S(1)}, bf16[2,8,64,256]{3,2,1,0:T(8,128)(2,1)S(1)}, u32[]{:S(2)}, u32[]{:S(2)}) collective-permute-start(bf16[2,8,64,256]{3,2,1,0:T(8,128)(2,1)S(1)} %get-tuple-element.54), channel_id=1, source_target_pairs={{0,16},{8,24},{16,0},{24,8},{1,17},{9,25},{17,1},{25,9},{2,18},{10... | collective-permute-start | bytes 1572872 | tf_op jit(solution)/shard_map/ppermute | solution.py:440
  79.8 4.1 %collective-permute-done.15 = bf16[2,2,8,32,256]{4,3,2,1,0:T(8,128)(2,1)S(1)} collective-permute-done((bf16[2,2,8,32,256]{4,3,2,1,0:T(8,128)(2,1)S(1)}, bf16[2,2,8,32,256]{4,3,2,1,0:T(8,128)(2,1)S(1)}, u32[]{:S(2)}, u32[]{:S(2)}) %collective-permute-start.15) | collective-permute-done | bytes 524320 | tf_op jit(solution)/shard_map/ppermute | solution.py:440
  84.1 2.0 %collective-permute-start.16 = (bf16[4,8,32,256]{3,2,1,0:T(8,128)(2,1)S(1)}, bf16[4,8,32,256]{3,2,1,0:T(8,128)(2,1)S(1)}, u32[]{:S(2)}, u32[]{:S(2)}) collective-permute-start(bf16[4,8,32,256]{3,2,1,0:T(8,128)(2,1)S(1)} %get-tuple-element.59.held), channel_id=1, source_target_pairs={{0,1},{1,0},{2,3},{3,2},{4,5},{5,4},{6,7},{7,6},{8,9},{9,8},{10,11... | collective-permute-start | bytes 1572872 | tf_op jit(solution)/shard_map/ppermute | solution.py:440
  86.1 5.3 %shard_map.87.refs_0_ = bf16[4,2,512,128]{3,2,1,0:T(8,128)(2,1)S(1)} custom-call(bf16[8,64,256]{2,1,0:T(8,128)(2,1)S(1)} %get-tuple-element.47.here, bf16[2,8,64,256]{3,2,1,0:T(8,128)(2,1)S(1)} %collective-permute-done.9.near, bf16[2,8,64,256]{3,2,1,0:T(8,128)(2,1)S(1)} %collective-permute-done.8.far, bf16[8,512,256]{2,1,0:T(8,128)(2,1)S(1)} %shard_map.86.by_channel), custom_call_target="tpu_custom_call" | custom-call | flops 603979776 | bytes 4194304 | tf_op jit(solution)/shard_map/pallas_call | solution.py:311
  91.4 1.3 collective-permute-done.12.far
  92.8 4.4 %collective-permute-done.16.across = bf16[4,8,32,256]{3,2,1,0:T(8,128)(2,1)S(1)} collective-permute-done((bf16[4,8,32,256]{3,2,1,0:T(8,128)(2,1)S(1)}, bf16[4,8,32,256]{3,2,1,0:T(8,128)(2,1)S(1)}, u32[]{:S(2)}, u32[]{:S(2)}) %collective-permute-start.16) | collective-permute-done | bytes 524320 | tf_op jit(solution)/shard_map/ppermute | solution.py:440
  97.7 1.6 %collective-permute-start.17 = (bf16[2,8,64,256]{3,2,1,0:T(8,128)(2,1)S(1)}, bf16[2,8,64,256]{3,2,1,0:T(8,128)(2,1)S(1)}, u32[]{:S(2)}, u32[]{:S(2)}) collective-permute-start(bf16[2,8,64,256]{3,2,1,0:T(8,128)(2,1)S(1)} %get-tuple-element.63), channel_id=1, source_target_pairs={{0,16},{8,24},{16,0},{24,8},{1,17},{9,25},{17,1},{25,9},{2,18},{10... | collective-permute-start | bytes 1572872 | tf_op jit(solution)/shard_map/ppermute | solution.py:440
  99.2 1.7 %collective-permute-start.19 = (bf16[4,8,32,256]{3,2,1,0:T(8,128)(2,1)S(1)}, bf16[4,8,32,256]{3,2,1,0:T(8,128)(2,1)S(1)}, u32[]{:S(2)}, u32[]{:S(2)}) collective-permute-start(bf16[4,8,32,256]{3,2,1,0:T(8,128)(2,1)S(1)} %get-tuple-element.65.held), channel_id=1, source_target_pairs={{0,1},{1,0},{2,3},{3,2},{4,5},{5,4},{6,7},{7,6},{8,9},{9,8},{10,11... | collective-permute-start | bytes 1572872 | tf_op jit(solution)/shard_map/ppermute | solution.py:440
  101.0 5.5 %shard_map.89.refs_1_ = bf16[4,2,512,128]{3,2,1,0:T(8,128)(2,1)S(1)} custom-call(bf16[8,64,256]{2,1,0:T(8,128)(2,1)S(1)} %get-tuple-element.52.here, bf16[2,8,64,256]{3,2,1,0:T(8,128)(2,1)S(1)} %collective-permute-done.13.near, bf16[2,8,64,256]{3,2,1,0:T(8,128)(2,1)S(1)} %collective-permute-done.12.far, bf16[8,512,256]{2,1,0:T(8,128)(2,1)S(1)} %shard_map.86.by_channel), custom_call_target="tpu_custom_call" | custom-call | flops 603979776 | bytes 4194304 | tf_op jit(solution)/shard_map/pallas_call | solution.py:311
  106.5 3.4 %collective-permute-done.17.far = bf16[2,8,64,256]{3,2,1,0:T(8,128)(2,1)S(1)} collective-permute-done((bf16[2,8,64,256]{3,2,1,0:T(8,128)(2,1)S(1)}, bf16[2,8,64,256]{3,2,1,0:T(8,128)(2,1)S(1)}, u32[]{:S(2)}, u32[]{:S(2)}) %collective-permute-start.17) | collective-permute-done | bytes 524320 | tf_op jit(solution)/shard_map/ppermute | solution.py:440
  112.1 5.3 %shard_map.91.refs_2_ = bf16[4,2,512,128]{3,2,1,0:T(8,128)(2,1)S(1)} custom-call(bf16[8,64,256]{2,1,0:T(8,128)(2,1)S(1)} %get-tuple-element.61.here, bf16[2,8,64,256]{3,2,1,0:T(8,128)(2,1)S(1)} %collective-permute-done.18.near, bf16[2,8,64,256]{3,2,1,0:T(8,128)(2,1)S(1)} %collective-permute-done.17.far, bf16[8,512,256]{2,1,0:T(8,128)(2,1)S(1)} %shard_map.86.by_channel), custom_call_target="tpu_custom_call" | custom-call | flops 603979776 | bytes 4194304 | tf_op jit(solution)/shard_map/pallas_call | solution.py:311
  117.5 7.4 %collective-permute-done.20.far = bf16[2,8,64,256]{3,2,1,0:T(8,128)(2,1)S(1)} collective-permute-done((bf16[2,8,64,256]{3,2,1,0:T(8,128)(2,1)S(1)}, bf16[2,8,64,256]{3,2,1,0:T(8,128)(2,1)S(1)}, u32[]{:S(2)}, u32[]{:S(2)}) %collective-permute-start.20) | collective-permute-done | bytes 524320 | tf_op jit(solution)/shard_map/ppermute | solution.py:440
  125.0 1.9 %collective-permute-done.21.near = bf16[2,8,64,256]{3,2,1,0:T(8,128)(2,1)S(1)} collective-permute-done((bf16[2,8,64,256]{3,2,1,0:T(8,128)(2,1)S(1)}, bf16[2,8,64,256]{3,2,1,0:T(8,128)(2,1)S(1)}, u32[]{:S(2)}, u32[]{:S(2)}) %collective-permute-start.21) | collective-permute-done | bytes 524320 | tf_op jit(solution)/shard_map/ppermute | solution.py:440
  126.9 5.3 %shard_map.93.refs_3_ = bf16[4,2,512,128]{3,2,1,0:T(8,128)(2,1)S(1)} custom-call(bf16[8,64,256]{2,1,0:T(8,128)(2,1)S(1)} %get-tuple-element.67.here, bf16[2,8,64,256]{3,2,1,0:T(8,128)(2,1)S(1)} %collective-permute-done.21.near, bf16[2,8,64,256]{3,2,1,0:T(8,128)(2,1)S(1)} %collective-permute-done.20.far, bf16[8,512,256]{2,1,0:T(8,128)(2,1)S(1)} %shard_map.86.by_channel), custom_call_target="tpu_custom_call" | custom-call | flops 603979776 | bytes 4194304 | tf_op jit(solution)/shard_map/pallas_call | solution.py:311
  132.2 9.9 %shard_map.94 = f32[64,32,2048]{2,1,0:T(8,128)} custom-call(bf16[4,2,512,128]{3,2,1,0:T(8,128)(2,1)S(1)} %shard_map.87.refs_0_, bf16[4,2,512,128]{3,2,1,0:T(8,128)(2,1)S(1)} %shard_map.89.refs_1_, bf16[4,2,512,128]{3,2,1,0:T(8,128)(2,1)S(1)} %shard_map.91.refs_2_, bf16[4,2,512,128]{3,2,1,0:T(8,128)(2,1)S(1)} %shard_map.93.refs_3_, ...), custom_call_target="tpu_custom_call" | custom-call | flops 4294967296 | bytes 16777216 | tf_op jit(solution)/shard_map/pallas_call | solution.py:361
  (72 shorter events, 13.6 us)
Async XLA Ops:
  0.0 17.1 %copy-start.5 = (bf16[32]{0:T(256)(128)(2,1)S(1)}, bf16[32]{0:T(256)(128)(2,1)}, u32[]{:S(2)}) copy-start(bf16[32]{0:T(256)(128)(2,1)} %param.9) | copy-start | bytes 196
  0.0 17.4 %copy-start.2 = (f32[512,272]{1,0:T(8,128)S(1)}, f32[512,272]{1,0:T(8,128)}, u32[]{:S(2)}) copy-start(f32[512,272]{1,0:T(8,128)} %constant.33.clone.angles) | copy-start | bytes 1671172
  0.0 20.0 %copy-start.7 = (s32[8]{0:T(128)S(1)}, s32[8]{0:T(128)}, u32[]{:S(2)}) copy-start(s32[8]{0:T(128)} %constant.34.clone) | copy-start | bytes 100
  0.0 27.0 %copy-start.4 = (s32[32]{0:T(128)S(1)}, s32[32]{0:T(128)}, u32[]{:S(2)}) copy-start(s32[32]{0:T(128)} %param.10) | copy-start | bytes 388
  10.6 23.5 %copy-start.6 = (s32[256]{0:T(256)S(1)}, s32[256]{0:T(256)}, u32[]{:S(2)}) copy-start(s32[256]{0:T(256)} %param.11) | copy-start | bytes 3076
  10.6 16.5 %collective-permute-start = (bf16[8,16,1024]{2,1,0:T(8,128)(2,1)}, bf16[8,16,1024]{2,1,0:T(8,128)(2,1)S(1)}, u32[]{:S(2)}, u32[]{:S(2)}) collective-permute-start(bf16[8,16,1024]{2,1,0:T(8,128)(2,1)} %get-tuple-element.39), channel_id=1, source_target_pairs={{0,1},{1,2},{2,3},{3,4},{4,5},{5,6},{6,7},{8,9},{9,10},{10,11},{11... | collective-permute-start | bytes 786440 | tf_op jit(solution)/shard_map/ppermute | solution.py:453
  15.6 11.5 %collective-permute-start.1 = (bf16[8,16,1024]{2,1,0:T(8,128)(2,1)}, bf16[8,16,1024]{2,1,0:T(8,128)(2,1)S(1)}, u32[]{:S(2)}, u32[]{:S(2)}) collective-permute-start(bf16[8,16,1024]{2,1,0:T(8,128)(2,1)} %get-tuple-element.41), channel_id=1, source_target_pairs={{1,0},{2,1},{3,2},{4,3},{5,4},{6,5},{7,6},{9,8},{10,9},{11,10},{12... | collective-permute-start | bytes 786440 | tf_op jit(solution)/shard_map/ppermute | solution.py:454
  18.7 1.4 copy-start
  27.0 1.2 copy-start.1
  29.5 14.4 %collective-permute-start.2 = (bf16[1,1,8,32,256]{4,3,2,1,0:T(8,128)(2,1)S(1)}, bf16[1,1,8,32,256]{4,3,2,1,0:T(8,128)(2,1)S(1)}, u32[]{:S(2)}, u32[]{:S(2)}) collective-permute-start(bf16[1,1,8,32,256]{4,3,2,1,0:T(8,128)(2,1)S(1)} %get-tuple-element.42), channel_id=1, source_target_pairs={{0,4},{1,5},{2,6},{3,7},{4,0},{5,1},{6,2},{7,3},{8,12},{9,13},{10,... | collective-permute-start | bytes 393224 | tf_op jit(solution)/shard_map/ppermute | solution.py:440
  34.1 12.0 %collective-permute-start.5 = (bf16[1,1,8,32,256]{4,3,2,1,0:T(8,128)(2,1)S(1)}, bf16[1,1,8,32,256]{4,3,2,1,0:T(8,128)(2,1)S(1)}, u32[]{:S(2)}, u32[]{:S(2)}) collective-permute-start(bf16[1,1,8,32,256]{4,3,2,1,0:T(8,128)(2,1)S(1)} %get-tuple-element.43), channel_id=1, source_target_pairs={{0,4},{1,5},{2,6},{3,7},{4,0},{5,1},{6,2},{7,3},{8,12},{9,13},{10,... | collective-permute-start | bytes 393224 | tf_op jit(solution)/shard_map/ppermute | solution.py:440
  34.2 17.7 %collective-permute-start.6 = (bf16[8,32,1024]{2,1,0:T(8,128)(2,1)S(1)}, bf16[8,32,1024]{2,1,0:T(8,128)(2,1)S(1)}, u32[]{:S(2)}, u32[]{:S(2)}) collective-permute-start(bf16[8,32,1024]{2,1,0:T(8,128)(2,1)S(1)} %get-tuple-element.44.here), channel_id=1, source_target_pairs={{0,16},{8,24},{16,0},{24,8},{1,17},{9,25},{17,1},{25,9},{2,18},{10... | collective-permute-start | bytes 1572872 | tf_op jit(solution)/shard_map/ppermute | solution.py:440
  43.9 7.8 %collective-permute-start.3 = (bf16[1,2,8,32,256]{4,3,2,1,0:T(8,128)(2,1)S(1)}, bf16[1,2,8,32,256]{4,3,2,1,0:T(8,128)(2,1)S(1)}, u32[]{:S(2)}, u32[]{:S(2)}) collective-permute-start(bf16[1,2,8,32,256]{4,3,2,1,0:T(8,128)(2,1)S(1)} %constant_dynamic-update-slice_fusion), channel_id=1, source_target_pairs={{0,2},{1,3},{2,0},{3,1},{4,6},{5,7},{6,4},{7,5},{8,10},{9,11},{10,... | collective-permute-start | bytes 786440 | tf_op jit(solution)/shard_map/ppermute | solution.py:440
  51.8 12.5 %collective-permute-start.4 = (bf16[4,8,32,256]{3,2,1,0:T(8,128)(2,1)S(1)}, bf16[4,8,32,256]{3,2,1,0:T(8,128)(2,1)S(1)}, u32[]{:S(2)}, u32[]{:S(2)}) collective-permute-start(bf16[4,8,32,256]{3,2,1,0:T(8,128)(2,1)S(1)} %pad_maximum_fusion.1.held), channel_id=1, source_target_pairs={{0,1},{1,0},{2,3},{3,2},{4,5},{5,4},{6,7},{7,6},{8,9},{9,8},{10,11... | collective-permute-start | bytes 1572872 | tf_op jit(solution)/shard_map/ppermute | solution.py:440
  51.9 8.3 %collective-permute-start.7 = (bf16[1,2,8,32,256]{4,3,2,1,0:T(8,128)(2,1)}, bf16[1,2,8,32,256]{4,3,2,1,0:T(8,128)(2,1)}, u32[]{:S(2)}, u32[]{:S(2)}) collective-permute-start(bf16[1,2,8,32,256]{4,3,2,1,0:T(8,128)(2,1)} %constant_dynamic-update-slice_fusion.2), channel_id=1, source_target_pairs={{0,2},{1,3},{2,0},{3,1},{4,6},{5,7},{6,4},{7,5},{8,10},{9,11},{10,... | collective-permute-start | bytes 786440 | tf_op jit(solution)/shard_map/ppermute | solution.py:440
  53.6 22.9 %collective-permute-start.10 = (bf16[2,8,32,1024]{3,2,1,0:T(8,128)(2,1)}, bf16[2,8,32,1024]{3,2,1,0:T(8,128)(2,1)S(1)}, u32[]{:S(2)}, u32[]{:S(2)}) collective-permute-start(bf16[2,8,32,1024]{3,2,1,0:T(8,128)(2,1)} %pad_maximum_fusion), channel_id=1, source_target_pairs={{0,8},{8,0},{16,24},{24,16},{1,9},{9,1},{17,25},{25,17},{2,10},{10... | collective-permute-start | bytes 3145736 | tf_op jit(solution)/shard_map/ppermute | solution.py:440
  53.9 16.2 %collective-permute-start.14 = (bf16[2,1,8,32,256]{4,3,2,1,0:T(8,128)(2,1)S(1)}, bf16[2,1,8,32,256]{4,3,2,1,0:T(8,128)(2,1)S(1)}, u32[]{:S(2)}, u32[]{:S(2)}) collective-permute-start(bf16[2,1,8,32,256]{4,3,2,1,0:T(8,128)(2,1)S(1)} %get-tuple-element.57), channel_id=1, source_target_pairs={{0,4},{1,5},{2,6},{3,7},{4,0},{5,1},{6,2},{7,3},{8,12},{9,13},{10,... | collective-permute-start | bytes 786440 | tf_op jit(solution)/shard_map/ppermute | solution.py:440
  64.7 11.6 %collective-permute-start.8 = (bf16[2,8,64,256]{3,2,1,0:T(8,128)(2,1)S(1)}, bf16[2,8,64,256]{3,2,1,0:T(8,128)(2,1)S(1)}, u32[]{:S(2)}, u32[]{:S(2)}) collective-permute-start(bf16[2,8,64,256]{3,2,1,0:T(8,128)(2,1)S(1)} %get-tuple-element.49), channel_id=1, source_target_pairs={{0,16},{8,24},{16,0},{24,8},{1,17},{9,25},{17,1},{25,9},{2,18},{10... | collective-permute-start | bytes 1572872 | tf_op jit(solution)/shard_map/ppermute | solution.py:440
  66.3 11.6 %collective-permute-start.11 = (bf16[4,8,32,256]{3,2,1,0:T(8,128)(2,1)S(1)}, bf16[4,8,32,256]{3,2,1,0:T(8,128)(2,1)S(1)}, u32[]{:S(2)}, u32[]{:S(2)}) collective-permute-start(bf16[4,8,32,256]{3,2,1,0:T(8,128)(2,1)S(1)} %pad_maximum_fusion.2.held), channel_id=1, source_target_pairs={{0,1},{1,0},{2,3},{3,2},{4,5},{5,4},{6,7},{7,6},{8,9},{9,8},{10,11... | collective-permute-start | bytes 1572872 | tf_op jit(solution)/shard_map/ppermute | solution.py:440
  70.1 13.8 %collective-permute-start.15 = (bf16[2,2,8,32,256]{4,3,2,1,0:T(8,128)(2,1)S(1)}, bf16[2,2,8,32,256]{4,3,2,1,0:T(8,128)(2,1)S(1)}, u32[]{:S(2)}, u32[]{:S(2)}) collective-permute-start(bf16[2,2,8,32,256]{4,3,2,1,0:T(8,128)(2,1)S(1)} %pad_maximum_fusion.5), channel_id=1, source_target_pairs={{0,2},{1,3},{2,0},{3,1},{4,6},{5,7},{6,4},{7,5},{8,10},{9,11},{10,... | collective-permute-start | bytes 1572872 | tf_op jit(solution)/shard_map/ppermute | solution.py:440
  76.4 9.7 %collective-permute-start.9 = (bf16[2,8,64,256]{3,2,1,0:T(8,128)(2,1)S(1)}, bf16[2,8,64,256]{3,2,1,0:T(8,128)(2,1)S(1)}, u32[]{:S(2)}, u32[]{:S(2)}) collective-permute-start(bf16[2,8,64,256]{3,2,1,0:T(8,128)(2,1)S(1)} %pad_maximum_fusion.3), channel_id=1, source_target_pairs={{0,8},{8,0},{16,24},{24,16},{1,9},{9,1},{17,25},{25,17},{2,10},{10... | collective-permute-start | bytes 1572872 | tf_op jit(solution)/shard_map/ppermute | solution.py:440
  78.3 14.4 %collective-permute-start.12 = (bf16[2,8,64,256]{3,2,1,0:T(8,128)(2,1)S(1)}, bf16[2,8,64,256]{3,2,1,0:T(8,128)(2,1)S(1)}, u32[]{:S(2)}, u32[]{:S(2)}) collective-permute-start(bf16[2,8,64,256]{3,2,1,0:T(8,128)(2,1)S(1)} %get-tuple-element.54), channel_id=1, source_target_pairs={{0,16},{8,24},{16,0},{24,8},{1,17},{9,25},{17,1},{25,9},{2,18},{10... | collective-permute-start | bytes 1572872 | tf_op jit(solution)/shard_map/ppermute | solution.py:440
  84.1 13.1 %collective-permute-start.16 = (bf16[4,8,32,256]{3,2,1,0:T(8,128)(2,1)S(1)}, bf16[4,8,32,256]{3,2,1,0:T(8,128)(2,1)S(1)}, u32[]{:S(2)}, u32[]{:S(2)}) collective-permute-start(bf16[4,8,32,256]{3,2,1,0:T(8,128)(2,1)S(1)} %get-tuple-element.59.held), channel_id=1, source_target_pairs={{0,1},{1,0},{2,3},{3,2},{4,5},{5,4},{6,7},{7,6},{8,9},{9,8},{10,11... | collective-permute-start | bytes 1572872 | tf_op jit(solution)/shard_map/ppermute | solution.py:440
  92.8 8.2 %collective-permute-start.13 = (bf16[2,8,64,256]{3,2,1,0:T(8,128)(2,1)S(1)}, bf16[2,8,64,256]{3,2,1,0:T(8,128)(2,1)S(1)}, u32[]{:S(2)}, u32[]{:S(2)}) collective-permute-start(bf16[2,8,64,256]{3,2,1,0:T(8,128)(2,1)S(1)} %pad_maximum_fusion.4), channel_id=1, source_target_pairs={{0,8},{8,0},{16,24},{24,16},{1,9},{9,1},{17,25},{25,17},{2,10},{10... | collective-permute-start | bytes 1572872 | tf_op jit(solution)/shard_map/ppermute | solution.py:440
  97.7 12.2 %collective-permute-start.17 = (bf16[2,8,64,256]{3,2,1,0:T(8,128)(2,1)S(1)}, bf16[2,8,64,256]{3,2,1,0:T(8,128)(2,1)S(1)}, u32[]{:S(2)}, u32[]{:S(2)}) collective-permute-start(bf16[2,8,64,256]{3,2,1,0:T(8,128)(2,1)S(1)} %get-tuple-element.63), channel_id=1, source_target_pairs={{0,16},{8,24},{16,0},{24,8},{1,17},{9,25},{17,1},{25,9},{2,18},{10... | collective-permute-start | bytes 1572872 | tf_op jit(solution)/shard_map/ppermute | solution.py:440
  99.2 11.9 %collective-permute-start.19 = (bf16[4,8,32,256]{3,2,1,0:T(8,128)(2,1)S(1)}, bf16[4,8,32,256]{3,2,1,0:T(8,128)(2,1)S(1)}, u32[]{:S(2)}, u32[]{:S(2)}) collective-permute-start(bf16[4,8,32,256]{3,2,1,0:T(8,128)(2,1)S(1)} %get-tuple-element.65.held), channel_id=1, source_target_pairs={{0,1},{1,0},{2,3},{3,2},{4,5},{5,4},{6,7},{7,6},{8,9},{9,8},{10,11... | collective-permute-start | bytes 1572872 | tf_op jit(solution)/shard_map/ppermute | solution.py:440
  109.9 2.2 %collective-permute-start.18 = (bf16[2,8,64,256]{3,2,1,0:T(8,128)(2,1)S(1)}, bf16[2,8,64,256]{3,2,1,0:T(8,128)(2,1)S(1)}, u32[]{:S(2)}, u32[]{:S(2)}) collective-permute-start(bf16[2,8,64,256]{3,2,1,0:T(8,128)(2,1)S(1)} %pad_maximum_fusion.7), channel_id=1, source_target_pairs={{0,8},{8,0},{16,24},{24,16},{1,9},{9,1},{17,25},{25,17},{2,10},{10... | collective-permute-start | bytes 1572872 | tf_op jit(solution)/shard_map/ppermute | solution.py:440
  111.5 13.3 %collective-permute-start.20 = (bf16[2,8,64,256]{3,2,1,0:T(8,128)(2,1)S(1)}, bf16[2,8,64,256]{3,2,1,0:T(8,128)(2,1)S(1)}, u32[]{:S(2)}, u32[]{:S(2)}) collective-permute-start(bf16[2,8,64,256]{3,2,1,0:T(8,128)(2,1)S(1)} %get-tuple-element.69), channel_id=1, source_target_pairs={{0,16},{8,24},{16,0},{24,8},{1,17},{9,25},{17,1},{25,9},{2,18},{10... | collective-permute-start | bytes 1572872 | tf_op jit(solution)/shard_map/ppermute | solution.py:440
  117.4 14.8 %copy-start.3 = (f32[2,512]{1,0:T(2,128)S(1)}, f32[2,512]{1,0:T(2,128)}, u32[]{:S(2)}) copy-start(f32[2,512]{1,0:T(2,128)} %constant.35.clone.refs_5_) | copy-start | bytes 12292
  124.9 2.0 %collective-permute-start.21 = (bf16[2,8,64,256]{3,2,1,0:T(8,128)(2,1)S(1)}, bf16[2,8,64,256]{3,2,1,0:T(8,128)(2,1)S(1)}, u32[]{:S(2)}, u32[]{:S(2)}) collective-permute-start(bf16[2,8,64,256]{3,2,1,0:T(8,128)(2,1)S(1)} %pad_maximum_fusion.9), channel_id=1, source_target_pairs={{0,8},{8,0},{16,24},{24,16},{1,9},{9,1},{17,25},{25,17},{2,10},{10... | collective-permute-start | bytes 1572872 | tf_op jit(solution)/shard_map/ppermute | solution.py:440

commit v5 on v4

--- a/solution.py
+++ b/solution.py
@@ -19,7 +19,7 @@
 STEP = 640
 FINE = 32
 CHUNKS = tuple((start, 128) for start in range(0, F, 128))
-Z_GROUPS = ((0, 1), (1, 2), (2, 4))
+Z_GROUPS = ((0, 1), (1, 2), (2, 3), (3, 4))
 GROUP = 16
 LAG_FINE = 128
 LAG_ROWS = 8
@@ -484,7 +484,7 @@
                 if step == blocks // 2:
                     first_held.append(held)
                     if gathered:
-                        held = after(held, picked[0][0] if picked else own_far)
+                        held = after(held, gathered[-1] if picked else own_far)
             step //= 2
         gathered.extend(jnp.concatenate([held[i], received[i]], axis=0) for i in range(part.shape[0]))
 

time: 142 us -> 144 us (1.014)
  starting transfers between devices: 26.7 us -> 29.5 us
    ppermute x20 -> x22, starting transfers between devices: 20.2 us -> 23.1 us  [swapped(): lax.ppermute(value, axis, [(i, i ^ step) for i in range(lax.axis_size(axi...]
    ppermute x20 -> x22, waiting for transfers between devices: 53.2 us -> 52.4 us  [swapped(): lax.ppermute(value, axis, [(i, i ^ step) for i in range(lax.axis_size(axi...]
    unnamed x18 -> x19, local copies, waits for them, and re-layouts: 3.29 us -> 3.28 us
  transfers between devices with their start and end apart: 22 -> 24, of which waited for: 15 -> 15; matrix products, arithmetic and copies ran while one was open for 3% -> 3% of each run, Pallas kernels for 14% -> 14%
where the time goes in v5:
time: 144 us
  waiting for transfers between devices  59.4 us (41%)
  Pallas kernels  47.6 us (33%)
  starting transfers between devices  29.5 us (20%)
  local copies, waits for them, and re-layouts  4.27 us (3%)
  other arithmetic  3 us (2%)
    ppermute x22, waiting for transfers between devices, swapped(): lax.ppermute(value, axis, [(i, i ^ step) for i in range(lax.axis_size(axi...  52.4 us
    ppermute x22, starting transfers between devices, swapped(): lax.ppermute(value, axis, [(i, i ^ step) for i in range(lax.axis_size(axi...  23.1 us
    pallas_call x4, Pallas kernels, cross(): pl.pallas_call(cross_kernel, grid=(1,), in_specs=[pl.BlockSpec(a.shape, f...  21.5 us
    pallas_call x1, Pallas kernels, transform(): pl.pallas_call(transform_kernel, grid=(steps,), in_specs=[pl.BlockSpec((r...  10.6 us
    pallas_call x1, Pallas kernels, lagged(): pl.pallas_call(functools.partial(lag_kernel, scaling), grid=(groups,), in...  9.94 us
    ppermute x1, waiting for transfers between devices, per_device(): left = lax.ppermute(tail, 'chan', [(i, i + 1) for i in range(blocks - 1)])  7.01 us
    ppermute x1, starting transfers between devices, per_device(): left = lax.ppermute(tail, 'chan', [(i, i + 1) for i in range(blocks - 1)])  4.98 us
    unnamed x19, local copies, waits for them, and re-layouts  3.28 us
  transfers between devices with their start and end apart: 24, of which 15 were waited for; matrix products, arithmetic and copies ran while one was open for 3% of the time, Pallas kernels for 14%

profile of v5, /device:TPU:0, one launch (start us, length us, event | category | flops | bytes accessed | tf_op | source)
XLA Modules:
  0.0 144.2 jit_solution(15525918070082295239)
XLA Ops:
  0.0 10.6 %shard_map.82 = (f32[8,32,1024]{2,1,0:T(8,128)}, bf16[8,16,1024]{2,1,0:T(8,128)(2,1)}, bf16[8,16,1024]{2,1,0:T(8,128)(2,1)}) custom-call(bf16[256,7680]{1,0:T(8,128)(2,1)} %bitcast.24, bf16[256,7680]{1,0:T(8,128)(2,1)} %bitcast.25, bf16[256,7680]{1,0:T(8,128)(2,1)} %bitcast.26, bf16[256,7680]{1,0:T(8,128)(2,1)} %bitcast.27, ...), custom_call_target="tpu_custom_call" | custom-call | flops 4026531840 | bytes 3932160 | tf_op jit(solution)/shard_map/pallas_call | solution.py:97
  10.6 5.0 %collective-permute-start = (bf16[8,16,1024]{2,1,0:T(8,128)(2,1)}, bf16[8,16,1024]{2,1,0:T(8,128)(2,1)S(1)}, u32[]{:S(2)}, u32[]{:S(2)}) collective-permute-start(bf16[8,16,1024]{2,1,0:T(8,128)(2,1)} %get-tuple-element.42), channel_id=1, source_target_pairs={{0,1},{1,2},{2,3},{3,4},{4,5},{5,6},{6,7},{8,9},{9,10},{10,11},{11... | collective-permute-start | bytes 786440 | tf_op jit(solution)/shard_map/ppermute | solution.py:453
  15.6 1.5 %collective-permute-start.1 = (bf16[8,16,1024]{2,1,0:T(8,128)(2,1)}, bf16[8,16,1024]{2,1,0:T(8,128)(2,1)S(1)}, u32[]{:S(2)}, u32[]{:S(2)}) collective-permute-start(bf16[8,16,1024]{2,1,0:T(8,128)(2,1)} %get-tuple-element.44), channel_id=1, source_target_pairs={{1,0},{2,1},{3,2},{4,3},{5,4},{6,5},{7,6},{9,8},{10,9},{11,10},{12... | collective-permute-start | bytes 786440 | tf_op jit(solution)/shard_map/ppermute | solution.py:454
  17.4 1.3 shard_map.83.refs_4_
  18.7 1.3 copy-done
  20.0 7.0 %collective-permute-done.left = bf16[8,16,1024]{2,1,0:T(8,128)(2,1)S(1)} collective-permute-done((bf16[8,16,1024]{2,1,0:T(8,128)(2,1)}, bf16[8,16,1024]{2,1,0:T(8,128)(2,1)S(1)}, u32[]{:S(2)}, u32[]{:S(2)}) %collective-permute-start) | collective-permute-done | bytes 262176 | tf_op jit(solution)/shard_map/ppermute | solution.py:453
  28.3 1.2 shard_map.84
  29.5 4.5 %collective-permute-start.2 = (bf16[1,1,8,32,256]{4,3,2,1,0:T(8,128)(2,1)S(1)}, bf16[1,1,8,32,256]{4,3,2,1,0:T(8,128)(2,1)S(1)}, u32[]{:S(2)}, u32[]{:S(2)}) collective-permute-start(bf16[1,1,8,32,256]{4,3,2,1,0:T(8,128)(2,1)S(1)} %get-tuple-element.45), channel_id=1, source_target_pairs={{0,4},{1,5},{2,6},{3,7},{4,0},{5,1},{6,2},{7,3},{8,12},{9,13},{10,... | collective-permute-start | bytes 393224 | tf_op jit(solution)/shard_map/ppermute | solution.py:440
  34.2 1.6 %collective-permute-start.6 = (bf16[8,32,1024]{2,1,0:T(8,128)(2,1)S(1)}, bf16[8,32,1024]{2,1,0:T(8,128)(2,1)S(1)}, u32[]{:S(2)}, u32[]{:S(2)}) collective-permute-start(bf16[8,32,1024]{2,1,0:T(8,128)(2,1)S(1)} %get-tuple-element.47.here), channel_id=1, source_target_pairs={{0,16},{8,24},{16,0},{24,8},{1,17},{9,25},{17,1},{25,9},{2,18},{10... | collective-permute-start | bytes 1572872 | tf_op jit(solution)/shard_map/ppermute | solution.py:440
  35.7 8.2 %collective-permute-done.2 = bf16[1,1,8,32,256]{4,3,2,1,0:T(8,128)(2,1)S(1)} collective-permute-done((bf16[1,1,8,32,256]{4,3,2,1,0:T(8,128)(2,1)S(1)}, bf16[1,1,8,32,256]{4,3,2,1,0:T(8,128)(2,1)S(1)}, u32[]{:S(2)}, u32[]{:S(2)}) %collective-permute-start.2) | collective-permute-done | bytes 131104 | tf_op jit(solution)/shard_map/ppermute | solution.py:440
  44.8 1.3 collective-permute-done.5
  46.8 4.9 %collective-permute-done.3 = bf16[1,2,8,32,256]{4,3,2,1,0:T(8,128)(2,1)S(1)} collective-permute-done((bf16[1,2,8,32,256]{4,3,2,1,0:T(8,128)(2,1)S(1)}, bf16[1,2,8,32,256]{4,3,2,1,0:T(8,128)(2,1)S(1)}, u32[]{:S(2)}, u32[]{:S(2)}) %collective-permute-start.3) | collective-permute-done | bytes 262176 | tf_op jit(solution)/shard_map/ppermute | solution.py:440
  53.9 5.2 %collective-permute-done.7 = bf16[1,2,8,32,256]{4,3,2,1,0:T(8,128)(2,1)} collective-permute-done((bf16[1,2,8,32,256]{4,3,2,1,0:T(8,128)(2,1)}, bf16[1,2,8,32,256]{4,3,2,1,0:T(8,128)(2,1)}, u32[]{:S(2)}, u32[]{:S(2)}) %collective-permute-start.7) | collective-permute-done | bytes 262176 | tf_op jit(solution)/shard_map/ppermute | solution.py:440
  60.1 4.1 %collective-permute-done.4.across = bf16[4,8,32,256]{3,2,1,0:T(8,128)(2,1)S(1)} collective-permute-done((bf16[4,8,32,256]{3,2,1,0:T(8,128)(2,1)S(1)}, bf16[4,8,32,256]{3,2,1,0:T(8,128)(2,1)S(1)}, u32[]{:S(2)}, u32[]{:S(2)}) %collective-permute-start.4) | collective-permute-done | bytes 524320 | tf_op jit(solution)/shard_map/ppermute | solution.py:440
  64.7 1.6 %collective-permute-start.8 = (bf16[2,8,64,256]{3,2,1,0:T(8,128)(2,1)S(1)}, bf16[2,8,64,256]{3,2,1,0:T(8,128)(2,1)S(1)}, u32[]{:S(2)}, u32[]{:S(2)}) collective-permute-start(bf16[2,8,64,256]{3,2,1,0:T(8,128)(2,1)S(1)} %get-tuple-element.52), channel_id=1, source_target_pairs={{0,16},{8,24},{16,0},{24,8},{1,17},{9,25},{17,1},{25,9},{2,18},{10... | collective-permute-start | bytes 1572872 | tf_op jit(solution)/shard_map/ppermute | solution.py:440
  66.5 3.1 %collective-permute-start.14 = (bf16[1,1,8,32,256]{4,3,2,1,0:T(8,128)(2,1)S(1)}, bf16[1,1,8,32,256]{4,3,2,1,0:T(8,128)(2,1)S(1)}, u32[]{:S(2)}, u32[]{:S(2)}) collective-permute-start(bf16[1,1,8,32,256]{4,3,2,1,0:T(8,128)(2,1)S(1)} %get-tuple-element.60), channel_id=1, source_target_pairs={{0,4},{1,5},{2,6},{3,7},{4,0},{5,1},{6,2},{7,3},{8,12},{9,13},{10,... | collective-permute-start | bytes 393224 | tf_op jit(solution)/shard_map/ppermute | solution.py:440
  69.6 4.7 %collective-permute-done.14 = bf16[1,1,8,32,256]{4,3,2,1,0:T(8,128)(2,1)S(1)} collective-permute-done((bf16[1,1,8,32,256]{4,3,2,1,0:T(8,128)(2,1)S(1)}, bf16[1,1,8,32,256]{4,3,2,1,0:T(8,128)(2,1)S(1)}, u32[]{:S(2)}, u32[]{:S(2)}) %collective-permute-start.14) | collective-permute-done | bytes 131104 | tf_op jit(solution)/shard_map/ppermute | solution.py:440
  76.4 1.4 shard_map.86.by_channel
  78.2 1.6 %collective-permute-start.12 = (bf16[2,8,64,256]{3,2,1,0:T(8,128)(2,1)S(1)}, bf16[2,8,64,256]{3,2,1,0:T(8,128)(2,1)S(1)}, u32[]{:S(2)}, u32[]{:S(2)}) collective-permute-start(bf16[2,8,64,256]{3,2,1,0:T(8,128)(2,1)S(1)} %get-tuple-element.57), channel_id=1, source_target_pairs={{0,16},{8,24},{16,0},{24,8},{1,17},{9,25},{17,1},{25,9},{2,18},{10... | collective-permute-start | bytes 1572872 | tf_op jit(solution)/shard_map/ppermute | solution.py:440
  80.8 1.6 %collective-permute-start.16 = (bf16[4,8,32,256]{3,2,1,0:T(8,128)(2,1)S(1)}, bf16[4,8,32,256]{3,2,1,0:T(8,128)(2,1)S(1)}, u32[]{:S(2)}, u32[]{:S(2)}) collective-permute-start(bf16[4,8,32,256]{3,2,1,0:T(8,128)(2,1)S(1)} %pad_maximum_fusion.5.held), channel_id=1, source_target_pairs={{0,1},{1,0},{2,3},{3,2},{4,5},{5,4},{6,7},{7,6},{8,9},{9,8},{10,11... | collective-permute-start | bytes 1572872 | tf_op jit(solution)/shard_map/ppermute | solution.py:440
  82.4 2.3 %collective-permute-start.19 = (bf16[1,1,8,32,256]{4,3,2,1,0:T(8,128)(2,1)S(1)}, bf16[1,1,8,32,256]{4,3,2,1,0:T(8,128)(2,1)S(1)}, u32[]{:S(2)}, u32[]{:S(2)}) collective-permute-start(bf16[1,1,8,32,256]{4,3,2,1,0:T(8,128)(2,1)S(1)} %get-tuple-element.69), channel_id=1, source_target_pairs={{0,4},{1,5},{2,6},{3,7},{4,0},{5,1},{6,2},{7,3},{8,12},{9,13},{10,... | collective-permute-start | bytes 393224 | tf_op jit(solution)/shard_map/ppermute | solution.py:440
  84.7 6.1 %collective-permute-done.19 = bf16[1,1,8,32,256]{4,3,2,1,0:T(8,128)(2,1)S(1)} collective-permute-done((bf16[1,1,8,32,256]{4,3,2,1,0:T(8,128)(2,1)S(1)}, bf16[1,1,8,32,256]{4,3,2,1,0:T(8,128)(2,1)S(1)}, u32[]{:S(2)}, u32[]{:S(2)}) %collective-permute-start.19) | collective-permute-done | bytes 131104 | tf_op jit(solution)/shard_map/ppermute | solution.py:440
  91.5 5.3 %shard_map.87.refs_0_ = bf16[4,2,512,128]{3,2,1,0:T(8,128)(2,1)S(1)} custom-call(bf16[8,64,256]{2,1,0:T(8,128)(2,1)S(1)} %get-tuple-element.50.here, bf16[2,8,64,256]{3,2,1,0:T(8,128)(2,1)S(1)} %collective-permute-done.9.near, bf16[2,8,64,256]{3,2,1,0:T(8,128)(2,1)S(1)} %collective-permute-done.8.far, bf16[8,512,256]{2,1,0:T(8,128)(2,1)S(1)} %shard_map.86.by_channel), custom_call_target="tpu_custom_call" | custom-call | flops 603979776 | bytes 4194304 | tf_op jit(solution)/shard_map/pallas_call | solution.py:311
  98.2 1.8 %collective-permute-start.21 = (bf16[4,8,32,256]{3,2,1,0:T(8,128)(2,1)S(1)}, bf16[4,8,32,256]{3,2,1,0:T(8,128)(2,1)S(1)}, u32[]{:S(2)}, u32[]{:S(2)}) collective-permute-start(bf16[4,8,32,256]{3,2,1,0:T(8,128)(2,1)S(1)} %pad_maximum_fusion.7.held), channel_id=1, source_target_pairs={{0,1},{1,0},{2,3},{3,2},{4,5},{5,4},{6,7},{7,6},{8,9},{9,8},{10,11... | collective-permute-start | bytes 1572872 | tf_op jit(solution)/shard_map/ppermute | solution.py:440
  100.0 5.5 %shard_map.89.refs_1_ = bf16[4,2,512,128]{3,2,1,0:T(8,128)(2,1)S(1)} custom-call(bf16[8,64,256]{2,1,0:T(8,128)(2,1)S(1)} %get-tuple-element.55.here, bf16[2,8,64,256]{3,2,1,0:T(8,128)(2,1)S(1)} %collective-permute-done.13.near, bf16[2,8,64,256]{3,2,1,0:T(8,128)(2,1)S(1)} %collective-permute-done.12.far, bf16[8,512,256]{2,1,0:T(8,128)(2,1)S(1)} %shard_map.86.by_channel), custom_call_target="tpu_custom_call" | custom-call | flops 603979776 | bytes 4194304 | tf_op jit(solution)/shard_map/pallas_call | solution.py:311
  105.6 6.3 %collective-permute-done.17.far = bf16[2,8,64,256]{3,2,1,0:T(8,128)(2,1)S(1)} collective-permute-done((bf16[2,8,64,256]{3,2,1,0:T(8,128)(2,1)S(1)}, bf16[2,8,64,256]{3,2,1,0:T(8,128)(2,1)S(1)}, u32[]{:S(2)}, u32[]{:S(2)}) %collective-permute-start.17) | collective-permute-done | bytes 524320 | tf_op jit(solution)/shard_map/ppermute | solution.py:440
  112.7 1.6 %collective-permute-start.22 = (bf16[2,8,64,256]{3,2,1,0:T(8,128)(2,1)S(1)}, bf16[2,8,64,256]{3,2,1,0:T(8,128)(2,1)S(1)}, u32[]{:S(2)}, u32[]{:S(2)}) collective-permute-start(bf16[2,8,64,256]{3,2,1,0:T(8,128)(2,1)S(1)} %get-tuple-element.75), channel_id=1, source_target_pairs={{0,16},{8,24},{16,0},{24,8},{1,17},{9,25},{17,1},{25,9},{2,18},{10... | collective-permute-start | bytes 1572872 | tf_op jit(solution)/shard_map/ppermute | solution.py:440
  114.3 5.3 %shard_map.91.refs_2_ = bf16[4,2,512,128]{3,2,1,0:T(8,128)(2,1)S(1)} custom-call(bf16[8,64,256]{2,1,0:T(8,128)(2,1)S(1)} %get-tuple-element.64.here, bf16[2,8,64,256]{3,2,1,0:T(8,128)(2,1)S(1)} %collective-permute-done.18.near, bf16[2,8,64,256]{3,2,1,0:T(8,128)(2,1)S(1)} %collective-permute-done.17.far, bf16[8,512,256]{2,1,0:T(8,128)(2,1)S(1)} %shard_map.86.by_channel), custom_call_target="tpu_custom_call" | custom-call | flops 603979776 | bytes 4194304 | tf_op jit(solution)/shard_map/pallas_call | solution.py:311
  119.6 7.3 %collective-permute-done.22.far = bf16[2,8,64,256]{3,2,1,0:T(8,128)(2,1)S(1)} collective-permute-done((bf16[2,8,64,256]{3,2,1,0:T(8,128)(2,1)S(1)}, bf16[2,8,64,256]{3,2,1,0:T(8,128)(2,1)S(1)}, u32[]{:S(2)}, u32[]{:S(2)}) %collective-permute-start.22) | collective-permute-done | bytes 524320 | tf_op jit(solution)/shard_map/ppermute | solution.py:440
  127.0 1.9 %collective-permute-done.23.near = bf16[2,8,64,256]{3,2,1,0:T(8,128)(2,1)S(1)} collective-permute-done((bf16[2,8,64,256]{3,2,1,0:T(8,128)(2,1)S(1)}, bf16[2,8,64,256]{3,2,1,0:T(8,128)(2,1)S(1)}, u32[]{:S(2)}, u32[]{:S(2)}) %collective-permute-start.23) | collective-permute-done | bytes 524320 | tf_op jit(solution)/shard_map/ppermute | solution.py:440
  128.9 5.3 %shard_map.93.refs_3_ = bf16[4,2,512,128]{3,2,1,0:T(8,128)(2,1)S(1)} custom-call(bf16[8,64,256]{2,1,0:T(8,128)(2,1)S(1)} %get-tuple-element.73.here, bf16[2,8,64,256]{3,2,1,0:T(8,128)(2,1)S(1)} %collective-permute-done.23.near, bf16[2,8,64,256]{3,2,1,0:T(8,128)(2,1)S(1)} %collective-permute-done.22.far, bf16[8,512,256]{2,1,0:T(8,128)(2,1)S(1)} %shard_map.86.by_channel), custom_call_target="tpu_custom_call" | custom-call | flops 603979776 | bytes 4194304 | tf_op jit(solution)/shard_map/pallas_call | solution.py:311
  134.3 9.9 %shard_map.94 = f32[64,32,2048]{2,1,0:T(8,128)} custom-call(bf16[4,2,512,128]{3,2,1,0:T(8,128)(2,1)S(1)} %shard_map.87.refs_0_, bf16[4,2,512,128]{3,2,1,0:T(8,128)(2,1)S(1)} %shard_map.89.refs_1_, bf16[4,2,512,128]{3,2,1,0:T(8,128)(2,1)S(1)} %shard_map.91.refs_2_, bf16[4,2,512,128]{3,2,1,0:T(8,128)(2,1)S(1)} %shard_map.93.refs_3_, ...), custom_call_target="tpu_custom_call" | custom-call | flops 4294967296 | bytes 16777216 | tf_op jit(solution)/shard_map/pallas_call | solution.py:361
  (77 shorter events, 13.8 us)
Async XLA Ops:
  0.0 17.1 %copy-start.5 = (bf16[32]{0:T(256)(128)(2,1)S(1)}, bf16[32]{0:T(256)(128)(2,1)}, u32[]{:S(2)}) copy-start(bf16[32]{0:T(256)(128)(2,1)} %param.9) | copy-start | bytes 196
  0.0 17.4 %copy-start.2 = (f32[512,272]{1,0:T(8,128)S(1)}, f32[512,272]{1,0:T(8,128)}, u32[]{:S(2)}) copy-start(f32[512,272]{1,0:T(8,128)} %constant.33.clone.angles) | copy-start | bytes 1671172
  0.0 20.0 %copy-start.7 = (s32[8]{0:T(128)S(1)}, s32[8]{0:T(128)}, u32[]{:S(2)}) copy-start(s32[8]{0:T(128)} %constant.34.clone) | copy-start | bytes 100
  0.0 27.0 %copy-start.4 = (s32[32]{0:T(128)S(1)}, s32[32]{0:T(128)}, u32[]{:S(2)}) copy-start(s32[32]{0:T(128)} %param.10) | copy-start | bytes 388
  10.6 23.5 %copy-start.6 = (s32[256]{0:T(256)S(1)}, s32[256]{0:T(256)}, u32[]{:S(2)}) copy-start(s32[256]{0:T(256)} %param.11) | copy-start | bytes 3076
  10.6 16.5 %collective-permute-start = (bf16[8,16,1024]{2,1,0:T(8,128)(2,1)}, bf16[8,16,1024]{2,1,0:T(8,128)(2,1)S(1)}, u32[]{:S(2)}, u32[]{:S(2)}) collective-permute-start(bf16[8,16,1024]{2,1,0:T(8,128)(2,1)} %get-tuple-element.42), channel_id=1, source_target_pairs={{0,1},{1,2},{2,3},{3,4},{4,5},{5,6},{6,7},{8,9},{9,10},{10,11},{11... | collective-permute-start | bytes 786440 | tf_op jit(solution)/shard_map/ppermute | solution.py:453
  15.6 11.5 %collective-permute-start.1 = (bf16[8,16,1024]{2,1,0:T(8,128)(2,1)}, bf16[8,16,1024]{2,1,0:T(8,128)(2,1)S(1)}, u32[]{:S(2)}, u32[]{:S(2)}) collective-permute-start(bf16[8,16,1024]{2,1,0:T(8,128)(2,1)} %get-tuple-element.44), channel_id=1, source_target_pairs={{1,0},{2,1},{3,2},{4,3},{5,4},{6,5},{7,6},{9,8},{10,9},{11,10},{12... | collective-permute-start | bytes 786440 | tf_op jit(solution)/shard_map/ppermute | solution.py:454
  18.7 1.4 copy-start
  27.0 1.2 copy-start.1
  29.5 14.4 %collective-permute-start.2 = (bf16[1,1,8,32,256]{4,3,2,1,0:T(8,128)(2,1)S(1)}, bf16[1,1,8,32,256]{4,3,2,1,0:T(8,128)(2,1)S(1)}, u32[]{:S(2)}, u32[]{:S(2)}) collective-permute-start(bf16[1,1,8,32,256]{4,3,2,1,0:T(8,128)(2,1)S(1)} %get-tuple-element.45), channel_id=1, source_target_pairs={{0,4},{1,5},{2,6},{3,7},{4,0},{5,1},{6,2},{7,3},{8,12},{9,13},{10,... | collective-permute-start | bytes 393224 | tf_op jit(solution)/shard_map/ppermute | solution.py:440
  34.1 12.0 %collective-permute-start.5 = (bf16[1,1,8,32,256]{4,3,2,1,0:T(8,128)(2,1)S(1)}, bf16[1,1,8,32,256]{4,3,2,1,0:T(8,128)(2,1)S(1)}, u32[]{:S(2)}, u32[]{:S(2)}) collective-permute-start(bf16[1,1,8,32,256]{4,3,2,1,0:T(8,128)(2,1)S(1)} %get-tuple-element.46), channel_id=1, source_target_pairs={{0,4},{1,5},{2,6},{3,7},{4,0},{5,1},{6,2},{7,3},{8,12},{9,13},{10,... | collective-permute-start | bytes 393224 | tf_op jit(solution)/shard_map/ppermute | solution.py:440
  34.2 17.7 %collective-permute-start.6 = (bf16[8,32,1024]{2,1,0:T(8,128)(2,1)S(1)}, bf16[8,32,1024]{2,1,0:T(8,128)(2,1)S(1)}, u32[]{:S(2)}, u32[]{:S(2)}) collective-permute-start(bf16[8,32,1024]{2,1,0:T(8,128)(2,1)S(1)} %get-tuple-element.47.here), channel_id=1, source_target_pairs={{0,16},{8,24},{16,0},{24,8},{1,17},{9,25},{17,1},{25,9},{2,18},{10... | collective-permute-start | bytes 1572872 | tf_op jit(solution)/shard_map/ppermute | solution.py:440
  43.9 7.8 %collective-permute-start.3 = (bf16[1,2,8,32,256]{4,3,2,1,0:T(8,128)(2,1)S(1)}, bf16[1,2,8,32,256]{4,3,2,1,0:T(8,128)(2,1)S(1)}, u32[]{:S(2)}, u32[]{:S(2)}) collective-permute-start(bf16[1,2,8,32,256]{4,3,2,1,0:T(8,128)(2,1)S(1)} %constant_dynamic-update-slice_fusion), channel_id=1, source_target_pairs={{0,2},{1,3},{2,0},{3,1},{4,6},{5,7},{6,4},{7,5},{8,10},{9,11},{10,... | collective-permute-start | bytes 786440 | tf_op jit(solution)/shard_map/ppermute | solution.py:440
  51.7 12.5 %collective-permute-start.4 = (bf16[4,8,32,256]{3,2,1,0:T(8,128)(2,1)S(1)}, bf16[4,8,32,256]{3,2,1,0:T(8,128)(2,1)S(1)}, u32[]{:S(2)}, u32[]{:S(2)}) collective-permute-start(bf16[4,8,32,256]{3,2,1,0:T(8,128)(2,1)S(1)} %pad_maximum_fusion.1.held), channel_id=1, source_target_pairs={{0,1},{1,0},{2,3},{3,2},{4,5},{5,4},{6,7},{7,6},{8,9},{9,8},{10,11... | collective-permute-start | bytes 1572872 | tf_op jit(solution)/shard_map/ppermute | solution.py:440
  51.8 7.2 %collective-permute-start.7 = (bf16[1,2,8,32,256]{4,3,2,1,0:T(8,128)(2,1)}, bf16[1,2,8,32,256]{4,3,2,1,0:T(8,128)(2,1)}, u32[]{:S(2)}, u32[]{:S(2)}) collective-permute-start(bf16[1,2,8,32,256]{4,3,2,1,0:T(8,128)(2,1)} %constant_dynamic-update-slice_fusion.2), channel_id=1, source_target_pairs={{0,2},{1,3},{2,0},{3,1},{4,6},{5,7},{6,4},{7,5},{8,10},{9,11},{10,... | collective-permute-start | bytes 786440 | tf_op jit(solution)/shard_map/ppermute | solution.py:440
  53.6 22.8 %collective-permute-start.10 = (bf16[2,8,32,1024]{3,2,1,0:T(8,128)(2,1)}, bf16[2,8,32,1024]{3,2,1,0:T(8,128)(2,1)S(1)}, u32[]{:S(2)}, u32[]{:S(2)}) collective-permute-start(bf16[2,8,32,1024]{3,2,1,0:T(8,128)(2,1)} %pad_maximum_fusion), channel_id=1, source_target_pairs={{0,8},{8,0},{16,24},{24,16},{1,9},{9,1},{17,25},{25,17},{2,10},{10... | collective-permute-start | bytes 3145736 | tf_op jit(solution)/shard_map/ppermute | solution.py:440
  64.7 11.6 %collective-permute-start.8 = (bf16[2,8,64,256]{3,2,1,0:T(8,128)(2,1)S(1)}, bf16[2,8,64,256]{3,2,1,0:T(8,128)(2,1)S(1)}, u32[]{:S(2)}, u32[]{:S(2)}) collective-permute-start(bf16[2,8,64,256]{3,2,1,0:T(8,128)(2,1)S(1)} %get-tuple-element.52), channel_id=1, source_target_pairs={{0,16},{8,24},{16,0},{24,8},{1,17},{9,25},{17,1},{25,9},{2,18},{10... | collective-permute-start | bytes 1572872 | tf_op jit(solution)/shard_map/ppermute | solution.py:440
  66.2 11.6 %collective-permute-start.11 = (bf16[4,8,32,256]{3,2,1,0:T(8,128)(2,1)S(1)}, bf16[4,8,32,256]{3,2,1,0:T(8,128)(2,1)S(1)}, u32[]{:S(2)}, u32[]{:S(2)}) collective-permute-start(bf16[4,8,32,256]{3,2,1,0:T(8,128)(2,1)S(1)} %pad_maximum_fusion.2.held), channel_id=1, source_target_pairs={{0,1},{1,0},{2,3},{3,2},{4,5},{5,4},{6,7},{7,6},{8,9},{9,8},{10,11... | collective-permute-start | bytes 1572872 | tf_op jit(solution)/shard_map/ppermute | solution.py:440
  66.5 7.7 %collective-permute-start.14 = (bf16[1,1,8,32,256]{4,3,2,1,0:T(8,128)(2,1)S(1)}, bf16[1,1,8,32,256]{4,3,2,1,0:T(8,128)(2,1)S(1)}, u32[]{:S(2)}, u32[]{:S(2)}) collective-permute-start(bf16[1,1,8,32,256]{4,3,2,1,0:T(8,128)(2,1)S(1)} %get-tuple-element.60), channel_id=1, source_target_pairs={{0,4},{1,5},{2,6},{3,7},{4,0},{5,1},{6,2},{7,3},{8,12},{9,13},{10,... | collective-permute-start | bytes 393224 | tf_op jit(solution)/shard_map/ppermute | solution.py:440
  74.3 6.4 %collective-permute-start.15 = (bf16[1,2,8,32,256]{4,3,2,1,0:T(8,128)(2,1)S(1)}, bf16[1,2,8,32,256]{4,3,2,1,0:T(8,128)(2,1)S(1)}, u32[]{:S(2)}, u32[]{:S(2)}) collective-permute-start(bf16[1,2,8,32,256]{4,3,2,1,0:T(8,128)(2,1)S(1)} %constant_dynamic-update-slice_fusion.4), channel_id=1, source_target_pairs={{0,2},{1,3},{2,0},{3,1},{4,6},{5,7},{6,4},{7,5},{8,10},{9,11},{10,... | collective-permute-start | bytes 786440 | tf_op jit(solution)/shard_map/ppermute | solution.py:440
  76.3 15.2 %collective-permute-start.9 = (bf16[2,8,64,256]{3,2,1,0:T(8,128)(2,1)S(1)}, bf16[2,8,64,256]{3,2,1,0:T(8,128)(2,1)S(1)}, u32[]{:S(2)}, u32[]{:S(2)}) collective-permute-start(bf16[2,8,64,256]{3,2,1,0:T(8,128)(2,1)S(1)} %pad_maximum_fusion.3), channel_id=1, source_target_pairs={{0,8},{8,0},{16,24},{24,16},{1,9},{9,1},{17,25},{25,17},{2,10},{10... | collective-permute-start | bytes 1572872 | tf_op jit(solution)/shard_map/ppermute | solution.py:440
  78.2 18.6 %collective-permute-start.12 = (bf16[2,8,64,256]{3,2,1,0:T(8,128)(2,1)S(1)}, bf16[2,8,64,256]{3,2,1,0:T(8,128)(2,1)S(1)}, u32[]{:S(2)}, u32[]{:S(2)}) collective-permute-start(bf16[2,8,64,256]{3,2,1,0:T(8,128)(2,1)S(1)} %get-tuple-element.57), channel_id=1, source_target_pairs={{0,16},{8,24},{16,0},{24,8},{1,17},{9,25},{17,1},{25,9},{2,18},{10... | collective-permute-start | bytes 1572872 | tf_op jit(solution)/shard_map/ppermute | solution.py:440
  80.8 16.3 %collective-permute-start.16 = (bf16[4,8,32,256]{3,2,1,0:T(8,128)(2,1)S(1)}, bf16[4,8,32,256]{3,2,1,0:T(8,128)(2,1)S(1)}, u32[]{:S(2)}, u32[]{:S(2)}) collective-permute-start(bf16[4,8,32,256]{3,2,1,0:T(8,128)(2,1)S(1)} %pad_maximum_fusion.5.held), channel_id=1, source_target_pairs={{0,1},{1,0},{2,3},{3,2},{4,5},{5,4},{6,7},{7,6},{8,9},{9,8},{10,11... | collective-permute-start | bytes 1572872 | tf_op jit(solution)/shard_map/ppermute | solution.py:440
  82.4 8.4 %collective-permute-start.19 = (bf16[1,1,8,32,256]{4,3,2,1,0:T(8,128)(2,1)S(1)}, bf16[1,1,8,32,256]{4,3,2,1,0:T(8,128)(2,1)S(1)}, u32[]{:S(2)}, u32[]{:S(2)}) collective-permute-start(bf16[1,1,8,32,256]{4,3,2,1,0:T(8,128)(2,1)S(1)} %get-tuple-element.69), channel_id=1, source_target_pairs={{0,4},{1,5},{2,6},{3,7},{4,0},{5,1},{6,2},{7,3},{8,12},{9,13},{10,... | collective-permute-start | bytes 393224 | tf_op jit(solution)/shard_map/ppermute | solution.py:440
  90.8 7.4 %collective-permute-start.20 = (bf16[1,2,8,32,256]{4,3,2,1,0:T(8,128)(2,1)S(1)}, bf16[1,2,8,32,256]{4,3,2,1,0:T(8,128)(2,1)S(1)}, u32[]{:S(2)}, u32[]{:S(2)}) collective-permute-start(bf16[1,2,8,32,256]{4,3,2,1,0:T(8,128)(2,1)S(1)} %pad_maximum_fusion.9), channel_id=1, source_target_pairs={{0,2},{1,3},{2,0},{3,1},{4,6},{5,7},{6,4},{7,5},{8,10},{9,11},{10,... | collective-permute-start | bytes 786440 | tf_op jit(solution)/shard_map/ppermute | solution.py:440
  97.0 3.0 %collective-permute-start.13 = (bf16[2,8,64,256]{3,2,1,0:T(8,128)(2,1)S(1)}, bf16[2,8,64,256]{3,2,1,0:T(8,128)(2,1)S(1)}, u32[]{:S(2)}, u32[]{:S(2)}) collective-permute-start(bf16[2,8,64,256]{3,2,1,0:T(8,128)(2,1)S(1)} %pad_maximum_fusion.4), channel_id=1, source_target_pairs={{0,8},{8,0},{16,24},{24,16},{1,9},{9,1},{17,25},{25,17},{2,10},{10... | collective-permute-start | bytes 1572872 | tf_op jit(solution)/shard_map/ppermute | solution.py:440
  97.5 14.4 %collective-permute-start.17 = (bf16[2,8,64,256]{3,2,1,0:T(8,128)(2,1)S(1)}, bf16[2,8,64,256]{3,2,1,0:T(8,128)(2,1)S(1)}, u32[]{:S(2)}, u32[]{:S(2)}) collective-permute-start(bf16[2,8,64,256]{3,2,1,0:T(8,128)(2,1)S(1)} %get-tuple-element.66), channel_id=1, source_target_pairs={{0,16},{8,24},{16,0},{24,8},{1,17},{9,25},{17,1},{25,9},{2,18},{10... | collective-permute-start | bytes 1572872 | tf_op jit(solution)/shard_map/ppermute | solution.py:440
  98.2 14.0 %collective-permute-start.21 = (bf16[4,8,32,256]{3,2,1,0:T(8,128)(2,1)S(1)}, bf16[4,8,32,256]{3,2,1,0:T(8,128)(2,1)S(1)}, u32[]{:S(2)}, u32[]{:S(2)}) collective-permute-start(bf16[4,8,32,256]{3,2,1,0:T(8,128)(2,1)S(1)} %pad_maximum_fusion.7.held), channel_id=1, source_target_pairs={{0,1},{1,0},{2,3},{3,2},{4,5},{5,4},{6,7},{7,6},{8,9},{9,8},{10,11... | collective-permute-start | bytes 1572872 | tf_op jit(solution)/shard_map/ppermute | solution.py:440
  112.0 2.3 %collective-permute-start.18 = (bf16[2,8,64,256]{3,2,1,0:T(8,128)(2,1)S(1)}, bf16[2,8,64,256]{3,2,1,0:T(8,128)(2,1)S(1)}, u32[]{:S(2)}, u32[]{:S(2)}) collective-permute-start(bf16[2,8,64,256]{3,2,1,0:T(8,128)(2,1)S(1)} %pad_maximum_fusion.6), channel_id=1, source_target_pairs={{0,8},{8,0},{16,24},{24,16},{1,9},{9,1},{17,25},{25,17},{2,10},{10... | collective-permute-start | bytes 1572872 | tf_op jit(solution)/shard_map/ppermute | solution.py:440
  112.7 14.2 %collective-permute-start.22 = (bf16[2,8,64,256]{3,2,1,0:T(8,128)(2,1)S(1)}, bf16[2,8,64,256]{3,2,1,0:T(8,128)(2,1)S(1)}, u32[]{:S(2)}, u32[]{:S(2)}) collective-permute-start(bf16[2,8,64,256]{3,2,1,0:T(8,128)(2,1)S(1)} %get-tuple-element.75), channel_id=1, source_target_pairs={{0,16},{8,24},{16,0},{24,8},{1,17},{9,25},{17,1},{25,9},{2,18},{10... | collective-permute-start | bytes 1572872 | tf_op jit(solution)/shard_map/ppermute | solution.py:440
  119.6 14.7 %copy-start.3 = (f32[2,512]{1,0:T(2,128)S(1)}, f32[2,512]{1,0:T(2,128)}, u32[]{:S(2)}) copy-start(f32[2,512]{1,0:T(2,128)} %constant.35.clone.refs_5_) | copy-start | bytes 12292
  127.0 2.0 %collective-permute-start.23 = (bf16[2,8,64,256]{3,2,1,0:T(8,128)(2,1)S(1)}, bf16[2,8,64,256]{3,2,1,0:T(8,128)(2,1)S(1)}, u32[]{:S(2)}, u32[]{:S(2)}) collective-permute-start(bf16[2,8,64,256]{3,2,1,0:T(8,128)(2,1)S(1)} %pad_maximum_fusion.8), channel_id=1, source_target_pairs={{0,8},{8,0},{16,24},{24,16},{1,9},{9,1},{17,25},{25,17},{2,10},{10... | collective-permute-start | bytes 1572872 | tf_op jit(solution)/shard_map/ppermute | solution.py:440
